TPU v7x, 512 devices: a whole 4x4x16 slice. The times are simulated.
512 devices in a mesh: ctx: 64 (over y_hi, z, core), head: 8 (over y_lo, x).
Axes of the slice: x: 4, y: 4 (y_hi: 2, y_lo: 2; y = y_hi * 2 + y_lo), z: 16, core: 2. Of those that a mesh axis runs over, the one named last changes fastest.
Arguments:
- queries: bfloat16 [16384, 2048], P(('ctx', 'head')), may hold values from -16 to 16
- keys: bfloat16 [16384, 2048], P(('ctx', 'head')), may hold values from -16 to 16
- values: bfloat16 [16384, 2048], P(('ctx', 'head')), may hold values from -6 to 6
- d_attn: bfloat16 [16384, 2048], P(('ctx', 'head')), may hold values from -12 to 12
- fisher_key_prior: float32 [16384, 2048], P(('ctx', 'head')), may hold values from 0.05 to 0.5
- fisher_value_prior: float32 [16384, 2048], P(('ctx', 'head')), may hold values from 0.05 to 0.5
- doc_lengths: int32 [32], replicated, may hold values from 1 to 1024, 16384 in all
Outputs:
- grad_queries: bfloat16 [16384, 2048], P(('ctx', 'head'))
- grad_keys: bfloat16 [16384, 2048], P(('ctx', 'head'))
- grad_values: bfloat16 [16384, 2048], P(('ctx', 'head'))
- fisher_key: float32 [16384, 2048], P(('ctx', 'head'))
- fisher_value: float32 [16384, 2048], P(('ctx', 'head'))
Inputs may be any that keep to these rules, and one draw needn't show every extreme that they name: `doc_lengths`: they sum to 16384; the longest has exactly 1024 tokens.
All inputs are finite; a program needn't handle non-finite values.
Results may differ from a plain program's by a relative error of at most 0.019.
Values may be sent and summed in bfloat16 or wider, within the bound.
No kernel may reach another device: no remote copies, remote signals or barrier semaphores. Data moves between devices by JAX's collectives and lax.ppermute only.
A program may use at most 64 MiB of HBM per device.

v0:
```python
import jax
import jax.numpy as jnp
from jax import lax
from jax.sharding import PartitionSpec as P

HD = 128
HEAD_DEV = 2


neg_large = -1e30


def passed_along(block, axis, distance):
    devices = range(lax.axis_size(axis))
    route = [(i - distance, i) for i in devices if i - distance in devices]
    return lax.ppermute(block, axis, route)


def documents(positions, bounds):
    return jnp.sum((positions[:, None] >= bounds[None, :]).astype(jnp.int32), axis=1)


def shards(queries, keys, values, d_attn, fisher_key_prior, fisher_value_prior, doc_lengths):
    head_width = HEAD_DEV * HD
    score_scale = 1.0 / HD**0.5
    q_here, k_here, v_here, d_here = (
        lax.all_to_all(queries, "head", split_axis=1, concat_axis=0, tiled=True),
        lax.all_to_all(keys, "head", split_axis=1, concat_axis=0, tiled=True),
        lax.all_to_all(values, "head", split_axis=1, concat_axis=0, tiled=True),
        lax.all_to_all(d_attn, "head", split_axis=1, concat_axis=0, tiled=True),
    )
    row_count = q_here.shape[0]
    half_rows = row_count // 2
    ctx_count = lax.axis_size("ctx")
    reach = min(8, ctx_count // 4)
    tile_count = 2 * reach + 1
    device = lax.axis_index("ctx")
    bounds = jnp.cumsum(doc_lengths)
    offsets = [0] + [-step for step in range(1, reach + 1)] + [step for step in range(1, reach + 1)]
    source = device + jnp.array(offsets, dtype=jnp.int32)
    row_index = jnp.arange(row_count, dtype=jnp.int32)
    lower_rows = row_index < half_rows
    inner_rows = row_index % half_rows
    lower_pos = source[:, None] * half_rows + inner_rows[None, :]
    upper_pos = (2 * ctx_count - 1 - source[:, None]) * half_rows + inner_rows[None, :]
    tile_pos = jnp.where(lower_rows[None, :], lower_pos, upper_pos)
    inside = (source >= 0) & (source < ctx_count)
    tile_docs = jnp.where(
        inside[:, None], documents(tile_pos.reshape(-1), bounds).reshape(tile_count, row_count), -1
    )
    own_pos = tile_pos[0]
    own_docs = tile_docs[0]
    q_heads = q_here.reshape(row_count, HEAD_DEV, HD)
    k_heads = k_here.reshape(row_count, HEAD_DEV, HD)
    v_heads = v_here.reshape(row_count, HEAD_DEV, HD)
    d_heads = d_here.reshape(row_count, HEAD_DEV, HD)
    key_value = jnp.concatenate([k_here, v_here], axis=1)
    left_list = []
    right_list = []
    from_left = key_value
    from_right = key_value
    for step in range(reach):
        from_left = passed_along(from_left, "ctx", 1)
        from_right = passed_along(from_right, "ctx", -1)
        left_list.append(from_left)
        right_list.append(from_right)
    kv_tiles = jnp.stack([key_value] + left_list + right_list, axis=0)
    k_tiles = kv_tiles[:, :, :head_width].reshape(tile_count, row_count, HEAD_DEV, HD)
    v_tiles = kv_tiles[:, :, head_width:].reshape(tile_count, row_count, HEAD_DEV, HD)

    def query_allowed(pos_tile, docs_tile):
        return (own_docs[:, None] == docs_tile[None, :]) & (pos_tile[None, :] <= own_pos[:, None])

    def query_scores(k_tile):
        return (
            jnp.einsum("qhd,khd->hqk", q_heads, k_tile, preferred_element_type=jnp.float32)
            * score_scale
        )

    def stats_step(carried, tile_data):
        k_tile, pos_tile, docs_tile = tile_data
        allowed = query_allowed(pos_tile, docs_tile)
        top_score, running_sum = carried
        scores = query_scores(k_tile)
        new_top = jnp.maximum(
            top_score, jnp.max(jnp.where(allowed[None], scores, neg_large), axis=2)
        )
        terms = jnp.where(allowed[None], jnp.exp(scores - new_top[:, :, None]), 0.0)
        return (
            (new_top, running_sum * jnp.exp(top_score - new_top) + jnp.sum(terms, axis=2)),
            None,
        )

    stats_start = (
        jnp.full((HEAD_DEV, row_count), neg_large, jnp.float32),
        jnp.zeros((HEAD_DEV, row_count), jnp.float32),
    )
    (top_score, running_sum), unused_stats = lax.scan(
        stats_step, stats_start, (k_tiles, tile_pos, tile_docs)
    )
    log_total = top_score + jnp.log(running_sum)

    def output_step(carried, tile_data):
        k_tile, v_tile, pos_tile, docs_tile = tile_data
        allowed = query_allowed(pos_tile, docs_tile)
        weights = jnp.where(
            allowed[None], jnp.exp(query_scores(k_tile) - log_total[:, :, None]), 0.0
        )
        return (
            carried
            + jnp.einsum(
                "hqk,khd->qhd",
                weights.astype(jnp.bfloat16),
                v_tile,
                preferred_element_type=jnp.float32,
            ),
            None,
        )

    zero_heads = jnp.zeros((row_count, HEAD_DEV, HD), jnp.float32)
    attended, unused_output = lax.scan(
        output_step, zero_heads, (k_tiles, v_tiles, tile_pos, tile_docs)
    )
    row_delta = jnp.sum(d_heads.astype(jnp.float32) * attended, axis=2).T
    blank_part = jnp.zeros((1,), jnp.float32)

    def grad_step(carried, tile_data):
        k_tile, v_tile, pos_tile, docs_tile = tile_data
        allowed = query_allowed(pos_tile, docs_tile)
        q_accum = carried
        weights = jnp.where(
            allowed[None], jnp.exp(query_scores(k_tile) - log_total[:, :, None]), 0.0
        )
        d_weights = jnp.einsum("qhd,khd->hqk", d_heads, v_tile, preferred_element_type=jnp.float32)
        d_scores = (weights * (d_weights - row_delta[:, :, None])).astype(jnp.bfloat16)
        q_accum = q_accum + jnp.einsum(
            "hqk,khd->qhd", d_scores, k_tile, preferred_element_type=jnp.float32
        )
        return (q_accum, blank_part)

    d_query, tile_grads = lax.scan(grad_step, zero_heads, (k_tiles, v_tiles, tile_pos, tile_docs))
    query_pack = jnp.concatenate([q_here, d_here], axis=1)
    stat_pack = jnp.concatenate([log_total.T, row_delta.T], axis=1)
    left_queries = [passed_along(query_pack, "ctx", step) for step in range(1, reach + 1)]
    right_queries = [passed_along(query_pack, "ctx", -step) for step in range(1, reach + 1)]
    left_stats = [passed_along(stat_pack, "ctx", step) for step in range(1, reach + 1)]
    right_stats = [passed_along(stat_pack, "ctx", -step) for step in range(1, reach + 1)]
    query_tiles = jnp.stack([query_pack] + left_queries + right_queries, axis=0)
    stat_tiles = jnp.stack([stat_pack] + left_stats + right_stats, axis=0)
    q_tiles = query_tiles[:, :, :head_width].reshape(tile_count, row_count, HEAD_DEV, HD)
    d_tiles = query_tiles[:, :, head_width:].reshape(tile_count, row_count, HEAD_DEV, HD)
    log_tiles = stat_tiles[:, :, :HEAD_DEV]
    delta_tiles = stat_tiles[:, :, HEAD_DEV:]

    def key_step(carried, tile_data):
        q_tile, d_tile, log_tile, delta_tile, pos_tile, docs_tile = tile_data
        allowed = (docs_tile[:, None] == own_docs[None, :]) & (
            own_pos[None, :] <= pos_tile[:, None]
        )
        key_accum, value_accum = carried
        scores = (
            jnp.einsum("qhd,khd->hqk", q_tile, k_heads, preferred_element_type=jnp.float32)
            * score_scale
        )
        weights = jnp.where(allowed[None], jnp.exp(scores - log_tile.T[:, :, None]), 0.0)
        d_weights = jnp.einsum("qhd,khd->hqk", d_tile, v_heads, preferred_element_type=jnp.float32)
        d_scores = (weights * (d_weights - delta_tile.T[:, :, None])).astype(jnp.bfloat16)
        key_accum = key_accum + jnp.einsum(
            "hqk,qhd->khd", d_scores, q_tile, preferred_element_type=jnp.float32
        )
        value_accum = value_accum + jnp.einsum(
            "hqk,qhd->khd", weights.astype(jnp.bfloat16), d_tile, preferred_element_type=jnp.float32
        )
        return ((key_accum, value_accum), None)

    (key_accum, value_accum), unused_keys = lax.scan(
        key_step,
        (zero_heads, zero_heads),
        (q_tiles, d_tiles, log_tiles, delta_tiles, tile_pos, tile_docs),
    )
    d_key = key_accum.reshape(row_count, head_width) * score_scale
    d_value = value_accum.reshape(row_count, head_width)
    grad_q = (d_query * score_scale).astype(jnp.bfloat16).reshape(row_count, head_width)
    grad_k = d_key.astype(jnp.bfloat16)
    grad_v = d_value.astype(jnp.bfloat16)
    back_q, back_k, back_v = (
        lax.all_to_all(grad_q, "head", split_axis=0, concat_axis=1, tiled=True),
        lax.all_to_all(grad_k, "head", split_axis=0, concat_axis=1, tiled=True),
        lax.all_to_all(grad_v, "head", split_axis=0, concat_axis=1, tiled=True),
    )
    key_wide = back_k.astype(jnp.float32)
    value_wide = back_v.astype(jnp.float32)
    fisher_key = fisher_key_prior + key_wide * key_wide
    fisher_value = fisher_value_prior + value_wide * value_wide
    return (back_q, back_k, back_v, fisher_key, fisher_value)


def solution(mesh):
    placed = (
        P(("ctx", "head"), None),
        P(("ctx", "head"), None),
        P(("ctx", "head"), None),
        P(("ctx", "head"), None),
        P(("ctx", "head"), None),
        P(("ctx", "head"), None),
        P(),
    )
    return jax.shard_map(
        shards,
        mesh=mesh,
        in_specs=placed,
        out_specs=(
            P(("ctx", "head"), None),
            P(("ctx", "head"), None),
            P(("ctx", "head"), None),
            P(("ctx", "head"), None),
            P(("ctx", "head"), None),
        ),
        check_vma=False,
    )
```

profile of v0, /device:TPU:16, one launch (start us, length us, event | category | flops | bytes accessed | tf_op | source)
XLA Modules:
  0.0 672.3 jit_solution(3017992458815332821)
XLA Ops:
  13.9 5.7 all-to-all-start.2
  20.2 5.9 all-to-all-done.2
  29.6 6.4 all-to-all-done.3
  47.9 7.3 %collective-permute-start.8 = (bf16[256,512]{1,0:T(8,128)(2,1)S(1)}, bf16[256,512]{1,0:T(8,128)(2,1)S(1)}, u32[]{:S(2)}, u32[]{:S(2)}) collective-permute-start(bf16[256,512]{1,0:T(8,128)(2,1)S(1)} %pad_maximum_fusion), channel_id=1, source_target_pairs={{8,0},{16,8},{24,16},{32,24},{40,32},{48,40},{56,48},{64,56},{72,6... | collective-permute-start | bytes 786440 | tf_op jit(solution)/shard_map/ppermute | solution.py:16
  61.4 6.2 collective-permute-start.19
  76.4 13.6 %collective-permute-start.21 = (bf16[256,512]{1,0:T(8,128)(2,1)S(1)}, bf16[256,512]{1,0:T(8,128)(2,1)S(1)}, u32[]{:S(2)}, u32[]{:S(2)}) collective-permute-start(bf16[256,512]{1,0:T(8,128)(2,1)S(1)} %pad_maximum_fusion.1), channel_id=1, source_target_pairs={{0,48},{8,56},{16,64},{24,72},{32,80},{40,88},{48,96},{56,104},{64... | collective-permute-start | bytes 786440 | tf_op jit(solution)/shard_map/ppermute | solution.py:16
  90.7 9.9 %collective-permute-start.22 = (bf16[256,512]{1,0:T(8,128)(2,1)S(1)}, bf16[256,512]{1,0:T(8,128)(2,1)S(1)}, u32[]{:S(2)}, u32[]{:S(2)}) collective-permute-start(bf16[256,512]{1,0:T(8,128)(2,1)S(1)} %pad_maximum_fusion.1), channel_id=1, source_target_pairs={{0,56},{8,64},{16,72},{24,80},{32,88},{40,96},{48,104},{56,112},{6... | collective-permute-start | bytes 786440 | tf_op jit(solution)/shard_map/ppermute | solution.py:16
  103.3 11.4 %collective-permute-start.23 = (bf16[256,512]{1,0:T(8,128)(2,1)S(1)}, bf16[256,512]{1,0:T(8,128)(2,1)S(1)}, u32[]{:S(2)}, u32[]{:S(2)}) collective-permute-start(bf16[256,512]{1,0:T(8,128)(2,1)S(1)} %pad_maximum_fusion.1), channel_id=1, source_target_pairs={{0,64},{8,72},{16,80},{24,88},{32,96},{40,104},{48,112},{56,120},{... | collective-permute-start | bytes 786440 | tf_op jit(solution)/shard_map/ppermute | solution.py:16
  115.3 10.0 %collective-permute-done.21 = bf16[256,512]{1,0:T(8,128)(2,1)S(1)} collective-permute-done((bf16[256,512]{1,0:T(8,128)(2,1)S(1)}, bf16[256,512]{1,0:T(8,128)(2,1)S(1)}, u32[]{:S(2)}, u32[]{:S(2)}) %collective-permute-start.21) | collective-permute-done | bytes 262176 | tf_op jit(solution)/shard_map/ppermute | solution.py:16
  128.0 9.1 %collective-permute-done.22 = bf16[256,512]{1,0:T(8,128)(2,1)S(1)} collective-permute-done((bf16[256,512]{1,0:T(8,128)(2,1)S(1)}, bf16[256,512]{1,0:T(8,128)(2,1)S(1)}, u32[]{:S(2)}, u32[]{:S(2)}) %collective-permute-start.22) | collective-permute-done | bytes 262176 | tf_op jit(solution)/shard_map/ppermute | solution.py:16
  144.9 18.4 %collective-permute-start.26 = (bf16[256,512]{1,0:T(8,128)(2,1)S(1)}, bf16[256,512]{1,0:T(8,128)(2,1)S(1)}, u32[]{:S(2)}, u32[]{:S(2)}) collective-permute-start(bf16[256,512]{1,0:T(8,128)(2,1)S(1)} %pad_maximum_fusion.1), channel_id=1, source_target_pairs={{24,0},{32,8},{40,16},{48,24},{56,32},{64,40},{72,48},{80,56},{88,... | collective-permute-start | bytes 786440 | tf_op jit(solution)/shard_map/ppermute | solution.py:16
  166.7 8.3 %collective-permute-start.28 = (bf16[256,512]{1,0:T(8,128)(2,1)S(1)}, bf16[256,512]{1,0:T(8,128)(2,1)S(1)}, u32[]{:S(2)}, u32[]{:S(2)}) collective-permute-start(bf16[256,512]{1,0:T(8,128)(2,1)S(1)} %pad_maximum_fusion.1), channel_id=1, source_target_pairs={{40,0},{48,8},{56,16},{64,24},{72,32},{80,40},{88,48},{96,56},{104... | collective-permute-start | bytes 786440 | tf_op jit(solution)/shard_map/ppermute | solution.py:16
  184.6 17.0 %collective-permute-start.30 = (bf16[256,512]{1,0:T(8,128)(2,1)S(1)}, bf16[256,512]{1,0:T(8,128)(2,1)S(1)}, u32[]{:S(2)}, u32[]{:S(2)}) collective-permute-start(bf16[256,512]{1,0:T(8,128)(2,1)S(1)} %pad_maximum_fusion.1), channel_id=1, source_target_pairs={{56,0},{64,8},{72,16},{80,24},{88,32},{96,40},{104,48},{112,56},{1... | collective-permute-start | bytes 786440 | tf_op jit(solution)/shard_map/ppermute | solution.py:16
  204.6 7.3 %collective-permute-done.28 = bf16[256,512]{1,0:T(8,128)(2,1)S(1)} collective-permute-done((bf16[256,512]{1,0:T(8,128)(2,1)S(1)}, bf16[256,512]{1,0:T(8,128)(2,1)S(1)}, u32[]{:S(2)}, u32[]{:S(2)}) %collective-permute-start.28) | collective-permute-done | bytes 262176 | tf_op jit(solution)/shard_map/ppermute | solution.py:16
  218.8 40.4 %collective-permute-done.9 = bf16[256,512]{1,0:T(8,128)(2,1)S(1)} collective-permute-done((bf16[256,512]{1,0:T(8,128)(2,1)S(1)}, bf16[256,512]{1,0:T(8,128)(2,1)S(1)}, u32[]{:S(2)}, u32[]{:S(2)}) %collective-permute-start.9) | collective-permute-done | bytes 262176 | tf_op jit(solution)/shard_map/ppermute | solution.py:16
  259.2 7.4 %collective-permute-start.10 = (bf16[256,512]{1,0:T(8,128)(2,1)S(1)}, bf16[256,512]{1,0:T(8,128)(2,1)S(1)}, u32[]{:S(2)}, u32[]{:S(2)}) collective-permute-start(bf16[256,512]{1,0:T(8,128)(2,1)S(1)} %collective-permute-done.9), channel_id=1, source_target_pairs={{8,0},{16,8},{24,16},{32,24},{40,32},{48,40},{56,48},{64,56},{72,6... | collective-permute-start | bytes 786440 | tf_op jit(solution)/shard_map/ppermute | solution.py:16
  270.5 7.4 %collective-permute-start.11 = (bf16[256,512]{1,0:T(8,128)(2,1)S(1)}, bf16[256,512]{1,0:T(8,128)(2,1)}, u32[]{:S(2)}, u32[]{:S(2)}) collective-permute-start(bf16[256,512]{1,0:T(8,128)(2,1)S(1)} %collective-permute-done.10), channel_id=1, source_target_pairs={{8,0},{16,8},{24,16},{32,24},{40,32},{48,40},{56,48},{64,56},{72,6... | collective-permute-start | bytes 786440 | tf_op jit(solution)/shard_map/ppermute | solution.py:16
  284.1 7.2 %collective-permute-start.12 = (bf16[256,512]{1,0:T(8,128)(2,1)}, bf16[256,512]{1,0:T(8,128)(2,1)}, u32[]{:S(2)}, u32[]{:S(2)}) collective-permute-start(bf16[256,512]{1,0:T(8,128)(2,1)} %collective-permute-done.11), channel_id=1, source_target_pairs={{8,0},{16,8},{24,16},{32,24},{40,32},{48,40},{56,48},{64,56},{72,6... | collective-permute-start | bytes 786440 | tf_op jit(solution)/shard_map/ppermute | solution.py:16
  302.1 7.2 %collective-permute-start.13 = (bf16[256,512]{1,0:T(8,128)(2,1)}, bf16[256,512]{1,0:T(8,128)(2,1)S(1)}, u32[]{:S(2)}, u32[]{:S(2)}) collective-permute-start(bf16[256,512]{1,0:T(8,128)(2,1)} %collective-permute-done.12), channel_id=1, source_target_pairs={{8,0},{16,8},{24,16},{32,24},{40,32},{48,40},{56,48},{64,56},{72,6... | collective-permute-start | bytes 786440 | tf_op jit(solution)/shard_map/ppermute | solution.py:16
  314.6 7.2 %collective-permute-start.14 = (bf16[256,512]{1,0:T(8,128)(2,1)S(1)}, bf16[256,512]{1,0:T(8,128)(2,1)S(1)}, u32[]{:S(2)}, u32[]{:S(2)}) collective-permute-start(bf16[256,512]{1,0:T(8,128)(2,1)S(1)} %collective-permute-done.13), channel_id=1, source_target_pairs={{8,0},{16,8},{24,16},{32,24},{40,32},{48,40},{56,48},{64,56},{72,6... | collective-permute-start | bytes 786440 | tf_op jit(solution)/shard_map/ppermute | solution.py:16
  326.2 7.2 %collective-permute-start.15 = (bf16[256,512]{1,0:T(8,128)(2,1)S(1)}, bf16[256,512]{1,0:T(8,128)(2,1)S(1)}, u32[]{:S(2)}, u32[]{:S(2)}) collective-permute-start(bf16[256,512]{1,0:T(8,128)(2,1)S(1)} %collective-permute-done.14), channel_id=1, source_target_pairs={{8,0},{16,8},{24,16},{32,24},{40,32},{48,40},{56,48},{64,56},{72,6... | collective-permute-start | bytes 786440 | tf_op jit(solution)/shard_map/ppermute | solution.py:16
  355.7 37.7 %while.48 = (s32[]{:T(128)}, f32[2,256]{1,0:T(2,128)S(1)}, f32[2,256]{1,0:T(2,128)S(1)}, s32[1,256]{1,0:T(1,128)S(1)}, s32[17,256]{1,0:T(8,128)}, /*index=5*/s32...) while((s32[]{:T(128)}, f32[2,256]{1,0:T(2,128)S(1)}, ...), condition=%wide.region_5.6_spmd.clone, body=%wide.region_2.5_spmd.clone.sunk | while | flops 34540032 | bytes 1542280 | solution.py:98
  397.6 39.3 %while.49 = (s32[]{:T(128)}, f32[256,2,128]{0,2,1:T(8,128)S(1)}, bf16[17,256,2,128]{1,3,2,0:T(8,128)(2,1)}, s32[1,256]{1,0:T(1,128)S(1)}, s32[17,256]{1,0:T(8,12...) while((s32[]{:T(128)}, f32[256,2,128]{0,2,1:T(8,128)S(1)}, ...), condition=%wide.region_7.8_spmd.clone, body=%wide.region_6.7_spmd.clone.sunk | while | flops 67960832 | bytes 1060490 | solution.py:121
  447.2 60.5 %while.50 = (s32[]{:T(128)}, f32[256,2,128]{0,2,1:T(8,128)S(1)}, bf16[17,256,2,128]{3,1,2,0:T(8,128)(2,1)}, s32[1,256]{1,0:T(1,128)S(1)}, s32[17,256]{1,0:T(8,12...) while((s32[]{:T(128)}, f32[256,2,128]{0,2,1:T(8,128)S(1)}, ...), condition=%wide.region_10.11_spmd.clone, body=%wide.region_9.10_spmd.clone.sunk | while | flops 101777408 | bytes 2373278 | solution.py:141
  518.5 6.6 collective-permute-start.40
  532.2 6.0 collective-permute-start.43
  543.8 6.7 collective-permute-start.45
  550.5 6.2 collective-permute-start.46
  566.2 80.9 %while.51 = (s32[]{:T(128)}, f32[256,2,128]{0,2,1:T(8,128)S(1)}, f32[256,2,128]{0,2,1:T(8,128)S(1)}, bf16[17,256,2,128]{1,3,2,0:T(8,128)(2,1)}, s32[17,256]{1,0:...) while((s32[]{:T(128)}, f32[256,2,128]{0,2,1:T(8,128)S(1)}, ...), condition=%wide.region_12.13_spmd.clone, body=%wide.region_11.12_spmd.clone.sunk | while | flops 135593984 | bytes 3821748 | solution.py:176
  648.0 6.3 all-to-all-start.5
  655.2 5.7 all-to-all-done.5
  665.0 5.8 all-to-all-done.6
  (584 shorter events, 403.4 us)
Async XLA Ops:
  39.4 21.9 %collective-permute-start.16 = (bf16[256,512]{1,0:T(8,128)(2,1)S(1)}, bf16[256,512]{1,0:T(8,128)(2,1)S(1)}, u32[]{:S(2)}, u32[]{:S(2)}) collective-permute-start(bf16[256,512]{1,0:T(8,128)(2,1)S(1)} %pad_maximum_fusion.1), channel_id=1, source_target_pairs={{0,8},{8,16},{16,24},{24,32},{32,40},{40,48},{48,56},{56,64},{64,7... | collective-permute-start | bytes 786440 | tf_op jit(solution)/shard_map/ppermute | solution.py:16
  46.0 129.9 %collective-permute-start = (bf16[256,512]{1,0:T(8,128)(2,1)S(1)}, bf16[256,512]{1,0:T(8,128)(2,1)S(1)}, u32[]{:S(2)}, u32[]{:S(2)}) collective-permute-start(bf16[256,512]{1,0:T(8,128)(2,1)S(1)} %pad_maximum_fusion), channel_id=1, source_target_pairs={{0,8},{8,16},{16,24},{24,32},{32,40},{40,48},{48,56},{56,64},{64,7... | collective-permute-start | bytes 786440 | tf_op jit(solution)/shard_map/ppermute | solution.py:16
  47.9 154.4 %collective-permute-start.8 = (bf16[256,512]{1,0:T(8,128)(2,1)S(1)}, bf16[256,512]{1,0:T(8,128)(2,1)S(1)}, u32[]{:S(2)}, u32[]{:S(2)}) collective-permute-start(bf16[256,512]{1,0:T(8,128)(2,1)S(1)} %pad_maximum_fusion), channel_id=1, source_target_pairs={{8,0},{16,8},{24,16},{32,24},{40,32},{48,40},{56,48},{64,56},{72,6... | collective-permute-start | bytes 786440 | tf_op jit(solution)/shard_map/ppermute | solution.py:16
  61.4 29.3 %collective-permute-start.19 = (bf16[256,512]{1,0:T(8,128)(2,1)S(1)}, bf16[256,512]{1,0:T(8,128)(2,1)S(1)}, u32[]{:S(2)}, u32[]{:S(2)}) collective-permute-start(bf16[256,512]{1,0:T(8,128)(2,1)S(1)} %pad_maximum_fusion.1), channel_id=1, source_target_pairs={{0,32},{8,40},{16,48},{24,56},{32,64},{40,72},{48,80},{56,88},{64,... | collective-permute-start | bytes 786440 | tf_op jit(solution)/shard_map/ppermute | solution.py:16
  71.0 32.2 %collective-permute-start.20 = (bf16[256,512]{1,0:T(8,128)(2,1)S(1)}, bf16[256,512]{1,0:T(8,128)(2,1)S(1)}, u32[]{:S(2)}, u32[]{:S(2)}) collective-permute-start(bf16[256,512]{1,0:T(8,128)(2,1)S(1)} %pad_maximum_fusion.1), channel_id=1, source_target_pairs={{0,40},{8,48},{16,56},{24,64},{32,72},{40,80},{48,88},{56,96},{64,... | collective-permute-start | bytes 786440 | tf_op jit(solution)/shard_map/ppermute | solution.py:16
  76.4 49.0 %collective-permute-start.21 = (bf16[256,512]{1,0:T(8,128)(2,1)S(1)}, bf16[256,512]{1,0:T(8,128)(2,1)S(1)}, u32[]{:S(2)}, u32[]{:S(2)}) collective-permute-start(bf16[256,512]{1,0:T(8,128)(2,1)S(1)} %pad_maximum_fusion.1), channel_id=1, source_target_pairs={{0,48},{8,56},{16,64},{24,72},{32,80},{40,88},{48,96},{56,104},{64... | collective-permute-start | bytes 786440 | tf_op jit(solution)/shard_map/ppermute | solution.py:16
  90.7 46.4 %collective-permute-start.22 = (bf16[256,512]{1,0:T(8,128)(2,1)S(1)}, bf16[256,512]{1,0:T(8,128)(2,1)S(1)}, u32[]{:S(2)}, u32[]{:S(2)}) collective-permute-start(bf16[256,512]{1,0:T(8,128)(2,1)S(1)} %pad_maximum_fusion.1), channel_id=1, source_target_pairs={{0,56},{8,64},{16,72},{24,80},{32,88},{40,96},{48,104},{56,112},{6... | collective-permute-start | bytes 786440 | tf_op jit(solution)/shard_map/ppermute | solution.py:16
  103.3 41.7 %collective-permute-start.23 = (bf16[256,512]{1,0:T(8,128)(2,1)S(1)}, bf16[256,512]{1,0:T(8,128)(2,1)S(1)}, u32[]{:S(2)}, u32[]{:S(2)}) collective-permute-start(bf16[256,512]{1,0:T(8,128)(2,1)S(1)} %pad_maximum_fusion.1), channel_id=1, source_target_pairs={{0,64},{8,72},{16,80},{24,88},{32,96},{40,104},{48,112},{56,120},{... | collective-permute-start | bytes 786440 | tf_op jit(solution)/shard_map/ppermute | solution.py:16
  125.4 38.6 %collective-permute-start.24 = (bf16[256,512]{1,0:T(8,128)(2,1)S(1)}, bf16[256,512]{1,0:T(8,128)(2,1)S(1)}, u32[]{:S(2)}, u32[]{:S(2)}) collective-permute-start(bf16[256,512]{1,0:T(8,128)(2,1)S(1)} %pad_maximum_fusion.1), channel_id=1, source_target_pairs={{8,0},{16,8},{24,16},{32,24},{40,32},{48,40},{56,48},{64,56},{72,6... | collective-permute-start | bytes 786440 | tf_op jit(solution)/shard_map/ppermute | solution.py:16
  137.1 29.6 %collective-permute-start.25 = (bf16[256,512]{1,0:T(8,128)(2,1)S(1)}, bf16[256,512]{1,0:T(8,128)(2,1)S(1)}, u32[]{:S(2)}, u32[]{:S(2)}) collective-permute-start(bf16[256,512]{1,0:T(8,128)(2,1)S(1)} %pad_maximum_fusion.1), channel_id=1, source_target_pairs={{16,0},{24,8},{32,16},{40,24},{48,32},{56,40},{64,48},{72,56},{80,... | collective-permute-start | bytes 786440 | tf_op jit(solution)/shard_map/ppermute | solution.py:16
  144.9 34.5 %collective-permute-start.26 = (bf16[256,512]{1,0:T(8,128)(2,1)S(1)}, bf16[256,512]{1,0:T(8,128)(2,1)S(1)}, u32[]{:S(2)}, u32[]{:S(2)}) collective-permute-start(bf16[256,512]{1,0:T(8,128)(2,1)S(1)} %pad_maximum_fusion.1), channel_id=1, source_target_pairs={{24,0},{32,8},{40,16},{48,24},{56,32},{64,40},{72,48},{80,56},{88,... | collective-permute-start | bytes 786440 | tf_op jit(solution)/shard_map/ppermute | solution.py:16
  164.0 20.6 %collective-permute-start.27 = (bf16[256,512]{1,0:T(8,128)(2,1)S(1)}, bf16[256,512]{1,0:T(8,128)(2,1)S(1)}, u32[]{:S(2)}, u32[]{:S(2)}) collective-permute-start(bf16[256,512]{1,0:T(8,128)(2,1)S(1)} %pad_maximum_fusion.1), channel_id=1, source_target_pairs={{32,0},{40,8},{48,16},{56,24},{64,32},{72,40},{80,48},{88,56},{96,... | collective-permute-start | bytes 786440 | tf_op jit(solution)/shard_map/ppermute | solution.py:16
  166.7 45.2 %collective-permute-start.28 = (bf16[256,512]{1,0:T(8,128)(2,1)S(1)}, bf16[256,512]{1,0:T(8,128)(2,1)S(1)}, u32[]{:S(2)}, u32[]{:S(2)}) collective-permute-start(bf16[256,512]{1,0:T(8,128)(2,1)S(1)} %pad_maximum_fusion.1), channel_id=1, source_target_pairs={{40,0},{48,8},{56,16},{64,24},{72,32},{80,40},{88,48},{96,56},{104... | collective-permute-start | bytes 786440 | tf_op jit(solution)/shard_map/ppermute | solution.py:16
  175.8 42.2 %collective-permute-start.29 = (bf16[256,512]{1,0:T(8,128)(2,1)S(1)}, bf16[256,512]{1,0:T(8,128)(2,1)S(1)}, u32[]{:S(2)}, u32[]{:S(2)}) collective-permute-start(bf16[256,512]{1,0:T(8,128)(2,1)S(1)} %pad_maximum_fusion.1), channel_id=1, source_target_pairs={{48,0},{56,8},{64,16},{72,24},{80,32},{88,40},{96,48},{104,56},{11... | collective-permute-start | bytes 786440 | tf_op jit(solution)/shard_map/ppermute | solution.py:16
  179.5 34.3 %collective-permute-start.1 = (bf16[256,512]{1,0:T(8,128)(2,1)S(1)}, bf16[256,512]{1,0:T(8,128)(2,1)S(1)}, u32[]{:S(2)}, u32[]{:S(2)}) collective-permute-start(bf16[256,512]{1,0:T(8,128)(2,1)S(1)} %collective-permute-done), channel_id=1, source_target_pairs={{0,8},{8,16},{16,24},{24,32},{32,40},{40,48},{48,56},{56,64},{64,7... | collective-permute-start | bytes 786440 | tf_op jit(solution)/shard_map/ppermute | solution.py:16
  184.6 84.0 %collective-permute-start.30 = (bf16[256,512]{1,0:T(8,128)(2,1)S(1)}, bf16[256,512]{1,0:T(8,128)(2,1)S(1)}, u32[]{:S(2)}, u32[]{:S(2)}) collective-permute-start(bf16[256,512]{1,0:T(8,128)(2,1)S(1)} %pad_maximum_fusion.1), channel_id=1, source_target_pairs={{56,0},{64,8},{72,16},{80,24},{88,32},{96,40},{104,48},{112,56},{1... | collective-permute-start | bytes 786440 | tf_op jit(solution)/shard_map/ppermute | solution.py:16
  202.3 67.0 %collective-permute-start.31 = (bf16[256,512]{1,0:T(8,128)(2,1)S(1)}, bf16[256,512]{1,0:T(8,128)(2,1)S(1)}, u32[]{:S(2)}, u32[]{:S(2)}) collective-permute-start(bf16[256,512]{1,0:T(8,128)(2,1)S(1)} %pad_maximum_fusion.1), channel_id=1, source_target_pairs={{64,0},{72,8},{80,16},{88,24},{96,32},{104,40},{112,48},{120,56},{... | collective-permute-start | bytes 786440 | tf_op jit(solution)/shard_map/ppermute | solution.py:16
  211.9 47.3 %collective-permute-start.9 = (bf16[256,512]{1,0:T(8,128)(2,1)S(1)}, bf16[256,512]{1,0:T(8,128)(2,1)S(1)}, u32[]{:S(2)}, u32[]{:S(2)}) collective-permute-start(bf16[256,512]{1,0:T(8,128)(2,1)S(1)} %collective-permute-done.8), channel_id=1, source_target_pairs={{8,0},{16,8},{24,16},{32,24},{40,32},{48,40},{56,48},{64,56},{72,6... | collective-permute-start | bytes 786440 | tf_op jit(solution)/shard_map/ppermute | solution.py:16
  213.8 52.8 %collective-permute-start.2 = (bf16[256,512]{1,0:T(8,128)(2,1)S(1)}, bf16[256,512]{1,0:T(8,128)(2,1)S(1)}, u32[]{:S(2)}, u32[]{:S(2)}) collective-permute-start(bf16[256,512]{1,0:T(8,128)(2,1)S(1)} %collective-permute-done.1), channel_id=1, source_target_pairs={{0,8},{8,16},{16,24},{24,32},{32,40},{40,48},{48,56},{56,64},{64,7... | collective-permute-start | bytes 786440 | tf_op jit(solution)/shard_map/ppermute | solution.py:16
  278.1 20.3 %collective-permute-start.4 = (bf16[256,512]{1,0:T(8,128)(2,1)}, bf16[256,512]{1,0:T(8,128)(2,1)}, u32[]{:S(2)}, u32[]{:S(2)}) collective-permute-start(bf16[256,512]{1,0:T(8,128)(2,1)} %collective-permute-done.3), channel_id=1, source_target_pairs={{0,8},{8,16},{16,24},{24,32},{32,40},{40,48},{48,56},{56,64},{64,7... | collective-permute-start | bytes 786440 | tf_op jit(solution)/shard_map/ppermute | solution.py:16
  437.5 75.2 %collective-permute-start.32 = (f32[256,4]{0,1:T(4,128)S(1)}, f32[256,4]{0,1:T(4,128)S(1)}, u32[]{:S(2)}, u32[]{:S(2)}) collective-permute-start(f32[256,4]{0,1:T(4,128)S(1)} %pad_maximum_fusion.2), channel_id=1, source_target_pairs={{0,8},{8,16},{16,24},{24,32},{32,40},{40,48},{48,56},{56,64},{64,7... | collective-permute-start | bytes 12296 | tf_op jit(solution)/shard_map/ppermute | solution.py:16
  439.4 75.2 %collective-permute-start.33 = (f32[256,4]{0,1:T(4,128)S(1)}, f32[256,4]{0,1:T(4,128)S(1)}, u32[]{:S(2)}, u32[]{:S(2)}) collective-permute-start(f32[256,4]{0,1:T(4,128)S(1)} %pad_maximum_fusion.2), channel_id=1, source_target_pairs={{0,16},{8,24},{16,32},{24,40},{32,48},{40,56},{48,64},{56,72},{64,... | collective-permute-start | bytes 12296 | tf_op jit(solution)/shard_map/ppermute | solution.py:16
  441.4 75.2 %collective-permute-start.34 = (f32[256,4]{0,1:T(4,128)S(1)}, f32[256,4]{0,1:T(4,128)S(1)}, u32[]{:S(2)}, u32[]{:S(2)}) collective-permute-start(f32[256,4]{0,1:T(4,128)S(1)} %pad_maximum_fusion.2), channel_id=1, source_target_pairs={{0,24},{8,32},{16,40},{24,48},{32,56},{40,64},{48,72},{56,80},{64,... | collective-permute-start | bytes 12296 | tf_op jit(solution)/shard_map/ppermute | solution.py:16
  443.3 75.2 %collective-permute-start.35 = (f32[256,4]{0,1:T(4,128)S(1)}, f32[256,4]{0,1:T(4,128)S(1)}, u32[]{:S(2)}, u32[]{:S(2)}) collective-permute-start(f32[256,4]{0,1:T(4,128)S(1)} %pad_maximum_fusion.2), channel_id=1, source_target_pairs={{0,32},{8,40},{16,48},{24,56},{32,64},{40,72},{48,80},{56,88},{64,... | collective-permute-start | bytes 12296 | tf_op jit(solution)/shard_map/ppermute | solution.py:16
  445.2 79.9 %collective-permute-start.36 = (f32[256,4]{0,1:T(4,128)S(1)}, f32[256,4]{0,1:T(4,128)S(1)}, u32[]{:S(2)}, u32[]{:S(2)}) collective-permute-start(f32[256,4]{0,1:T(4,128)S(1)} %pad_maximum_fusion.2), channel_id=1, source_target_pairs={{0,40},{8,48},{16,56},{24,64},{32,72},{40,80},{48,88},{56,96},{64,... | collective-permute-start | bytes 12296 | tf_op jit(solution)/shard_map/ppermute | solution.py:16
  508.6 139.4 %all-to-all-start.4 = ((bf16[8,32,256]{2,1,0:T(8,128)(2,1)}), bf16[8,32,256]{2,1,0:T(8,128)(2,1)S(1)}, u32[]{:S(2)}, u32[]{:S(2)}) async-start(bf16[8,32,256]{2,1,0:T(8,128)(2,1)} %all_to_all.108), calls=%async_computation.4 | async-start | bytes 262144 | tf_op jit(solution)/shard_map/all_to_all | solution.py:187
  516.6 21.6 %collective-permute-start.39 = (f32[256,4]{0,1:T(4,128)S(1)}, f32[256,4]{0,1:T(4,128)S(1)}, u32[]{:S(2)}, u32[]{:S(2)}) collective-permute-start(f32[256,4]{0,1:T(4,128)S(1)} %pad_maximum_fusion.2), channel_id=1, source_target_pairs={{0,64},{8,72},{16,80},{24,88},{32,96},{40,104},{48,112},{56,120},{... | collective-permute-start | bytes 12296 | tf_op jit(solution)/shard_map/ppermute | solution.py:16
  518.5 25.2 %collective-permute-start.40 = (f32[256,4]{0,1:T(4,128)S(1)}, f32[256,4]{0,1:T(4,128)S(1)}, u32[]{:S(2)}, u32[]{:S(2)}) collective-permute-start(f32[256,4]{0,1:T(4,128)S(1)} %pad_maximum_fusion.2), channel_id=1, source_target_pairs={{8,0},{16,8},{24,16},{32,24},{40,32},{48,40},{56,48},{64,56},{72,6... | collective-permute-start | bytes 12296 | tf_op jit(solution)/shard_map/ppermute | solution.py:16
  525.2 25.3 %collective-permute-start.41 = (f32[256,4]{0,1:T(4,128)S(1)}, f32[256,4]{0,1:T(4,128)S(1)}, u32[]{:S(2)}, u32[]{:S(2)}) collective-permute-start(f32[256,4]{0,1:T(4,128)S(1)} %pad_maximum_fusion.2), channel_id=1, source_target_pairs={{16,0},{24,8},{32,16},{40,24},{48,32},{56,40},{64,48},{72,56},{80,... | collective-permute-start | bytes 12296 | tf_op jit(solution)/shard_map/ppermute | solution.py:16
  528.8 27.9 %collective-permute-start.42 = (f32[256,4]{0,1:T(4,128)S(1)}, f32[256,4]{0,1:T(4,128)S(1)}, u32[]{:S(2)}, u32[]{:S(2)}) collective-permute-start(f32[256,4]{0,1:T(4,128)S(1)} %pad_maximum_fusion.2), channel_id=1, source_target_pairs={{24,0},{32,8},{40,16},{48,24},{56,32},{64,40},{72,48},{80,56},{88,... | collective-permute-start | bytes 12296 | tf_op jit(solution)/shard_map/ppermute | solution.py:16
  532.2 28.7 %collective-permute-start.43 = (f32[256,4]{0,1:T(4,128)S(1)}, f32[256,4]{0,1:T(4,128)S(1)}, u32[]{:S(2)}, u32[]{:S(2)}) collective-permute-start(f32[256,4]{0,1:T(4,128)S(1)} %pad_maximum_fusion.2), channel_id=1, source_target_pairs={{32,0},{40,8},{48,16},{56,24},{64,32},{72,40},{80,48},{88,56},{96,... | collective-permute-start | bytes 12296 | tf_op jit(solution)/shard_map/ppermute | solution.py:16
  538.2 22.8 %collective-permute-start.44 = (f32[256,4]{0,1:T(4,128)S(1)}, f32[256,4]{0,1:T(4,128)S(1)}, u32[]{:S(2)}, u32[]{:S(2)}) collective-permute-start(f32[256,4]{0,1:T(4,128)S(1)} %pad_maximum_fusion.2), channel_id=1, source_target_pairs={{40,0},{48,8},{56,16},{64,24},{72,32},{80,40},{88,48},{96,56},{104... | collective-permute-start | bytes 12296 | tf_op jit(solution)/shard_map/ppermute | solution.py:16
  (39 other events, 1042.1 us)
where the time goes:
time: 683 us; the launch traced here: 672 us
  starting transfers between devices  267 us (39%)
  matrix products  136 us (20%)
  local copies, waits for them, and re-layouts  135 us (20%)
  waiting for transfers between devices  112 us (16%)
  other arithmetic  17.1 us (3%)
    ppermute x48, starting transfers between devices, passed_along(): return lax.ppermute(block, axis, route)  236 us
    ppermute x48, waiting for transfers between devices, passed_along(): return lax.ppermute(block, axis, route)  83.3 us
    dynamic_slice x85, local copies, waits for them, and re-layouts, shards(): lax.scan(stats_step, stats_start, (k_tiles, tile_pos, tile_docs))  66.7 us
    unnamed x83, local copies, waits for them, and re-layouts  35.4 us
    dot_general x17, matrix products, grad_step(): jnp.einsum('hqk,khd->qhd', d_scores, k_tile, preferred_element_type=jnp.f...  25 us
    dot_general x17, matrix products, output_step(): jnp.einsum('hqk,khd->qhd', weights.astype(jnp.bfloat16), v_tile, preferre...  24 us
    dot_general x17, matrix products, key_step(): jnp.einsum('hqk,qhd->khd', d_scores, q_tile, preferred_element_type=jnp.f...  22.8 us
    dot_general x17, matrix products, key_step(): jnp.einsum('qhd,khd->hqk', q_tile, k_heads, preferred_element_type=jnp.fl...  20.7 us
  transfers between devices with their start and end apart: 55, of which 17 were waited for; matrix products, arithmetic and copies ran while one was open for 29% of the time, Pallas kernels for 0%

commit v1 on v0

v1 whole, which is shorter than its diff:
```python
import jax
import jax.numpy as jnp
from jax import lax
from jax.experimental import pallas as pl
from jax.experimental.pallas import tpu as pltpu
from jax.sharding import PartitionSpec as P

HD = 128
HEADS = 16
ROWS = 32
SEG = 512
SEGS = 32
NDOC = 32
TOKENS = SEG * SEGS
WIN = 2 * SEG
QB = 256
KB = 128
SCALE = 1.0 / HD**0.5
LOG2E = 1.4426950408889634
AXES = ("ctx", "head")
MASKED = -1e30


def device_of(segment, slot):
    column = slot % 4
    if segment < SEGS // 2:
        return (4 * segment + slot // 4) * 8 + column
    return (4 * (SEGS - 1 - segment) + 3 - slot // 4) * 8 + 4 + column


GROUPS = [[device_of(s, i) for i in range(16)] for s in range(SEGS)]
TO_NEXT = [(device_of(s, i), device_of((s + 1) % SEGS, i)) for s in range(SEGS) for i in range(16)]
TO_PREV = [(target, source) for source, target in TO_NEXT]


def to_next(block):
    return lax.ppermute(block, AXES, TO_NEXT)


def to_prev(block):
    return lax.ppermute(block, AXES, TO_PREV)


def exchange(chunks):
    return lax.all_to_all(
        chunks, AXES, split_axis=0, concat_axis=0, axis_index_groups=GROUPS, tiled=True
    )


def place():
    ctx = lax.axis_index("ctx")
    head = lax.axis_index("head")
    lower = head < 4
    segment = jnp.where(lower, ctx // 4, SEGS - 1 - ctx // 4)
    slot = jnp.where(lower, ctx % 4, 3 - ctx % 4) * 4 + head % 4
    return segment.astype(jnp.int32), slot.astype(jnp.int32)


def doc_table(lengths_ref):
    table = []
    first = jnp.int32(0)
    for doc in range(NDOC):
        end = first + lengths_ref[doc]
        middle = lax.shift_right_logical(first + end, 1)
        table.append((first, end, lax.shift_right_logical(middle, 9)))
        first = end
    return table


def halo_split(table, segment):
    split = jnp.int32(0)
    for first, end, owner in table:
        split = jnp.maximum(split, jnp.where(owner == segment, end - (segment + 1) * SEG, 0))
    return split


def own_split(table, segment):
    head_end = jnp.int32(0)
    tail_start = jnp.int32(SEG)
    for first, end, owner in table:
        head_end = jnp.maximum(head_end, jnp.where(owner == segment - 1, end - segment * SEG, 0))
        tail_start = jnp.minimum(
            tail_start, jnp.where(owner == segment + 1, first - segment * SEG, SEG)
        )
    return head_end, tail_start


def pick(condition, left, right):
    chosen = jnp.where(condition, left.astype(jnp.float32), right.astype(jnp.float32))
    return chosen.astype(jnp.bfloat16)


def pack_kernel(q_ref, d_ref, k_ref, v_ref, rows_ref, chunk_ref):
    rows_ref[0:ROWS, :] = q_ref[...]
    rows_ref[ROWS : 2 * ROWS, :] = d_ref[...]
    for h in range(HEADS):
        chunk_ref[h, 0:ROWS, :] = k_ref[:, h * HD : (h + 1) * HD]
        chunk_ref[h, ROWS : 2 * ROWS, :] = v_ref[:, h * HD : (h + 1) * HD]


def halo_kernel(lengths_ref, q_ref, d_ref, before_ref, after_ref, chunk_ref):
    segment, slot = place()
    split = halo_split(doc_table(lengths_ref), segment)
    row = slot * ROWS + lax.broadcasted_iota(jnp.int32, (ROWS, HD), 0)
    after = row < split
    for h in range(HEADS):
        cols = slice(h * HD, (h + 1) * HD)
        chunk_ref[h, 0:ROWS, :] = q_ref[:, cols]
        chunk_ref[h, ROWS : 2 * ROWS, :] = d_ref[:, cols]
        for part in range(2):
            rows = slice(part * ROWS, (part + 1) * ROWS)
            chunk_ref[h, (2 + part) * ROWS : (3 + part) * ROWS, :] = pick(
                after, after_ref[rows, cols], before_ref[rows, cols]
            )


def attention_kernel(
    lengths_ref,
    own_ref,
    before_ref,
    after_ref,
    qd_ref,
    halo_out,
    own_out,
    dq_out,
    q_win,
    d_win,
    k_win,
    v_win,
    s_buf,
    dp_buf,
    dk_acc,
    dv_acc,
):
    segment, unused_slot = place()
    table = doc_table(lengths_ref)
    split = halo_split(table, segment)
    tile_row = lax.broadcasted_iota(jnp.int32, (ROWS, HD), 0)
    for i in range(16):
        halo = slice(i * ROWS, (i + 1) * ROWS)
        mine = slice(SEG + i * ROWS, SEG + (i + 1) * ROWS)
        after = tile_row + i * ROWS < split
        k_win[halo, :] = pick(after, after_ref[i, 0:ROWS, :], before_ref[i, 0:ROWS, :])
        v_win[halo, :] = pick(
            after, after_ref[i, ROWS : 2 * ROWS, :], before_ref[i, ROWS : 2 * ROWS, :]
        )
        k_win[mine, :] = own_ref[i, 0:ROWS, :]
        v_win[mine, :] = own_ref[i, ROWS : 2 * ROWS, :]
        q_win[mine, :] = qd_ref[i, 0:ROWS, :]
        d_win[mine, :] = qd_ref[i, ROWS : 2 * ROWS, :]
        q_win[halo, :] = qd_ref[i, 2 * ROWS : 3 * ROWS, :]
        d_win[halo, :] = qd_ref[i, 3 * ROWS : 4 * ROWS, :]
    base = (segment - 1) * SEG
    contract_last = (((1,), (1,)), ((), ()))
    contract_first = (((0,), (0,)), ((), ()))
    for qb in range(WIN // QB):
        index = qb * QB + lax.broadcasted_iota(jnp.int32, (1, QB), 1)
        q_pos = base + index + jnp.where(index < split, WIN, 0)
        q_first = jnp.full((1, QB), -TOKENS, jnp.int32)
        for first, unused_end, unused_owner in table:
            q_first = jnp.where(q_pos >= first, first, q_first)
        q_first = jnp.where(q_pos >= TOKENS, TOKENS, q_first)
        rows = slice(qb * QB, (qb + 1) * QB)
        q_rows = q_win[rows, :]
        d_rows = d_win[rows, :]
        top = jnp.full((8, QB), MASKED, jnp.float32)
        for kb in range(WIN // KB):
            keys = slice(kb * KB, (kb + 1) * KB)
            k_index = kb * KB + lax.broadcasted_iota(jnp.int32, (KB, QB), 0)
            k_pos = base + k_index
            if kb * KB < SEG:
                k_pos = k_pos + jnp.where(k_index < split, WIN, 0)
            allowed = (k_pos >= q_first) & (k_pos <= q_pos)
            scores = lax.dot_general(
                k_win[keys, :], q_rows, contract_last, preferred_element_type=jnp.float32
            )
            scores = jnp.where(allowed, scores, MASKED)
            s_buf[keys, :] = scores
            top = jnp.maximum(top, jnp.max(scores.reshape(KB // 8, 8, QB), axis=0))
        top = jnp.max(top, axis=0, keepdims=True)
        total = jnp.zeros((8, QB), jnp.float32)
        for kb in range(WIN // KB):
            keys = slice(kb * KB, (kb + 1) * KB)
            terms = jnp.exp2((s_buf[keys, :] - top) * (SCALE * LOG2E))
            s_buf[keys, :] = terms
            total = total + jnp.sum(terms.reshape(KB // 8, 8, QB), axis=0)
        inverse = 1.0 / jnp.sum(total, axis=0, keepdims=True)
        delta = jnp.zeros((8, QB), jnp.float32)
        for kb in range(WIN // KB):
            keys = slice(kb * KB, (kb + 1) * KB)
            probs = s_buf[keys, :] * inverse
            probs_b = probs.astype(jnp.bfloat16)
            d_probs = lax.dot_general(
                v_win[keys, :], d_rows, contract_last, preferred_element_type=jnp.float32
            )
            s_buf[keys, :] = probs
            dp_buf[keys, :] = d_probs
            delta = delta + jnp.sum(
                (probs_b.astype(jnp.float32) * d_probs).reshape(KB // 8, 8, QB), axis=0
            )
            part = jnp.dot(probs_b, d_rows, preferred_element_type=jnp.float32)
            dv_acc[keys, :] = part if qb == 0 else dv_acc[keys, :] + part
        delta = jnp.sum(delta, axis=0, keepdims=True)
        dq = jnp.zeros((QB, HD), jnp.float32)
        for kb in range(WIN // KB):
            keys = slice(kb * KB, (kb + 1) * KB)
            d_scores = (s_buf[keys, :] * (dp_buf[keys, :] - delta)).astype(jnp.bfloat16)
            part = jnp.dot(d_scores, q_rows, preferred_element_type=jnp.float32)
            dk_acc[keys, :] = part if qb == 0 else dk_acc[keys, :] + part
            dq = dq + lax.dot_general(
                d_scores, k_win[keys, :], contract_first, preferred_element_type=jnp.float32
            )
        dq = (dq * SCALE).astype(jnp.bfloat16)
        for i in range(QB // ROWS):
            index = qb * (QB // ROWS) + i
            place_row = (1 - index // 16) * ROWS
            dq_out[index % 16, place_row : place_row + ROWS, :] = dq[i * ROWS : (i + 1) * ROWS, :]
    halo_out[0:SEG, :] = (dk_acc[0:SEG, :] * SCALE).astype(jnp.bfloat16)
    halo_out[SEG:WIN, :] = dv_acc[0:SEG, :].astype(jnp.bfloat16)
    own_out[0:SEG, :] = (dk_acc[SEG:WIN, :] * SCALE).astype(jnp.bfloat16)
    own_out[SEG:WIN, :] = dv_acc[SEG:WIN, :].astype(jnp.bfloat16)


def merge_kernel(lengths_ref, own_ref, before_ref, after_ref, chunk_ref):
    segment, unused_slot = place()
    head_end, tail_start = own_split(doc_table(lengths_ref), segment)
    tile_row = lax.broadcasted_iota(jnp.int32, (ROWS, HD), 0)
    for i in range(16):
        row = tile_row + i * ROWS
        for part in range(2):
            rows = slice(part * SEG + i * ROWS, part * SEG + (i + 1) * ROWS)
            chosen = jnp.where(
                row >= tail_start,
                after_ref[rows, :].astype(jnp.float32),
                own_ref[rows, :].astype(jnp.float32),
            )
            chosen = jnp.where(row < head_end, before_ref[rows, :].astype(jnp.float32), chosen)
            chunk_ref[i, part * ROWS : (part + 1) * ROWS, :] = chosen.astype(jnp.bfloat16)


def finish_kernel(
    lengths_ref,
    kv_ref,
    dq_ref,
    before_ref,
    after_ref,
    key_prior_ref,
    value_prior_ref,
    dq_out,
    dk_out,
    dv_out,
    key_out,
    value_out,
):
    segment, slot = place()
    head_end, tail_start = own_split(doc_table(lengths_ref), segment)
    row = slot * ROWS + lax.broadcasted_iota(jnp.int32, (ROWS, HD), 0)
    from_after = row >= tail_start
    from_before = row < head_end
    for h in range(HEADS):
        cols = slice(h * HD, (h + 1) * HD)
        chosen = jnp.where(
            from_after,
            after_ref[h].astype(jnp.float32),
            dq_ref[h, 0:ROWS, :].astype(jnp.float32),
        )
        chosen = jnp.where(from_before, before_ref[h].astype(jnp.float32), chosen)
        dq_out[:, cols] = chosen.astype(jnp.bfloat16)
        dk = kv_ref[h, 0:ROWS, :]
        dv = kv_ref[h, ROWS : 2 * ROWS, :]
        dk_out[:, cols] = dk
        dv_out[:, cols] = dv
        dk = dk.astype(jnp.float32)
        dv = dv.astype(jnp.float32)
        key_out[:, cols] = key_prior_ref[:, cols] + dk * dk
        value_out[:, cols] = value_prior_ref[:, cols] + dv * dv


SMEM = pl.BlockSpec(memory_space=pltpu.SMEM)
VMEM = pl.BlockSpec(memory_space=pltpu.VMEM)


def bf16(*shape):
    return jax.ShapeDtypeStruct(shape, jnp.bfloat16)


def call(kernel, inputs, outputs, scratch=(), smem=1, limit=16 << 20):
    return pl.pallas_call(
        kernel,
        in_specs=[SMEM] * smem + [VMEM] * (len(inputs) - smem),
        out_specs=[VMEM] * len(outputs),
        out_shape=list(outputs),
        scratch_shapes=list(scratch),
        compiler_params=pltpu.CompilerParams(vmem_limit_bytes=limit),
        name=kernel.__name__,
    )(*inputs)


def shards(queries, keys, values, d_attn, fisher_key_prior, fisher_value_prior, doc_lengths):
    width = HEADS * HD
    qd_rows, kv_chunks = call(
        pack_kernel,
        (queries, d_attn, keys, values),
        (bf16(2 * ROWS, width), bf16(HEADS, 2 * ROWS, HD)),
        smem=0,
    )
    qd_before = to_next(qd_rows)
    qd_after = to_prev(qd_rows)
    kv_own = exchange(kv_chunks)
    kv_before = to_next(kv_own)
    kv_after = to_prev(kv_own)
    (qd_chunks,) = call(
        halo_kernel,
        (doc_lengths, queries, d_attn, qd_before, qd_after),
        (bf16(HEADS, 4 * ROWS, HD),),
    )
    qd_heads = exchange(qd_chunks)
    window = [pltpu.VMEM((WIN, HD), jnp.bfloat16)] * 4
    halo_kv, own_kv, dq_chunks = call(
        attention_kernel,
        (doc_lengths, kv_own, kv_before, kv_after, qd_heads),
        (bf16(WIN, HD), bf16(WIN, HD), bf16(16, 2 * ROWS, HD)),
        scratch=window
        + [pltpu.VMEM((WIN, QB), jnp.float32)] * 2
        + [pltpu.VMEM((WIN, HD), jnp.float32)] * 2,
        limit=32 << 20,
    )
    halo_before = to_next(halo_kv)
    halo_after = to_prev(halo_kv)
    dq_heads = exchange(dq_chunks)
    dq_halo = dq_heads[:, ROWS:, :]
    dq_before = to_next(dq_halo)
    dq_after = to_prev(dq_halo)
    (kv_back,) = call(
        merge_kernel,
        (doc_lengths, own_kv, halo_before, halo_after),
        (bf16(16, 2 * ROWS, HD),),
    )
    kv_heads = exchange(kv_back)
    wide = jax.ShapeDtypeStruct((ROWS, width), jnp.float32)
    return call(
        finish_kernel,
        (doc_lengths, kv_heads, dq_heads, dq_before, dq_after, fisher_key_prior, fisher_value_prior),
        (bf16(ROWS, width), bf16(ROWS, width), bf16(ROWS, width), wide, wide),
    )


def solution(mesh):
    tokens = P(AXES, None)
    return jax.shard_map(
        shards,
        mesh=mesh,
        in_specs=(tokens,) * 6 + (P(),),
        out_specs=(tokens,) * 5,
        check_vma=False,
    )
```

time: 683 us -> 133 us (0.19)
  the two profiles are of different devices: /device:TPU:16 before, /device:TPU:51 now
where the time goes in v1:
time: 133 us
  starting transfers between devices  64.2 us (48%)
  waiting for transfers between devices  52.5 us (39%)
  Pallas kernels  11.6 us (9%)
  local copies, waits for them, and re-layouts  3.64 us (3%)
    all_to_all x4, starting transfers between devices, exchange(): lax.all_to_all(chunks, AXES, split_axis=0, concat_axis=0, axis_index_grou...  33.2 us
    ppermute x4, waiting for transfers between devices, to_prev(): return lax.ppermute(block, AXES, TO_PREV)  28.9 us
    ppermute x4, waiting for transfers between devices, to_next(): return lax.ppermute(block, AXES, TO_NEXT)  23.6 us
    ppermute x4, starting transfers between devices, to_prev(): return lax.ppermute(block, AXES, TO_PREV)  18.3 us
    ppermute x4, starting transfers between devices, to_next(): return lax.ppermute(block, AXES, TO_NEXT)  12.8 us
    pallas_call x5, Pallas kernels, call(): pl.pallas_call(kernel, in_specs=[SMEM] * smem + [VMEM] * (len(inputs) - s...  11.6 us
    unnamed x18, local copies, waits for them, and re-layouts  3.63 us
  transfers between devices with their start and end apart: 12, of which 8 were waited for; matrix products, arithmetic and copies ran while one was open for 0% of the time, Pallas kernels for 2%

profile of v1, /device:TPU:51, one launch (start us, length us, event | category | flops | bytes accessed | tf_op | source)
XLA Modules:
  0.0 132.6 jit_solution(9080706565307254221)
XLA Ops:
  0.6 0.0 copy-start
  0.6 0.9 copy-done
  1.5 0.9 copy-done.2
  2.4 0.9 copy-done.6
  3.4 0.9 copy-done.7
  4.3 0.8 pack_kernel.1
  5.0 6.2 %all-to-all-start = ((bf16[16,64,128]{2,1,0:T(8,128)(2,1)}), bf16[16,64,128]{2,1,0:T(8,128)(2,1)S(1)}, u32[]{:S(2)}, u32[]{:S(2)}) async-start(bf16[16,64,128]{2,1,0:T(8,128)(2,1)} %get-tuple-element.10), calls=%async_computation | async-start | bytes 524288 | tf_op jit(solution)/shard_map/all_to_all | solution.py:45
  11.2 10.4 %collective-permute-start.3 = (bf16[64,2048]{1,0:T(8,128)(2,1)S(1)}, bf16[64,2048]{1,0:T(8,128)(2,1)S(1)}, u32[]{:S(2)}, u32[]{:S(2)}) collective-permute-start(bf16[64,2048]{1,0:T(8,128)(2,1)S(1)} %get-tuple-element.11), channel_id=1, source_target_pairs={{32,0},{33,1},{34,2},{35,3},{40,8},{41,9},{42,10},{43,11},{48,16},... | collective-permute-start | bytes 786440 | tf_op jit(solution)/shard_map/ppermute | solution.py:41
  21.7 1.9 %collective-permute-start.2 = (bf16[64,2048]{1,0:T(8,128)(2,1)S(1)}, bf16[64,2048]{1,0:T(8,128)(2,1)S(1)}, u32[]{:S(2)}, u32[]{:S(2)}) collective-permute-start(bf16[64,2048]{1,0:T(8,128)(2,1)S(1)} %get-tuple-element.11), channel_id=1, source_target_pairs={{0,32},{1,33},{2,34},{3,35},{8,40},{9,41},{10,42},{11,43},{16,48},... | collective-permute-start | bytes 786440 | tf_op jit(solution)/shard_map/ppermute | solution.py:37
  23.6 6.9 %collective-permute-done.3.after_ref = bf16[64,2048]{1,0:T(8,128)(2,1)S(1)} collective-permute-done((bf16[64,2048]{1,0:T(8,128)(2,1)S(1)}, bf16[64,2048]{1,0:T(8,128)(2,1)S(1)}, u32[]{:S(2)}, u32[]{:S(2)}) %collective-permute-start.3) | collective-permute-done | bytes 262176 | tf_op jit(solution)/shard_map/ppermute | solution.py:41
  30.5 8.9 %collective-permute-done.2.before_ref = bf16[64,2048]{1,0:T(8,128)(2,1)S(1)} collective-permute-done((bf16[64,2048]{1,0:T(8,128)(2,1)S(1)}, bf16[64,2048]{1,0:T(8,128)(2,1)S(1)}, u32[]{:S(2)}, u32[]{:S(2)}) %collective-permute-start.2) | collective-permute-done | bytes 262176 | tf_op jit(solution)/shard_map/ppermute | solution.py:37
  39.4 1.6 %halo_kernel.1 = bf16[16,128,128]{2,1,0:T(8,128)(2,1)} custom-call(s32[32]{0:T(128)S(1)} %copy-done.8, bf16[32,2048]{1,0:T(8,128)(2,1)S(1)} %copy-done.1, bf16[32,2048]{1,0:T(8,128)(2,1)S(1)} %copy-done.3, bf16[64,2048]{1,0:T(8,128)(2,1)S(1)} %collective-permute-done.2.before_ref, bf16[64,2048]{1,0:T(8,128)(2,1)S(1)} %collective-permute-done.3.after_ref), custom_call_target="tpu_custom_call" | custom-call | tf_op jit(solution)/shard_map/halo_kernel/pallas_call | solution.py:288
  41.0 0.0 all-to-all-done.own_ref
  41.0 7.5 %all-to-all-start.1 = ((bf16[16,128,128]{2,1,0:T(8,128)(2,1)}), bf16[16,128,128]{2,1,0:T(8,128)(2,1)S(1)}, u32[]{:S(2)}, u32[]{:S(2)}) async-start(bf16[16,128,128]{2,1,0:T(8,128)(2,1)} %halo_kernel.1), calls=%async_computation.1 | async-start | bytes 1048576 | tf_op jit(solution)/shard_map/all_to_all | solution.py:45
  48.5 1.9 %collective-permute-start.1 = (bf16[16,64,128]{2,1,0:T(8,128)(2,1)S(1)}, bf16[16,64,128]{2,1,0:T(8,128)(2,1)S(1)}, u32[]{:S(2)}, u32[]{:S(2)}) collective-permute-start(bf16[16,64,128]{2,1,0:T(8,128)(2,1)S(1)} %all-to-all-done.own_ref), channel_id=1, source_target_pairs={{32,0},{33,1},{34,2},{35,3},{40,8},{41,9},{42,10},{43,11},{48,16},... | collective-permute-start | bytes 786440 | tf_op jit(solution)/shard_map/ppermute | solution.py:41
  50.4 4.3 %collective-permute-start = (bf16[16,64,128]{2,1,0:T(8,128)(2,1)S(1)}, bf16[16,64,128]{2,1,0:T(8,128)(2,1)S(1)}, u32[]{:S(2)}, u32[]{:S(2)}) collective-permute-start(bf16[16,64,128]{2,1,0:T(8,128)(2,1)S(1)} %all-to-all-done.own_ref), channel_id=1, source_target_pairs={{0,32},{1,33},{2,34},{3,35},{8,40},{9,41},{10,42},{11,43},{16,48},... | collective-permute-start | bytes 786440 | tf_op jit(solution)/shard_map/ppermute | solution.py:37
  54.6 10.9 %collective-permute-done.1.after_ref = bf16[16,64,128]{2,1,0:T(8,128)(2,1)S(1)} collective-permute-done((bf16[16,64,128]{2,1,0:T(8,128)(2,1)S(1)}, bf16[16,64,128]{2,1,0:T(8,128)(2,1)S(1)}, u32[]{:S(2)}, u32[]{:S(2)}) %collective-permute-start.1) | collective-permute-done | bytes 262176 | tf_op jit(solution)/shard_map/ppermute | solution.py:41
  65.5 3.0 %collective-permute-done.before_ref = bf16[16,64,128]{2,1,0:T(8,128)(2,1)S(1)} collective-permute-done((bf16[16,64,128]{2,1,0:T(8,128)(2,1)S(1)}, bf16[16,64,128]{2,1,0:T(8,128)(2,1)S(1)}, u32[]{:S(2)}, u32[]{:S(2)}) %collective-permute-start) | collective-permute-done | bytes 262176 | tf_op jit(solution)/shard_map/ppermute | solution.py:37
  68.6 0.0 all-to-all-done.1.qd_ref
  68.6 6.1 %attention_kernel.1 = (bf16[1024,128]{1,0:T(8,128)(2,1)S(1)}, bf16[1024,128]{1,0:T(8,128)(2,1)S(1)}, bf16[16,64,128]{2,1,0:T(8,128)(2,1)}) custom-call(s32[32]{0:T(128)S(1)} %copy-done.8, bf16[16,64,128]{2,1,0:T(8,128)(2,1)S(1)} %all-to-all-done.own_ref, bf16[16,64,128]{2,1,0:T(8,128)(2,1)S(1)} %collective-permute-done.before_ref, ...), custom_call_target="tpu_custom_call" | custom-call | tf_op jit(solution)/shard_map/attention_kernel/pallas_call | solution.py:288
  74.6 8.0 %all-to-all-start.3 = ((bf16[16,64,128]{2,1,0:T(8,128)(2,1)}), bf16[16,64,128]{2,1,0:T(8,128)(2,1)S(1)}, u32[]{:S(2)}, u32[]{:S(2)}) async-start(bf16[16,64,128]{2,1,0:T(8,128)(2,1)} %get-tuple-element.14), calls=%async_computation.3 | async-start | bytes 524288 | tf_op jit(solution)/shard_map/all_to_all | solution.py:45
  82.6 3.9 %collective-permute-start.5 = (bf16[1024,128]{1,0:T(8,128)(2,1)S(1)}, bf16[1024,128]{1,0:T(8,128)(2,1)S(1)}, u32[]{:S(2)}, u32[]{:S(2)}) collective-permute-start(bf16[1024,128]{1,0:T(8,128)(2,1)S(1)} %get-tuple-element.13), channel_id=1, source_target_pairs={{32,0},{33,1},{34,2},{35,3},{40,8},{41,9},{42,10},{43,11},{48,16},... | collective-permute-start | bytes 786440 | tf_op jit(solution)/shard_map/ppermute | solution.py:41
  86.5 2.3 %collective-permute-start.4 = (bf16[1024,128]{1,0:T(8,128)(2,1)S(1)}, bf16[1024,128]{1,0:T(8,128)(2,1)S(1)}, u32[]{:S(2)}, u32[]{:S(2)}) collective-permute-start(bf16[1024,128]{1,0:T(8,128)(2,1)S(1)} %get-tuple-element.13), channel_id=1, source_target_pairs={{0,32},{1,33},{2,34},{3,35},{8,40},{9,41},{10,42},{11,43},{16,48},... | collective-permute-start | bytes 786440 | tf_op jit(solution)/shard_map/ppermute | solution.py:37
  88.8 9.3 %collective-permute-done.5.after_ref = bf16[1024,128]{1,0:T(8,128)(2,1)S(1)} collective-permute-done((bf16[1024,128]{1,0:T(8,128)(2,1)S(1)}, bf16[1024,128]{1,0:T(8,128)(2,1)S(1)}, u32[]{:S(2)}, u32[]{:S(2)}) %collective-permute-start.5) | collective-permute-done | bytes 262176 | tf_op jit(solution)/shard_map/ppermute | solution.py:41
  98.1 3.1 %collective-permute-done.4.before_ref = bf16[1024,128]{1,0:T(8,128)(2,1)S(1)} collective-permute-done((bf16[1024,128]{1,0:T(8,128)(2,1)S(1)}, bf16[1024,128]{1,0:T(8,128)(2,1)S(1)}, u32[]{:S(2)}, u32[]{:S(2)}) %collective-permute-start.4) | collective-permute-done | bytes 262176 | tf_op jit(solution)/shard_map/ppermute | solution.py:37
  101.1 1.5 %merge_kernel.1 = bf16[16,64,128]{2,1,0:T(8,128)(2,1)} custom-call(s32[32]{0:T(128)S(1)} %copy-done.8, bf16[1024,128]{1,0:T(8,128)(2,1)S(1)} %get-tuple-element.12.own_ref, bf16[1024,128]{1,0:T(8,128)(2,1)S(1)} %collective-permute-done.4.before_ref, bf16[1024,128]{1,0:T(8,128)(2,1)S(1)} %collective-permute-done.5.after_ref), custom_call_target="tpu_custom_call" | custom-call | tf_op jit(solution)/shard_map/merge_kernel/pallas_call | solution.py:288
  102.7 11.5 %all-to-all-start.2 = ((bf16[16,64,128]{2,1,0:T(8,128)(2,1)}), bf16[16,64,128]{2,1,0:T(8,128)(2,1)S(1)}, u32[]{:S(2)}, u32[]{:S(2)}) async-start(bf16[16,64,128]{2,1,0:T(8,128)(2,1)} %merge_kernel.1), calls=%async_computation.2 | async-start | bytes 524288 | tf_op jit(solution)/shard_map/all_to_all | solution.py:45
  114.3 2.1 %collective-permute-start.7 = (bf16[16,32,128]{2,1,0:T(8,128)(2,1)S(1)}, bf16[16,32,128]{2,1,0:T(8,128)(2,1)S(1)}, u32[]{:S(2)}, u32[]{:S(2)}) collective-permute-start(bf16[16,32,128]{2,1,0:T(8,128)(2,1)S(1)} %slice.4), channel_id=1, source_target_pairs={{32,0},{33,1},{34,2},{35,3},{40,8},{41,9},{42,10},{43,11},{48,16},... | collective-permute-start | bytes 393224 | tf_op jit(solution)/shard_map/ppermute | solution.py:41
  116.3 4.3 %collective-permute-start.6 = (bf16[16,32,128]{2,1,0:T(8,128)(2,1)S(1)}, bf16[16,32,128]{2,1,0:T(8,128)(2,1)S(1)}, u32[]{:S(2)}, u32[]{:S(2)}) collective-permute-start(bf16[16,32,128]{2,1,0:T(8,128)(2,1)S(1)} %slice.4), channel_id=1, source_target_pairs={{0,32},{1,33},{2,34},{3,35},{8,40},{9,41},{10,42},{11,43},{16,48},... | collective-permute-start | bytes 393224 | tf_op jit(solution)/shard_map/ppermute | solution.py:37
  120.6 1.7 %collective-permute-done.7.after_ref = bf16[16,32,128]{2,1,0:T(8,128)(2,1)S(1)} collective-permute-done((bf16[16,32,128]{2,1,0:T(8,128)(2,1)S(1)}, bf16[16,32,128]{2,1,0:T(8,128)(2,1)S(1)}, u32[]{:S(2)}, u32[]{:S(2)}) %collective-permute-start.7) | collective-permute-done | bytes 131104 | tf_op jit(solution)/shard_map/ppermute | solution.py:41
  122.3 8.6 %collective-permute-done.6.before_ref = bf16[16,32,128]{2,1,0:T(8,128)(2,1)S(1)} collective-permute-done((bf16[16,32,128]{2,1,0:T(8,128)(2,1)S(1)}, bf16[16,32,128]{2,1,0:T(8,128)(2,1)S(1)}, u32[]{:S(2)}, u32[]{:S(2)}) %collective-permute-start.6) | collective-permute-done | bytes 131104 | tf_op jit(solution)/shard_map/ppermute | solution.py:37
  131.0 1.7 %finish_kernel.1 = (bf16[32,2048]{1,0:T(8,128)(2,1)}, bf16[32,2048]{1,0:T(8,128)(2,1)}, bf16[32,2048]{1,0:T(8,128)(2,1)}, f32[32,2048]{1,0:T(8,128)}, f32[32,2048]{1,0:T(8,128)}) custom-call(s32[32]{0:T(128)S(1)} %copy-done.8, bf16[16,64,128]{2,1,0:T(8,128)(2,1)S(1)} %all-to-all-done.2.kv_ref, bf16[16,64,128]{2,1,0:T(8,128)(2,1)S(1)} %all-to-all-done.3.dq_ref, ...), custom_call_target="tpu_custom_call" | custom-call | tf_op jit(solution)/shard_map/finish_kernel/pallas_call | solution.py:288
  (16 shorter events, 0.0 us)
Async XLA Ops:
  0.6 0.9 copy-start
  1.5 0.9 copy-start.2
  2.4 0.9 copy-start.6
  3.3 0.9 copy-start.7
  5.0 34.4 %copy-start.1 = (bf16[32,2048]{1,0:T(8,128)(2,1)S(1)}, bf16[32,2048]{1,0:T(8,128)(2,1)}, u32[]{:S(2)}) copy-start(bf16[32,2048]{1,0:T(8,128)(2,1)} %q_ref.3) | copy-start | bytes 393220
  5.0 34.4 %copy-start.3 = (bf16[32,2048]{1,0:T(8,128)(2,1)S(1)}, bf16[32,2048]{1,0:T(8,128)(2,1)}, u32[]{:S(2)}) copy-start(bf16[32,2048]{1,0:T(8,128)(2,1)} %d_ref.3) | copy-start | bytes 393220
  5.0 36.0 %all-to-all-start = ((bf16[16,64,128]{2,1,0:T(8,128)(2,1)}), bf16[16,64,128]{2,1,0:T(8,128)(2,1)S(1)}, u32[]{:S(2)}, u32[]{:S(2)}) async-start(bf16[16,64,128]{2,1,0:T(8,128)(2,1)} %get-tuple-element.10), calls=%async_computation | async-start | bytes 524288 | tf_op jit(solution)/shard_map/all_to_all | solution.py:45
  11.2 28.2 %copy-start.8 = (s32[32]{0:T(128)S(1)}, s32[32]{0:T(128)}, u32[]{:S(2)}) copy-start(s32[32]{0:T(128)} %lengths_ref.7) | copy-start | bytes 388
  11.2 19.3 %collective-permute-start.3 = (bf16[64,2048]{1,0:T(8,128)(2,1)S(1)}, bf16[64,2048]{1,0:T(8,128)(2,1)S(1)}, u32[]{:S(2)}, u32[]{:S(2)}) collective-permute-start(bf16[64,2048]{1,0:T(8,128)(2,1)S(1)} %get-tuple-element.11), channel_id=1, source_target_pairs={{32,0},{33,1},{34,2},{35,3},{40,8},{41,9},{42,10},{43,11},{48,16},... | collective-permute-start | bytes 786440 | tf_op jit(solution)/shard_map/ppermute | solution.py:41
  21.7 17.8 %collective-permute-start.2 = (bf16[64,2048]{1,0:T(8,128)(2,1)S(1)}, bf16[64,2048]{1,0:T(8,128)(2,1)S(1)}, u32[]{:S(2)}, u32[]{:S(2)}) collective-permute-start(bf16[64,2048]{1,0:T(8,128)(2,1)S(1)} %get-tuple-element.11), channel_id=1, source_target_pairs={{0,32},{1,33},{2,34},{3,35},{8,40},{9,41},{10,42},{11,43},{16,48},... | collective-permute-start | bytes 786440 | tf_op jit(solution)/shard_map/ppermute | solution.py:37
  41.0 27.6 %all-to-all-start.1 = ((bf16[16,128,128]{2,1,0:T(8,128)(2,1)}), bf16[16,128,128]{2,1,0:T(8,128)(2,1)S(1)}, u32[]{:S(2)}, u32[]{:S(2)}) async-start(bf16[16,128,128]{2,1,0:T(8,128)(2,1)} %halo_kernel.1), calls=%async_computation.1 | async-start | bytes 1048576 | tf_op jit(solution)/shard_map/all_to_all | solution.py:45
  48.5 17.1 %collective-permute-start.1 = (bf16[16,64,128]{2,1,0:T(8,128)(2,1)S(1)}, bf16[16,64,128]{2,1,0:T(8,128)(2,1)S(1)}, u32[]{:S(2)}, u32[]{:S(2)}) collective-permute-start(bf16[16,64,128]{2,1,0:T(8,128)(2,1)S(1)} %all-to-all-done.own_ref), channel_id=1, source_target_pairs={{32,0},{33,1},{34,2},{35,3},{40,8},{41,9},{42,10},{43,11},{48,16},... | collective-permute-start | bytes 786440 | tf_op jit(solution)/shard_map/ppermute | solution.py:41
  50.4 18.2 %collective-permute-start = (bf16[16,64,128]{2,1,0:T(8,128)(2,1)S(1)}, bf16[16,64,128]{2,1,0:T(8,128)(2,1)S(1)}, u32[]{:S(2)}, u32[]{:S(2)}) collective-permute-start(bf16[16,64,128]{2,1,0:T(8,128)(2,1)S(1)} %all-to-all-done.own_ref), channel_id=1, source_target_pairs={{0,32},{1,33},{2,34},{3,35},{8,40},{9,41},{10,42},{11,43},{16,48},... | collective-permute-start | bytes 786440 | tf_op jit(solution)/shard_map/ppermute | solution.py:37
  74.6 28.1 %all-to-all-start.3 = ((bf16[16,64,128]{2,1,0:T(8,128)(2,1)}), bf16[16,64,128]{2,1,0:T(8,128)(2,1)S(1)}, u32[]{:S(2)}, u32[]{:S(2)}) async-start(bf16[16,64,128]{2,1,0:T(8,128)(2,1)} %get-tuple-element.14), calls=%async_computation.3 | async-start | bytes 524288 | tf_op jit(solution)/shard_map/all_to_all | solution.py:45
  82.6 15.5 %collective-permute-start.5 = (bf16[1024,128]{1,0:T(8,128)(2,1)S(1)}, bf16[1024,128]{1,0:T(8,128)(2,1)S(1)}, u32[]{:S(2)}, u32[]{:S(2)}) collective-permute-start(bf16[1024,128]{1,0:T(8,128)(2,1)S(1)} %get-tuple-element.13), channel_id=1, source_target_pairs={{32,0},{33,1},{34,2},{35,3},{40,8},{41,9},{42,10},{43,11},{48,16},... | collective-permute-start | bytes 786440 | tf_op jit(solution)/shard_map/ppermute | solution.py:41
  86.5 14.7 %collective-permute-start.4 = (bf16[1024,128]{1,0:T(8,128)(2,1)S(1)}, bf16[1024,128]{1,0:T(8,128)(2,1)S(1)}, u32[]{:S(2)}, u32[]{:S(2)}) collective-permute-start(bf16[1024,128]{1,0:T(8,128)(2,1)S(1)} %get-tuple-element.13), channel_id=1, source_target_pairs={{0,32},{1,33},{2,34},{3,35},{8,40},{9,41},{10,42},{11,43},{16,48},... | collective-permute-start | bytes 786440 | tf_op jit(solution)/shard_map/ppermute | solution.py:37
  102.7 28.3 %copy-start.5 = (f32[32,2048]{1,0:T(8,128)S(1)}, f32[32,2048]{1,0:T(8,128)}, u32[]{:S(2)}) copy-start(f32[32,2048]{1,0:T(8,128)} %value_prior_ref.1) | copy-start | bytes 786436
  102.7 28.3 %all-to-all-start.2 = ((bf16[16,64,128]{2,1,0:T(8,128)(2,1)}), bf16[16,64,128]{2,1,0:T(8,128)(2,1)S(1)}, u32[]{:S(2)}, u32[]{:S(2)}) async-start(bf16[16,64,128]{2,1,0:T(8,128)(2,1)} %merge_kernel.1), calls=%async_computation.2 | async-start | bytes 524288 | tf_op jit(solution)/shard_map/all_to_all | solution.py:45
  114.2 16.7 %copy-start.4 = (f32[32,2048]{1,0:T(8,128)S(1)}, f32[32,2048]{1,0:T(8,128)}, u32[]{:S(2)}) copy-start(f32[32,2048]{1,0:T(8,128)} %key_prior_ref.1) | copy-start | bytes 786436
  114.3 8.1 %collective-permute-start.7 = (bf16[16,32,128]{2,1,0:T(8,128)(2,1)S(1)}, bf16[16,32,128]{2,1,0:T(8,128)(2,1)S(1)}, u32[]{:S(2)}, u32[]{:S(2)}) collective-permute-start(bf16[16,32,128]{2,1,0:T(8,128)(2,1)S(1)} %slice.4), channel_id=1, source_target_pairs={{32,0},{33,1},{34,2},{35,3},{40,8},{41,9},{42,10},{43,11},{48,16},... | collective-permute-start | bytes 393224 | tf_op jit(solution)/shard_map/ppermute | solution.py:41
  116.3 14.7 %collective-permute-start.6 = (bf16[16,32,128]{2,1,0:T(8,128)(2,1)S(1)}, bf16[16,32,128]{2,1,0:T(8,128)(2,1)S(1)}, u32[]{:S(2)}, u32[]{:S(2)}) collective-permute-start(bf16[16,32,128]{2,1,0:T(8,128)(2,1)S(1)} %slice.4), channel_id=1, source_target_pairs={{0,32},{1,33},{2,34},{3,35},{8,40},{9,41},{10,42},{11,43},{16,48},... | collective-permute-start | bytes 393224 | tf_op jit(solution)/shard_map/ppermute | solution.py:37

commit v2 on v1

--- a/solution.py
+++ b/solution.py
@@ -29,16 +29,25 @@
 
 
 GROUPS = [[device_of(s, i) for i in range(16)] for s in range(SEGS)]
-TO_NEXT = [(device_of(s, i), device_of((s + 1) % SEGS, i)) for s in range(SEGS) for i in range(16)]
-TO_PREV = [(target, source) for source, target in TO_NEXT]
-
-
-def to_next(block):
-    return lax.ppermute(block, AXES, TO_NEXT)
-
-
-def to_prev(block):
-    return lax.ppermute(block, AXES, TO_PREV)
+def swaps(first):
+    pairs = []
+    for s in range(first, SEGS - 1, 2):
+        for i in range(16):
+            here, there = device_of(s, i), device_of(s + 1, i)
+            pairs += [(here, there), (there, here)]
+    return pairs
+
+
+EVEN = swaps(0)
+ODD = swaps(1)
+
+
+def with_even(block):
+    return lax.ppermute(block, AXES, EVEN)
+
+
+def with_odd(block):
+    return lax.ppermute(block, AXES, ODD)
 
 
 def exchange(chunks):
@@ -90,43 +99,32 @@
     return chosen.astype(jnp.bfloat16)
 
 
-def pack_kernel(q_ref, d_ref, k_ref, v_ref, rows_ref, chunk_ref):
-    rows_ref[0:ROWS, :] = q_ref[...]
-    rows_ref[ROWS : 2 * ROWS, :] = d_ref[...]
-    for h in range(HEADS):
-        chunk_ref[h, 0:ROWS, :] = k_ref[:, h * HD : (h + 1) * HD]
-        chunk_ref[h, ROWS : 2 * ROWS, :] = v_ref[:, h * HD : (h + 1) * HD]
-
-
-def halo_kernel(lengths_ref, q_ref, d_ref, before_ref, after_ref, chunk_ref):
-    segment, slot = place()
-    split = halo_split(doc_table(lengths_ref), segment)
-    row = slot * ROWS + lax.broadcasted_iota(jnp.int32, (ROWS, HD), 0)
-    after = row < split
-    for h in range(HEADS):
-        cols = slice(h * HD, (h + 1) * HD)
-        chunk_ref[h, 0:ROWS, :] = q_ref[:, cols]
-        chunk_ref[h, ROWS : 2 * ROWS, :] = d_ref[:, cols]
-        for part in range(2):
-            rows = slice(part * ROWS, (part + 1) * ROWS)
-            chunk_ref[h, (2 + part) * ROWS : (3 + part) * ROWS, :] = pick(
-                after, after_ref[rows, cols], before_ref[rows, cols]
-            )
+def pack_kernel(q_hbm, k_hbm, v_hbm, d_hbm, chunk_ref, rows, sems):
+    copies = [
+        pltpu.make_async_copy(source, rows.at[part], sems.at[part])
+        for part, source in enumerate((q_hbm, k_hbm, v_hbm, d_hbm))
+    ]
+    for copy in copies:
+        copy.start()
+    for part, copy in enumerate(copies):
+        copy.wait()
+        for h in range(HEADS):
+            chunk_ref[h, part * ROWS : (part + 1) * ROWS, :] = rows[
+                part, :, h * HD : (h + 1) * HD
+            ]
 
 
 def attention_kernel(
     lengths_ref,
     own_ref,
-    before_ref,
-    after_ref,
-    qd_ref,
+    even_ref,
+    odd_ref,
+    own_out,
     halo_out,
-    own_out,
-    dq_out,
     q_win,
-    d_win,
     k_win,
     v_win,
+    d_win,
     s_buf,
     dp_buf,
     dk_acc,
@@ -136,20 +134,15 @@
     table = doc_table(lengths_ref)
     split = halo_split(table, segment)
     tile_row = lax.broadcasted_iota(jnp.int32, (ROWS, HD), 0)
+    odd = segment % 2 == 1
     for i in range(16):
         halo = slice(i * ROWS, (i + 1) * ROWS)
         mine = slice(SEG + i * ROWS, SEG + (i + 1) * ROWS)
-        after = tile_row + i * ROWS < split
-        k_win[halo, :] = pick(after, after_ref[i, 0:ROWS, :], before_ref[i, 0:ROWS, :])
-        v_win[halo, :] = pick(
-            after, after_ref[i, ROWS : 2 * ROWS, :], before_ref[i, ROWS : 2 * ROWS, :]
-        )
-        k_win[mine, :] = own_ref[i, 0:ROWS, :]
-        v_win[mine, :] = own_ref[i, ROWS : 2 * ROWS, :]
-        q_win[mine, :] = qd_ref[i, 0:ROWS, :]
-        d_win[mine, :] = qd_ref[i, ROWS : 2 * ROWS, :]
-        q_win[halo, :] = qd_ref[i, 2 * ROWS : 3 * ROWS, :]
-        d_win[halo, :] = qd_ref[i, 3 * ROWS : 4 * ROWS, :]
+        from_even = (tile_row + i * ROWS < split) != odd
+        for part, win in enumerate((q_win, k_win, v_win, d_win)):
+            rows = slice(part * ROWS, (part + 1) * ROWS)
+            win[halo, :] = pick(from_even, even_ref[i, rows, :], odd_ref[i, rows, :])
+            win[mine, :] = own_ref[i, rows, :]
     base = (segment - 1) * SEG
     contract_last = (((1,), (1,)), ((), ()))
     contract_first = (((0,), (0,)), ((), ()))
@@ -213,37 +206,35 @@
         dq = (dq * SCALE).astype(jnp.bfloat16)
         for i in range(QB // ROWS):
             index = qb * (QB // ROWS) + i
-            place_row = (1 - index // 16) * ROWS
-            dq_out[index % 16, place_row : place_row + ROWS, :] = dq[i * ROWS : (i + 1) * ROWS, :]
-    halo_out[0:SEG, :] = (dk_acc[0:SEG, :] * SCALE).astype(jnp.bfloat16)
-    halo_out[SEG:WIN, :] = dv_acc[0:SEG, :].astype(jnp.bfloat16)
-    own_out[0:SEG, :] = (dk_acc[SEG:WIN, :] * SCALE).astype(jnp.bfloat16)
-    own_out[SEG:WIN, :] = dv_acc[SEG:WIN, :].astype(jnp.bfloat16)
-
-
-def merge_kernel(lengths_ref, own_ref, before_ref, after_ref, chunk_ref):
+            target = halo_out if index < 16 else own_out
+            target[index % 16, 0:ROWS, :] = dq[i * ROWS : (i + 1) * ROWS, :]
+    for i in range(16):
+        halo = slice(i * ROWS, (i + 1) * ROWS)
+        mine = slice(SEG + i * ROWS, SEG + (i + 1) * ROWS)
+        for target, rows in ((halo_out, halo), (own_out, mine)):
+            target[i, ROWS : 2 * ROWS, :] = (dk_acc[rows, :] * SCALE).astype(jnp.bfloat16)
+            target[i, 2 * ROWS : 3 * ROWS, :] = dv_acc[rows, :].astype(jnp.bfloat16)
+
+
+def merge_kernel(lengths_ref, own_ref, even_ref, odd_ref, chunk_ref):
     segment, unused_slot = place()
     head_end, tail_start = own_split(doc_table(lengths_ref), segment)
+    odd = segment % 2 == 1
     tile_row = lax.broadcasted_iota(jnp.int32, (ROWS, HD), 0)
     for i in range(16):
         row = tile_row + i * ROWS
-        for part in range(2):
-            rows = slice(part * SEG + i * ROWS, part * SEG + (i + 1) * ROWS)
-            chosen = jnp.where(
-                row >= tail_start,
-                after_ref[rows, :].astype(jnp.float32),
-                own_ref[rows, :].astype(jnp.float32),
-            )
-            chosen = jnp.where(row < head_end, before_ref[rows, :].astype(jnp.float32), chosen)
-            chunk_ref[i, part * ROWS : (part + 1) * ROWS, :] = chosen.astype(jnp.bfloat16)
+        before = row < head_end
+        after = row >= tail_start
+        from_even = (before & odd) | (after & jnp.logical_not(odd))
+        from_own = jnp.logical_not(before | after)
+        for part in range(3):
+            rows = slice(part * ROWS, (part + 1) * ROWS)
+            chosen = pick(from_even, even_ref[i, rows, :], odd_ref[i, rows, :])
+            chunk_ref[i, rows, :] = pick(from_own, own_ref[i, rows, :], chosen)
 
 
 def finish_kernel(
-    lengths_ref,
-    kv_ref,
-    dq_ref,
-    before_ref,
-    after_ref,
+    back_ref,
     key_prior_ref,
     value_prior_ref,
     dq_out,
@@ -252,22 +243,11 @@
     key_out,
     value_out,
 ):
-    segment, slot = place()
-    head_end, tail_start = own_split(doc_table(lengths_ref), segment)
-    row = slot * ROWS + lax.broadcasted_iota(jnp.int32, (ROWS, HD), 0)
-    from_after = row >= tail_start
-    from_before = row < head_end
     for h in range(HEADS):
         cols = slice(h * HD, (h + 1) * HD)
-        chosen = jnp.where(
-            from_after,
-            after_ref[h].astype(jnp.float32),
-            dq_ref[h, 0:ROWS, :].astype(jnp.float32),
-        )
-        chosen = jnp.where(from_before, before_ref[h].astype(jnp.float32), chosen)
-        dq_out[:, cols] = chosen.astype(jnp.bfloat16)
-        dk = kv_ref[h, 0:ROWS, :]
-        dv = kv_ref[h, ROWS : 2 * ROWS, :]
+        dq_out[:, cols] = back_ref[h, 0:ROWS, :]
+        dk = back_ref[h, ROWS : 2 * ROWS, :]
+        dv = back_ref[h, 2 * ROWS : 3 * ROWS, :]
         dk_out[:, cols] = dk
         dv_out[:, cols] = dv
         dk = dk.astype(jnp.float32)
@@ -284,10 +264,13 @@
     return jax.ShapeDtypeStruct(shape, jnp.bfloat16)
 
 
-def call(kernel, inputs, outputs, scratch=(), smem=1, limit=16 << 20):
+ANY = pl.BlockSpec(memory_space=pl.ANY)
+
+
+def call(kernel, inputs, outputs, specs, scratch=(), limit=16 << 20):
     return pl.pallas_call(
         kernel,
-        in_specs=[SMEM] * smem + [VMEM] * (len(inputs) - smem),
+        in_specs=specs,
         out_specs=[VMEM] * len(outputs),
         out_shape=list(outputs),
         scratch_shapes=list(scratch),
@@ -298,50 +281,37 @@
 
 def shards(queries, keys, values, d_attn, fisher_key_prior, fisher_value_prior, doc_lengths):
     width = HEADS * HD
-    qd_rows, kv_chunks = call(
+    (chunks,) = call(
         pack_kernel,
-        (queries, d_attn, keys, values),
-        (bf16(2 * ROWS, width), bf16(HEADS, 2 * ROWS, HD)),
-        smem=0,
-    )
-    qd_before = to_next(qd_rows)
-    qd_after = to_prev(qd_rows)
-    kv_own = exchange(kv_chunks)
-    kv_before = to_next(kv_own)
-    kv_after = to_prev(kv_own)
-    (qd_chunks,) = call(
-        halo_kernel,
-        (doc_lengths, queries, d_attn, qd_before, qd_after),
+        (queries, keys, values, d_attn),
         (bf16(HEADS, 4 * ROWS, HD),),
-    )
-    qd_heads = exchange(qd_chunks)
-    window = [pltpu.VMEM((WIN, HD), jnp.bfloat16)] * 4
-    halo_kv, own_kv, dq_chunks = call(
+        [ANY] * 4,
+        scratch=[pltpu.VMEM((4, ROWS, width), jnp.bfloat16), pltpu.SemaphoreType.DMA((4,))],
+    )
+    own = exchange(chunks)
+    own_grads, halo_grads = call(
         attention_kernel,
-        (doc_lengths, kv_own, kv_before, kv_after, qd_heads),
-        (bf16(WIN, HD), bf16(WIN, HD), bf16(16, 2 * ROWS, HD)),
-        scratch=window
+        (doc_lengths, own, with_even(own), with_odd(own)),
+        (bf16(16, 3 * ROWS, HD), bf16(16, 3 * ROWS, HD)),
+        [SMEM] + [VMEM] * 3,
+        scratch=[pltpu.VMEM((WIN, HD), jnp.bfloat16)] * 4
         + [pltpu.VMEM((WIN, QB), jnp.float32)] * 2
         + [pltpu.VMEM((WIN, HD), jnp.float32)] * 2,
         limit=32 << 20,
     )
-    halo_before = to_next(halo_kv)
-    halo_after = to_prev(halo_kv)
-    dq_heads = exchange(dq_chunks)
-    dq_halo = dq_heads[:, ROWS:, :]
-    dq_before = to_next(dq_halo)
-    dq_after = to_prev(dq_halo)
-    (kv_back,) = call(
+    (merged,) = call(
         merge_kernel,
-        (doc_lengths, own_kv, halo_before, halo_after),
-        (bf16(16, 2 * ROWS, HD),),
-    )
-    kv_heads = exchange(kv_back)
+        (doc_lengths, own_grads, with_even(halo_grads), with_odd(halo_grads)),
+        (bf16(16, 3 * ROWS, HD),),
+        [SMEM] + [VMEM] * 3,
+    )
+    back = exchange(merged)
     wide = jax.ShapeDtypeStruct((ROWS, width), jnp.float32)
     return call(
         finish_kernel,
-        (doc_lengths, kv_heads, dq_heads, dq_before, dq_after, fisher_key_prior, fisher_value_prior),
+        (back, fisher_key_prior, fisher_value_prior),
         (bf16(ROWS, width), bf16(ROWS, width), bf16(ROWS, width), wide, wide),
+        [VMEM] * 3,
     )
 
 

time: 133 us -> 105 us (0.79)
  the two profiles are of different devices: /device:TPU:51 before, /device:TPU:25 now
where the time goes in v2:
time: 105 us; the launch traced here: 104 us
  waiting for transfers between devices  36.8 us (35%)
  blocking collectives  28.1 us (27%)
  starting transfers between devices  26.3 us (25%)
  Pallas kernels  8.21 us (8%)
  local copies, waits for them, and re-layouts  3.63 us (3%)
    all_to_all x2, blocking collectives, exchange(): lax.all_to_all(chunks, AXES, split_axis=0, concat_axis=0, axis_index_grou...  28.1 us
    ppermute x2, waiting for transfers between devices, with_odd(): return lax.ppermute(block, AXES, ODD)  28 us
    ppermute x2, starting transfers between devices, with_odd(): return lax.ppermute(block, AXES, ODD)  22.4 us
    ppermute x2, waiting for transfers between devices, with_even(): return lax.ppermute(block, AXES, EVEN)  8.82 us
    pallas_call x4, Pallas kernels, call(): pl.pallas_call(kernel, in_specs=specs, out_specs=[VMEM] * len(outputs), o...  8.21 us
    ppermute x2, starting transfers between devices, with_even(): return lax.ppermute(block, AXES, EVEN)  3.84 us
    unnamed x14, local copies, waits for them, and re-layouts  3.63 us
  transfers between devices with their start and end apart: 4, of which 4 were waited for; matrix products, arithmetic and copies ran while one was open for 0% of the time, Pallas kernels for 0%

profile of v2, /device:TPU:25, one launch (start us, length us, event | category | flops | bytes accessed | tf_op | source)
XLA Modules:
  0.0 103.8 jit_solution(2078088312163627549)
XLA Ops:
  0.6 0.0 copy-start.2
  0.6 0.9 copy-done.2
  1.5 0.0 copy-start.3
  1.5 0.9 copy-done.3
  2.4 0.0 copy-start.4
  2.4 0.9 copy-done.4
  3.3 0.0 copy-start.5
  3.3 0.9 copy-done.5
  4.3 0.8 pack_kernel.1
  5.0 0.0 copy-start.6
  5.0 15.5 %all_to_all.10.own_ref = bf16[16,128,128]{2,1,0:T(8,128)(2,1)S(1)} all-to-all(bf16[16,128,128]{2,1,0:T(8,128)(2,1)S(1)} %pack_kernel.1), channel_id=1, replica_groups={{0,1,2,3,8,9,10,11,16,17,18,19,24,25,26,27},{32,33,34,35,40,41,42,43,48..., dimensions={0} | all-to-all | bytes 1048576 | tf_op jit(solution)/shard_map/all_to_all | solution.py:54
  20.5 11.8 %collective-permute-start.1 = (bf16[16,128,128]{2,1,0:T(8,128)(2,1)S(1)}, bf16[16,128,128]{2,1,0:T(8,128)(2,1)S(1)}, u32[]{:S(2)}, u32[]{:S(2)}) collective-permute-start(bf16[16,128,128]{2,1,0:T(8,128)(2,1)S(1)} %all_to_all.10.own_ref), channel_id=1, source_target_pairs={{32,64},{64,32},{33,65},{65,33},{34,66},{66,34},{35,67},{67,35},{4... | collective-permute-start | bytes 1572872 | tf_op jit(solution)/shard_map/ppermute | solution.py:50
  32.3 1.9 %collective-permute-start = (bf16[16,128,128]{2,1,0:T(8,128)(2,1)S(1)}, bf16[16,128,128]{2,1,0:T(8,128)(2,1)S(1)}, u32[]{:S(2)}, u32[]{:S(2)}) collective-permute-start(bf16[16,128,128]{2,1,0:T(8,128)(2,1)S(1)} %all_to_all.10.own_ref), channel_id=1, source_target_pairs={{0,32},{32,0},{1,33},{33,1},{2,34},{34,2},{3,35},{35,3},{8,40},{40... | collective-permute-start | bytes 1572872 | tf_op jit(solution)/shard_map/ppermute | solution.py:46
  34.2 16.3 %collective-permute-done.1.odd_ref = bf16[16,128,128]{2,1,0:T(8,128)(2,1)S(1)} collective-permute-done((bf16[16,128,128]{2,1,0:T(8,128)(2,1)S(1)}, bf16[16,128,128]{2,1,0:T(8,128)(2,1)S(1)}, u32[]{:S(2)}, u32[]{:S(2)}) %collective-permute-start.1) | collective-permute-done | bytes 524320 | tf_op jit(solution)/shard_map/ppermute | solution.py:50
  50.6 1.6 %collective-permute-done.even_ref = bf16[16,128,128]{2,1,0:T(8,128)(2,1)S(1)} collective-permute-done((bf16[16,128,128]{2,1,0:T(8,128)(2,1)S(1)}, bf16[16,128,128]{2,1,0:T(8,128)(2,1)S(1)}, u32[]{:S(2)}, u32[]{:S(2)}) %collective-permute-start) | collective-permute-done | bytes 524320 | tf_op jit(solution)/shard_map/ppermute | solution.py:46
  52.2 0.0 copy-done.6
  52.2 5.5 %attention_kernel.1 = (bf16[16,96,128]{2,1,0:T(8,128)(2,1)S(1)}, bf16[16,96,128]{2,1,0:T(8,128)(2,1)S(1)}) custom-call(s32[32]{0:T(128)S(1)} %copy-done.6, bf16[16,128,128]{2,1,0:T(8,128)(2,1)S(1)} %all_to_all.10.own_ref, bf16[16,128,128]{2,1,0:T(8,128)(2,1)S(1)} %collective-permute-done.even_ref, bf16[16,128,128]{2,1,0:T(8,128)(2,1)S(1)} %collective-permute-done.1.odd_ref), custom_call_target="tpu_custom_call" | custom-call | tf_op jit(solution)/shard_map/attention_kernel/pallas_call | solution.py:271
  57.7 10.7 %collective-permute-start.3 = (bf16[16,96,128]{2,1,0:T(8,128)(2,1)S(1)}, bf16[16,96,128]{2,1,0:T(8,128)(2,1)S(1)}, u32[]{:S(2)}, u32[]{:S(2)}) collective-permute-start(bf16[16,96,128]{2,1,0:T(8,128)(2,1)S(1)} %get-tuple-element.8), channel_id=1, source_target_pairs={{32,64},{64,32},{33,65},{65,33},{34,66},{66,34},{35,67},{67,35},{4... | collective-permute-start | bytes 1179656 | tf_op jit(solution)/shard_map/ppermute | solution.py:50
  68.4 1.9 %collective-permute-start.2 = (bf16[16,96,128]{2,1,0:T(8,128)(2,1)S(1)}, bf16[16,96,128]{2,1,0:T(8,128)(2,1)S(1)}, u32[]{:S(2)}, u32[]{:S(2)}) collective-permute-start(bf16[16,96,128]{2,1,0:T(8,128)(2,1)S(1)} %get-tuple-element.8), channel_id=1, source_target_pairs={{0,32},{32,0},{1,33},{33,1},{2,34},{34,2},{3,35},{35,3},{8,40},{40... | collective-permute-start | bytes 1179656 | tf_op jit(solution)/shard_map/ppermute | solution.py:46
  70.3 11.6 %collective-permute-done.3.odd_ref = bf16[16,96,128]{2,1,0:T(8,128)(2,1)S(1)} collective-permute-done((bf16[16,96,128]{2,1,0:T(8,128)(2,1)S(1)}, bf16[16,96,128]{2,1,0:T(8,128)(2,1)S(1)}, u32[]{:S(2)}, u32[]{:S(2)}) %collective-permute-start.3) | collective-permute-done | bytes 393248 | tf_op jit(solution)/shard_map/ppermute | solution.py:50
  82.0 7.2 %collective-permute-done.2.even_ref = bf16[16,96,128]{2,1,0:T(8,128)(2,1)S(1)} collective-permute-done((bf16[16,96,128]{2,1,0:T(8,128)(2,1)S(1)}, bf16[16,96,128]{2,1,0:T(8,128)(2,1)S(1)}, u32[]{:S(2)}, u32[]{:S(2)}) %collective-permute-start.2) | collective-permute-done | bytes 393248 | tf_op jit(solution)/shard_map/ppermute | solution.py:46
  89.2 0.9 merge_kernel.1
  90.1 0.0 copy-start
  90.1 0.0 copy-start.1
  90.1 12.7 %all_to_all.11.back_ref = bf16[16,96,128]{2,1,0:T(8,128)(2,1)S(1)} all-to-all(bf16[16,96,128]{2,1,0:T(8,128)(2,1)S(1)} %merge_kernel.1), channel_id=1, replica_groups={{0,1,2,3,8,9,10,11,16,17,18,19,24,25,26,27},{32,33,34,35,40,41,42,43,48..., dimensions={0} | all-to-all | bytes 786432 | tf_op jit(solution)/shard_map/all_to_all | solution.py:54
  102.8 0.0 copy-done
  102.8 0.0 copy-done.1
  102.8 1.0 finish_kernel.1
Async XLA Ops:
  0.6 0.9 copy-start.2
  1.5 0.9 copy-start.3
  2.4 0.9 copy-start.4
  3.3 0.9 copy-start.5
  5.0 47.2 %copy-start.6 = (s32[32]{0:T(128)S(1)}, s32[32]{0:T(128)}, u32[]{:S(2)}) copy-start(s32[32]{0:T(128)} %lengths_ref.3) | copy-start | bytes 388
  20.5 30.1 %collective-permute-start.1 = (bf16[16,128,128]{2,1,0:T(8,128)(2,1)S(1)}, bf16[16,128,128]{2,1,0:T(8,128)(2,1)S(1)}, u32[]{:S(2)}, u32[]{:S(2)}) collective-permute-start(bf16[16,128,128]{2,1,0:T(8,128)(2,1)S(1)} %all_to_all.10.own_ref), channel_id=1, source_target_pairs={{32,64},{64,32},{33,65},{65,33},{34,66},{66,34},{35,67},{67,35},{4... | collective-permute-start | bytes 1572872 | tf_op jit(solution)/shard_map/ppermute | solution.py:50
  32.3 19.9 %collective-permute-start = (bf16[16,128,128]{2,1,0:T(8,128)(2,1)S(1)}, bf16[16,128,128]{2,1,0:T(8,128)(2,1)S(1)}, u32[]{:S(2)}, u32[]{:S(2)}) collective-permute-start(bf16[16,128,128]{2,1,0:T(8,128)(2,1)S(1)} %all_to_all.10.own_ref), channel_id=1, source_target_pairs={{0,32},{32,0},{1,33},{33,1},{2,34},{34,2},{3,35},{35,3},{8,40},{40... | collective-permute-start | bytes 1572872 | tf_op jit(solution)/shard_map/ppermute | solution.py:46
  57.7 24.2 %collective-permute-start.3 = (bf16[16,96,128]{2,1,0:T(8,128)(2,1)S(1)}, bf16[16,96,128]{2,1,0:T(8,128)(2,1)S(1)}, u32[]{:S(2)}, u32[]{:S(2)}) collective-permute-start(bf16[16,96,128]{2,1,0:T(8,128)(2,1)S(1)} %get-tuple-element.8), channel_id=1, source_target_pairs={{32,64},{64,32},{33,65},{65,33},{34,66},{66,34},{35,67},{67,35},{4... | collective-permute-start | bytes 1179656 | tf_op jit(solution)/shard_map/ppermute | solution.py:50
  68.4 20.7 %collective-permute-start.2 = (bf16[16,96,128]{2,1,0:T(8,128)(2,1)S(1)}, bf16[16,96,128]{2,1,0:T(8,128)(2,1)S(1)}, u32[]{:S(2)}, u32[]{:S(2)}) collective-permute-start(bf16[16,96,128]{2,1,0:T(8,128)(2,1)S(1)} %get-tuple-element.8), channel_id=1, source_target_pairs={{0,32},{32,0},{1,33},{33,1},{2,34},{34,2},{3,35},{35,3},{8,40},{40... | collective-permute-start | bytes 1179656 | tf_op jit(solution)/shard_map/ppermute | solution.py:46
  90.1 12.7 %copy-start = (f32[32,2048]{1,0:T(8,128)S(1)}, f32[32,2048]{1,0:T(8,128)}, u32[]{:S(2)}) copy-start(f32[32,2048]{1,0:T(8,128)} %key_prior_ref.1) | copy-start | bytes 786436
  90.1 12.7 %copy-start.1 = (f32[32,2048]{1,0:T(8,128)S(1)}, f32[32,2048]{1,0:T(8,128)}, u32[]{:S(2)}) copy-start(f32[32,2048]{1,0:T(8,128)} %value_prior_ref.1) | copy-start | bytes 786436

commit v3 on v2

v3 whole, which is shorter than its diff:
```python
import jax
import jax.numpy as jnp
from jax import lax
from jax.experimental import pallas as pl
from jax.experimental.pallas import tpu as pltpu
from jax.sharding import PartitionSpec as P

HD = 128
HEADS = 16
ROWS = 32
SEG = 512
SEGS = 32
NDOC = 32
TOKENS = SEG * SEGS
WIN = 2 * SEG
QB = 256
KB = 128
SCALE = 1.0 / HD**0.5
LOG2E = 1.4426950408889634
EXPONENT = SCALE * LOG2E
AXES = ("ctx", "head")
MASKED = -1e30


def device_of(segment, slot):
    column = slot % 4
    if segment < SEGS // 2:
        return (4 * segment + slot // 4) * 8 + column
    return (4 * (SEGS - 1 - segment) + 3 - slot // 4) * 8 + 4 + column


GROUPS = [[device_of(s, i) for i in range(16)] for s in range(SEGS)]
UP = [(device_of(s, i), device_of(s + 1, i)) for s in range(SEGS - 1) for i in range(16)]
DOWN = [(target, source) for source, target in UP]


def to_after(block):
    return lax.ppermute(block, AXES, UP)


def to_before(block):
    return lax.ppermute(block, AXES, DOWN)


def exchange(chunks):
    return lax.all_to_all(
        chunks, AXES, split_axis=0, concat_axis=0, axis_index_groups=GROUPS, tiled=True
    )


def place():
    ctx = lax.axis_index("ctx")
    head = lax.axis_index("head")
    lower = head < 4
    segment = jnp.where(lower, ctx // 4, SEGS - 1 - ctx // 4)
    slot = jnp.where(lower, ctx % 4, 3 - ctx % 4) * 4 + head % 4
    return segment.astype(jnp.int32), slot.astype(jnp.int32)


def doc_bounds(lengths_ref):
    bounds = []
    first = jnp.int32(0)
    for doc in range(NDOC):
        bounds.append(first)
        first = first + lengths_ref[doc]
    return bounds


def rows_after(lengths_ref, segment):
    start = segment * SEG
    count = jnp.int32(0)
    first = jnp.int32(0)
    for doc in range(NDOC):
        end = first + lengths_ref[doc]
        count = jnp.maximum(count, jnp.where(first < start, end - start - SEG, 0))
        first = end
    return count


def first_positions(bounds, q_pos):
    q_first = jnp.zeros(q_pos.shape, jnp.int32)
    for first in bounds:
        q_first = jnp.where(q_pos >= first, first, q_first)
    return jnp.where(q_pos >= TOKENS, TOKENS, q_first)


def tiles_of(qb):
    return range(6) if qb == 0 else range(8) if qb == 1 else range(4)


def fill_windows(own_ref, before_ref, after_ref, k_win, v_win, q_win, d_win):
    for i in range(16):
        low = slice(i * ROWS, (i + 1) * ROWS)
        high = slice(SEG + i * ROWS, SEG + (i + 1) * ROWS)
        first = slice(0, ROWS)
        second = slice(ROWS, 2 * ROWS)
        k_win[low, :] = before_ref[i, first, :]
        v_win[low, :] = before_ref[i, second, :]
        k_win[high, :] = own_ref[i, first, :]
        v_win[high, :] = own_ref[i, second, :]
        q_win[low, :] = own_ref[i, 2 * ROWS : 3 * ROWS, :]
        d_win[low, :] = own_ref[i, 3 * ROWS : 4 * ROWS, :]
        q_win[high, :] = after_ref[i, first, :]
        d_win[high, :] = after_ref[i, second, :]


def tile_allowed(base, q_pos, q_first, qb, kb):
    k_pos = base + kb * KB + lax.broadcasted_iota(jnp.int32, (KB, QB), 0)
    allowed = k_pos >= q_first
    if kb >= 4 + 2 * qb:
        allowed = allowed & (k_pos <= q_pos)
    return allowed


CONTRACT_LAST = (((1,), (1,)), ((), ()))
CONTRACT_FIRST = (((0,), (0,)), ((), ()))


def dot_t(left, right):
    return lax.dot_general(left, right, CONTRACT_LAST, preferred_element_type=jnp.float32)


def pack_kernel(q_hbm, k_hbm, v_hbm, d_hbm, chunk_ref, rows, sems):
    copies = [
        pltpu.make_async_copy(source, rows.at[part], sems.at[part])
        for part, source in enumerate((k_hbm, v_hbm, q_hbm, d_hbm))
    ]
    for copy in copies:
        copy.start()
    for part, copy in enumerate(copies):
        copy.wait()
        for h in range(HEADS):
            chunk_ref[h, part * ROWS : (part + 1) * ROWS, :] = rows[
                part, :, h * HD : (h + 1) * HD
            ]


def split_kernel(own_ref, kv_ref, qd_ref):
    for i in range(16):
        kv_ref[i] = own_ref[i, 0 : 2 * ROWS, :]
        qd_ref[i] = own_ref[i, 2 * ROWS : 4 * ROWS, :]


def stats_kernel(
    lengths_ref,
    own_ref,
    before_ref,
    after_ref,
    own_stats,
    after_stats,
    k_win,
    v_win,
    q_win,
    d_win,
    s_buf,
):
    segment, unused_slot = place()
    fill_windows(own_ref, before_ref, after_ref, k_win, v_win, q_win, d_win)
    bounds = doc_bounds(lengths_ref)
    base = (segment - 1) * SEG

    def block(qb):
        q_pos = segment * SEG + qb * QB + lax.broadcasted_iota(jnp.int32, (1, QB), 1)
        q_first = first_positions(bounds, q_pos)
        q_rows = q_win[qb * QB : (qb + 1) * QB, :]
        d_rows = d_win[qb * QB : (qb + 1) * QB, :]
        top = jnp.full((8, QB), MASKED, jnp.float32)
        for kb in tiles_of(qb):
            keys = slice(kb * KB, (kb + 1) * KB)
            allowed = tile_allowed(base, q_pos, q_first, qb, kb)
            scores = jnp.where(allowed, dot_t(k_win[keys, :], q_rows), MASKED)
            s_buf[keys, :] = scores
            top = jnp.maximum(top, jnp.max(scores.reshape(KB // 8, 8, QB), axis=0))
        top = jnp.max(top, axis=0, keepdims=True)
        total = jnp.zeros((8, QB), jnp.float32)
        delta = jnp.zeros((8, QB), jnp.float32)
        for kb in tiles_of(qb):
            keys = slice(kb * KB, (kb + 1) * KB)
            terms = jnp.exp2((s_buf[keys, :] - top) * EXPONENT)
            s_buf[keys, :] = terms
            total = total + jnp.sum(terms.reshape(KB // 8, 8, QB), axis=0)
        total = jnp.sum(total, axis=0, keepdims=True)
        inverse = 1.0 / total
        for kb in tiles_of(qb):
            keys = slice(kb * KB, (kb + 1) * KB)
            probs_b = (s_buf[keys, :] * inverse).astype(jnp.bfloat16).astype(jnp.float32)
            weighted = probs_b * dot_t(v_win[keys, :], d_rows)
            delta = delta + jnp.sum(weighted.reshape(KB // 8, 8, QB), axis=0)
        target = own_stats if qb < 2 else after_stats
        cols = slice((qb % 2) * QB, (qb % 2 + 1) * QB)
        target[0:1, cols] = top
        target[1:2, cols] = total
        target[2:3, cols] = jnp.sum(delta, axis=0, keepdims=True) * total

    block(1)
    block(0)
    row = lax.broadcasted_iota(jnp.int32, (8, SEG), 0)
    after_stats[...] = jnp.where(row == 0, MASKED, 0.0)
    own_stats[3:8, :] = jnp.zeros((5, SEG), jnp.float32)
    count = rows_after(lengths_ref, segment)
    pl.when(count > 0)(lambda: block(2))
    pl.when(count > QB)(lambda: block(3))


def grads_kernel(
    lengths_ref,
    own_ref,
    before_ref,
    after_ref,
    own_stats,
    after_stats,
    own_there,
    after_there,
    own_out,
    before_out,
    after_out,
    k_win,
    v_win,
    q_win,
    d_win,
    dk_acc,
    dv_acc,
    dq_acc,
):
    segment, unused_slot = place()
    fill_windows(own_ref, before_ref, after_ref, k_win, v_win, q_win, d_win)
    bounds = doc_bounds(lengths_ref)
    base = (segment - 1) * SEG
    missing = segment == 0

    def block(qb):
        q_pos = segment * SEG + qb * QB + lax.broadcasted_iota(jnp.int32, (1, QB), 1)
        q_first = first_positions(bounds, q_pos)
        rows = slice(qb * QB, (qb + 1) * QB)
        q_rows = q_win[rows, :]
        d_rows = d_win[rows, :]
        cols = slice((qb % 2) * QB, (qb % 2 + 1) * QB)
        here = (own_stats if qb < 2 else after_stats)[:, cols]
        there = (own_there if qb < 2 else after_there)[:, cols]
        if qb < 2:
            row = lax.broadcasted_iota(jnp.int32, (8, QB), 0)
            there = jnp.where(missing, jnp.where(row == 0, MASKED, 0.0), there)
        top = jnp.maximum(here[0:1, :], there[0:1, :])
        here_share = jnp.exp2((here[0:1, :] - top) * EXPONENT)
        there_share = jnp.exp2((there[0:1, :] - top) * EXPONENT)
        total = here[1:2, :] * here_share + there[1:2, :] * there_share
        total = jnp.maximum(total, 1e-30)
        delta = (here[2:3, :] * here_share + there[2:3, :] * there_share) / total
        log_total = top * EXPONENT + jnp.log2(total)
        dq = jnp.zeros((QB, HD), jnp.float32)
        for kb in tiles_of(qb):
            keys = slice(kb * KB, (kb + 1) * KB)
            allowed = tile_allowed(base, q_pos, q_first, qb, kb)
            k_rows = k_win[keys, :]
            power = jnp.where(allowed, dot_t(k_rows, q_rows) * EXPONENT - log_total, MASKED)
            probs = jnp.exp2(power)
            d_probs = dot_t(v_win[keys, :], d_rows)
            d_scores = (probs * (d_probs - delta)).astype(jnp.bfloat16)
            dv = jnp.dot(probs.astype(jnp.bfloat16), d_rows, preferred_element_type=jnp.float32)
            dk = jnp.dot(d_scores, q_rows, preferred_element_type=jnp.float32)
            if qb == 1:
                dv_acc[keys, :] = dv
                dk_acc[keys, :] = dk
            else:
                dv_acc[keys, :] = dv_acc[keys, :] + dv
                dk_acc[keys, :] = dk_acc[keys, :] + dk
            dq = dq + lax.dot_general(
                d_scores, k_rows, CONTRACT_FIRST, preferred_element_type=jnp.float32
            )
        dq_acc[rows, :] = dq * SCALE

    dq_acc[SEG:WIN, :] = jnp.zeros((SEG, HD), jnp.float32)
    block(1)
    block(0)
    count = rows_after(lengths_ref, segment)
    pl.when(count > 0)(lambda: block(2))
    pl.when(count > QB)(lambda: block(3))

    for i in range(16):
        low = slice(i * ROWS, (i + 1) * ROWS)
        high = slice(SEG + i * ROWS, SEG + (i + 1) * ROWS)
        own_out[i, 0:ROWS, :] = dq_acc[low, :]
        own_out[i, ROWS : 2 * ROWS, :] = dk_acc[high, :] * SCALE
        own_out[i, 2 * ROWS : 3 * ROWS, :] = dv_acc[high, :]
        before_out[i, 0:ROWS, :] = (dk_acc[low, :] * SCALE).astype(jnp.bfloat16)
        before_out[i, ROWS : 2 * ROWS, :] = dv_acc[low, :].astype(jnp.bfloat16)
        after_out[i] = dq_acc[high, :].astype(jnp.bfloat16)


def merge_kernel(own_ref, dq_ref, dkv_ref, chunk_ref):
    for i in range(16):
        dq = own_ref[i, 0:ROWS, :] + dq_ref[i].astype(jnp.float32)
        dkv = own_ref[i, ROWS : 3 * ROWS, :] + dkv_ref[i].astype(jnp.float32)
        chunk_ref[i, 0:ROWS, :] = dq.astype(jnp.bfloat16)
        chunk_ref[i, ROWS : 3 * ROWS, :] = dkv.astype(jnp.bfloat16)


def finish_kernel(
    back_ref,
    key_prior_ref,
    value_prior_ref,
    dq_out,
    dk_out,
    dv_out,
    key_out,
    value_out,
):
    for h in range(HEADS):
        cols = slice(h * HD, (h + 1) * HD)
        dq_out[:, cols] = back_ref[h, 0:ROWS, :]
        dk = back_ref[h, ROWS : 2 * ROWS, :]
        dv = back_ref[h, 2 * ROWS : 3 * ROWS, :]
        dk_out[:, cols] = dk
        dv_out[:, cols] = dv
        dk = dk.astype(jnp.float32)
        dv = dv.astype(jnp.float32)
        key_out[:, cols] = key_prior_ref[:, cols] + dk * dk
        value_out[:, cols] = value_prior_ref[:, cols] + dv * dv


SMEM = pl.BlockSpec(memory_space=pltpu.SMEM)
VMEM = pl.BlockSpec(memory_space=pltpu.VMEM)


def bf16(*shape):
    return jax.ShapeDtypeStruct(shape, jnp.bfloat16)


HBM = pl.BlockSpec(memory_space=pltpu.HBM)


def call(kernel, inputs, outputs, specs, scratch=(), limit=16 << 20):
    return pl.pallas_call(
        kernel,
        in_specs=specs,
        out_specs=[VMEM] * len(outputs),
        out_shape=list(outputs),
        scratch_shapes=list(scratch),
        compiler_params=pltpu.CompilerParams(vmem_limit_bytes=limit),
        name=kernel.__name__,
    )(*inputs)


def shards(queries, keys, values, d_attn, fisher_key_prior, fisher_value_prior, doc_lengths):
    width = HEADS * HD
    half = bf16(16, 2 * ROWS, HD)
    (chunks,) = call(
        pack_kernel,
        (queries, keys, values, d_attn),
        (bf16(HEADS, 4 * ROWS, HD),),
        [HBM] * 4,
        scratch=[pltpu.VMEM((4, ROWS, width), jnp.bfloat16), pltpu.SemaphoreType.DMA((4,))],
        limit=60 << 20,
    )
    own = exchange(chunks)
    kv, qd = call(split_kernel, (own,), (half, half), [VMEM])
    kv_before = to_after(kv)
    qd_after = to_before(qd)
    windows = [pltpu.VMEM((WIN, HD), jnp.bfloat16)] * 4
    stats = jax.ShapeDtypeStruct((8, SEG), jnp.float32)
    own_stats, after_stats = call(
        stats_kernel,
        (doc_lengths, own, kv_before, qd_after),
        (stats, stats),
        [SMEM] + [VMEM] * 3,
        scratch=windows + [pltpu.VMEM((WIN, QB), jnp.float32)],
        limit=32 << 20,
    )
    own_there = to_after(after_stats)
    after_there = to_before(own_stats)
    own_grads, before_grads, after_grads = call(
        grads_kernel,
        (doc_lengths, own, kv_before, qd_after, own_stats, after_stats, own_there, after_there),
        (jax.ShapeDtypeStruct((16, 3 * ROWS, HD), jnp.float32), half, bf16(16, ROWS, HD)),
        [SMEM] + [VMEM] * 7,
        scratch=windows + [pltpu.VMEM((WIN, HD), jnp.float32)] * 3,
        limit=32 << 20,
    )
    dkv_there = to_before(before_grads)
    dq_there = to_after(after_grads)
    (merged,) = call(
        merge_kernel,
        (own_grads, dq_there, dkv_there),
        (bf16(16, 3 * ROWS, HD),),
        [VMEM] * 3,
    )
    back = exchange(merged)
    wide = jax.ShapeDtypeStruct((ROWS, width), jnp.float32)
    return call(
        finish_kernel,
        (back, fisher_key_prior, fisher_value_prior),
        (bf16(ROWS, width), bf16(ROWS, width), bf16(ROWS, width), wide, wide),
        [VMEM] * 3,
    )


def solution(mesh):
    tokens = P(AXES, None)
    return jax.shard_map(
        shards,
        mesh=mesh,
        in_specs=(tokens,) * 6 + (P(),),
        out_specs=(tokens,) * 5,
        check_vma=False,
    )
```

time: 105 us -> 99.1 us (0.944)
  waiting for transfers between devices: 36.8 us -> 27.2 us
  starting transfers between devices: 26.3 us -> 33.6 us
  local copies, waits for them, and re-layouts: 3.63 us -> 0.02 us
    ppermute x4 -> x6, waiting for transfers between devices: 36.8 us -> 27.2 us  [the longest x3 14.7 us: to_before(): return lax.ppermute(block, AXES, DOWN)]
    ppermute x4 -> x6, starting transfers between devices: 26.3 us -> 33.6 us  [the longest x3 27.8 us: to_after(): return lax.ppermute(block, AXES, UP)]
    unnamed x14 -> x6, local copies, waits for them, and re-layouts: 3.63 us -> 0.02 us
    pallas_call x4 -> x6, Pallas kernels: 8.21 us -> 8.2 us  [call(): pl.pallas_call(kernel, in_specs=specs, out_specs=[VMEM] * len(outputs), o...]
  transfers between devices with their start and end apart: 4 -> 6, of which waited for: 4 -> 5; matrix products, arithmetic and copies ran while one was open for 0% -> 0% of each run, Pallas kernels for 0% -> 0%
where the time goes in v3:
time: 99.1 us; the launch traced here: 98.7 us
  starting transfers between devices  33.6 us (34%)
  blocking collectives  28.9 us (29%)
  waiting for transfers between devices  27.2 us (27%)
  Pallas kernels  8.2 us (8%)
    all_to_all x2, blocking collectives, exchange(): lax.all_to_all(chunks, AXES, split_axis=0, concat_axis=0, axis_index_grou...  28.9 us
    ppermute x3, starting transfers between devices, to_after(): return lax.ppermute(block, AXES, UP)  27.8 us
    ppermute x3, waiting for transfers between devices, to_before(): return lax.ppermute(block, AXES, DOWN)  14.7 us
    ppermute x3, waiting for transfers between devices, to_after(): return lax.ppermute(block, AXES, UP)  12.6 us
    pallas_call x6, Pallas kernels, call(): pl.pallas_call(kernel, in_specs=specs, out_specs=[VMEM] * len(outputs), o...  8.2 us
    ppermute x3, starting transfers between devices, to_before(): return lax.ppermute(block, AXES, DOWN)  5.76 us
  transfers between devices with their start and end apart: 6, of which 5 were waited for; matrix products, arithmetic and copies ran while one was open for 0% of the time, Pallas kernels for 0%

profile of v3, /device:TPU:25, one launch (start us, length us, event | category | flops | bytes accessed | tf_op | source)
XLA Modules:
  0.0 98.7 jit_solution(3874154785922884161)
XLA Ops:
  0.6 1.9 %pack_kernel.1 = bf16[16,128,128]{2,1,0:T(8,128)(2,1)} custom-call(bf16[32,2048]{1,0:T(8,128)(2,1)} %q_hbm.1, bf16[32,2048]{1,0:T(8,128)(2,1)} %k_hbm.1, bf16[32,2048]{1,0:T(8,128)(2,1)} %v_hbm.1, bf16[32,2048]{1,0:T(8,128)(2,1)} %d_hbm.1), custom_call_target="tpu_custom_call" | custom-call | tf_op jit(solution)/shard_map/pack_kernel/pallas_call | solution.py:333
  2.6 15.7 %all_to_all.10.own_ref = bf16[16,128,128]{2,1,0:T(8,128)(2,1)S(1)} all-to-all(bf16[16,128,128]{2,1,0:T(8,128)(2,1)} %pack_kernel.1), channel_id=1, replica_groups={{0,1,2,3,8,9,10,11,16,17,18,19,24,25,26,27},{32,33,34,35,40,41,42,43,48..., dimensions={0} | all-to-all | bytes 1048576 | tf_op jit(solution)/shard_map/all_to_all | solution.py:46
  18.3 0.0 copy-start.2
  18.3 11.8 %collective-permute-start = (bf16[16,64,128]{2,1,0:T(8,128)(2,1)S(1)}, bf16[16,64,128]{2,1,0:T(8,128)(2,1)S(1)}, u32[]{:S(2)}, u32[]{:S(2)}) collective-permute-start(bf16[16,64,128]{2,1,0:T(8,128)(2,1)S(1)} %get-tuple-element.12), channel_id=1, source_target_pairs={{0,32},{1,33},{2,34},{3,35},{8,40},{9,41},{10,42},{11,43},{16,48},... | collective-permute-start | bytes 786440 | tf_op jit(solution)/shard_map/ppermute | solution.py:38
  30.1 1.9 %collective-permute-start.1 = (bf16[16,64,128]{2,1,0:T(8,128)(2,1)S(1)}, bf16[16,64,128]{2,1,0:T(8,128)(2,1)S(1)}, u32[]{:S(2)}, u32[]{:S(2)}) collective-permute-start(bf16[16,64,128]{2,1,0:T(8,128)(2,1)S(1)} %get-tuple-element.13), channel_id=1, source_target_pairs={{32,0},{33,1},{34,2},{35,3},{40,8},{41,9},{42,10},{43,11},{48,16},... | collective-permute-start | bytes 786440 | tf_op jit(solution)/shard_map/ppermute | solution.py:42
  32.0 6.6 %collective-permute-done.before_ref = bf16[16,64,128]{2,1,0:T(8,128)(2,1)S(1)} collective-permute-done((bf16[16,64,128]{2,1,0:T(8,128)(2,1)S(1)}, bf16[16,64,128]{2,1,0:T(8,128)(2,1)S(1)}, u32[]{:S(2)}, u32[]{:S(2)}) %collective-permute-start) | collective-permute-done | bytes 262176 | tf_op jit(solution)/shard_map/ppermute | solution.py:38
  38.6 11.0 %collective-permute-done.1.after_ref = bf16[16,64,128]{2,1,0:T(8,128)(2,1)S(1)} collective-permute-done((bf16[16,64,128]{2,1,0:T(8,128)(2,1)S(1)}, bf16[16,64,128]{2,1,0:T(8,128)(2,1)S(1)}, u32[]{:S(2)}, u32[]{:S(2)}) %collective-permute-start.1) | collective-permute-done | bytes 262176 | tf_op jit(solution)/shard_map/ppermute | solution.py:42
  49.6 0.0 copy-done.2
  49.6 1.6 %stats_kernel.1 = (f32[8,512]{1,0:T(8,128)S(1)}, f32[8,512]{1,0:T(8,128)S(1)}) custom-call(s32[32]{0:T(128)S(1)} %copy-done.2, bf16[16,128,128]{2,1,0:T(8,128)(2,1)S(1)} %all_to_all.10.own_ref, bf16[16,64,128]{2,1,0:T(8,128)(2,1)S(1)} %collective-permute-done.before_ref, bf16[16,64,128]{2,1,0:T(8,128)(2,1)S(1)} %collective-permute-done.1.after_ref), custom_call_target="tpu_custom_call" | custom-call | tf_op jit(solution)/shard_map/stats_kernel/pallas_call | solution.py:333
  51.3 1.9 %collective-permute-start.3 = (f32[8,512]{1,0:T(8,128)S(1)}, f32[8,512]{1,0:T(8,128)S(1)}, u32[]{:S(2)}, u32[]{:S(2)}) collective-permute-start(f32[8,512]{1,0:T(8,128)S(1)} %get-tuple-element.14.own_stats), channel_id=1, source_target_pairs={{32,0},{33,1},{34,2},{35,3},{40,8},{41,9},{42,10},{43,11},{48,16},... | collective-permute-start | bytes 49160 | tf_op jit(solution)/shard_map/ppermute | solution.py:42
  53.2 7.9 %collective-permute-start.2 = (f32[8,512]{1,0:T(8,128)S(1)}, f32[8,512]{1,0:T(8,128)S(1)}, u32[]{:S(2)}, u32[]{:S(2)}) collective-permute-start(f32[8,512]{1,0:T(8,128)S(1)} %get-tuple-element.15.after_stats), channel_id=1, source_target_pairs={{0,32},{1,33},{2,34},{3,35},{8,40},{9,41},{10,42},{11,43},{16,48},... | collective-permute-start | bytes 49160 | tf_op jit(solution)/shard_map/ppermute | solution.py:38
  61.1 0.0 collective-permute-done.3.after_there
  61.1 0.8 collective-permute-done.2.own_there
  62.0 3.5 %grads_kernel.1 = (f32[16,96,128]{2,1,0:T(8,128)S(1)}, bf16[16,64,128]{2,1,0:T(8,128)(2,1)S(1)}, bf16[16,32,128]{2,1,0:T(8,128)(2,1)S(1)}) custom-call(s32[32]{0:T(128)S(1)} %copy-done.2, bf16[16,128,128]{2,1,0:T(8,128)(2,1)S(1)} %all_to_all.10.own_ref, bf16[16,64,128]{2,1,0:T(8,128)(2,1)S(1)} %collective-permute-done.before_ref, ...), custom_call_target="tpu_custom_call" | custom-call | tf_op jit(solution)/shard_map/grads_kernel/pallas_call | solution.py:333
  65.4 1.9 %collective-permute-start.5 = (bf16[16,64,128]{2,1,0:T(8,128)(2,1)S(1)}, bf16[16,64,128]{2,1,0:T(8,128)(2,1)S(1)}, u32[]{:S(2)}, u32[]{:S(2)}) collective-permute-start(bf16[16,64,128]{2,1,0:T(8,128)(2,1)S(1)} %get-tuple-element.18), channel_id=1, source_target_pairs={{32,0},{33,1},{34,2},{35,3},{40,8},{41,9},{42,10},{43,11},{48,16},... | collective-permute-start | bytes 786440 | tf_op jit(solution)/shard_map/ppermute | solution.py:42
  67.3 8.1 %collective-permute-start.4 = (bf16[16,32,128]{2,1,0:T(8,128)(2,1)S(1)}, bf16[16,32,128]{2,1,0:T(8,128)(2,1)S(1)}, u32[]{:S(2)}, u32[]{:S(2)}) collective-permute-start(bf16[16,32,128]{2,1,0:T(8,128)(2,1)S(1)} %get-tuple-element.17), channel_id=1, source_target_pairs={{0,32},{1,33},{2,34},{3,35},{8,40},{9,41},{10,42},{11,43},{16,48},... | collective-permute-start | bytes 393224 | tf_op jit(solution)/shard_map/ppermute | solution.py:38
  75.5 5.1 %collective-permute-done.4.dq_ref = bf16[16,32,128]{2,1,0:T(8,128)(2,1)S(1)} collective-permute-done((bf16[16,32,128]{2,1,0:T(8,128)(2,1)S(1)}, bf16[16,32,128]{2,1,0:T(8,128)(2,1)S(1)}, u32[]{:S(2)}, u32[]{:S(2)}) %collective-permute-start.4) | collective-permute-done | bytes 131104 | tf_op jit(solution)/shard_map/ppermute | solution.py:38
  80.6 3.6 %collective-permute-done.5.dkv_ref = bf16[16,64,128]{2,1,0:T(8,128)(2,1)S(1)} collective-permute-done((bf16[16,64,128]{2,1,0:T(8,128)(2,1)S(1)}, bf16[16,64,128]{2,1,0:T(8,128)(2,1)S(1)}, u32[]{:S(2)}, u32[]{:S(2)}) %collective-permute-start.5) | collective-permute-done | bytes 262176 | tf_op jit(solution)/shard_map/ppermute | solution.py:42
  84.3 0.1 merge_kernel.1
  84.4 0.0 copy-start
  84.4 0.0 copy-start.1
  84.4 13.2 %all_to_all.11.back_ref = bf16[16,96,128]{2,1,0:T(8,128)(2,1)S(1)} all-to-all(bf16[16,96,128]{2,1,0:T(8,128)(2,1)S(1)} %merge_kernel.1), channel_id=1, replica_groups={{0,1,2,3,8,9,10,11,16,17,18,19,24,25,26,27},{32,33,34,35,40,41,42,43,48..., dimensions={0} | all-to-all | bytes 786432 | tf_op jit(solution)/shard_map/all_to_all | solution.py:46
  97.6 0.0 copy-done
  97.6 0.0 copy-done.1
  97.6 1.0 %finish_kernel.1 = (bf16[32,2048]{1,0:T(8,128)(2,1)}, bf16[32,2048]{1,0:T(8,128)(2,1)}, bf16[32,2048]{1,0:T(8,128)(2,1)}, f32[32,2048]{1,0:T(8,128)}, f32[32,2048]{1,0:T(8,128)}) custom-call(bf16[16,96,128]{2,1,0:T(8,128)(2,1)S(1)} %all_to_all.11.back_ref, f32[32,2048]{1,0:T(8,128)S(1)} %copy-done, f32[32,2048]{1,0:T(8,128)S(1)} %copy-done.1), custom_call_target="tpu_custom_call" | custom-call | tf_op jit(solution)/shard_map/finish_kernel/pallas_call | solution.py:333
  (1 shorter events, 0.0 us)
Async XLA Ops:
  18.3 31.3 %copy-start.2 = (s32[32]{0:T(128)S(1)}, s32[32]{0:T(128)}, u32[]{:S(2)}) copy-start(s32[32]{0:T(128)} %lengths_ref.3) | copy-start | bytes 388
  18.3 20.3 %collective-permute-start = (bf16[16,64,128]{2,1,0:T(8,128)(2,1)S(1)}, bf16[16,64,128]{2,1,0:T(8,128)(2,1)S(1)}, u32[]{:S(2)}, u32[]{:S(2)}) collective-permute-start(bf16[16,64,128]{2,1,0:T(8,128)(2,1)S(1)} %get-tuple-element.12), channel_id=1, source_target_pairs={{0,32},{1,33},{2,34},{3,35},{8,40},{9,41},{10,42},{11,43},{16,48},... | collective-permute-start | bytes 786440 | tf_op jit(solution)/shard_map/ppermute | solution.py:38
  30.1 19.5 %collective-permute-start.1 = (bf16[16,64,128]{2,1,0:T(8,128)(2,1)S(1)}, bf16[16,64,128]{2,1,0:T(8,128)(2,1)S(1)}, u32[]{:S(2)}, u32[]{:S(2)}) collective-permute-start(bf16[16,64,128]{2,1,0:T(8,128)(2,1)S(1)} %get-tuple-element.13), channel_id=1, source_target_pairs={{32,0},{33,1},{34,2},{35,3},{40,8},{41,9},{42,10},{43,11},{48,16},... | collective-permute-start | bytes 786440 | tf_op jit(solution)/shard_map/ppermute | solution.py:42
  51.3 9.8 %collective-permute-start.3 = (f32[8,512]{1,0:T(8,128)S(1)}, f32[8,512]{1,0:T(8,128)S(1)}, u32[]{:S(2)}, u32[]{:S(2)}) collective-permute-start(f32[8,512]{1,0:T(8,128)S(1)} %get-tuple-element.14.own_stats), channel_id=1, source_target_pairs={{32,0},{33,1},{34,2},{35,3},{40,8},{41,9},{42,10},{43,11},{48,16},... | collective-permute-start | bytes 49160 | tf_op jit(solution)/shard_map/ppermute | solution.py:42
  53.2 8.7 %collective-permute-start.2 = (f32[8,512]{1,0:T(8,128)S(1)}, f32[8,512]{1,0:T(8,128)S(1)}, u32[]{:S(2)}, u32[]{:S(2)}) collective-permute-start(f32[8,512]{1,0:T(8,128)S(1)} %get-tuple-element.15.after_stats), channel_id=1, source_target_pairs={{0,32},{1,33},{2,34},{3,35},{8,40},{9,41},{10,42},{11,43},{16,48},... | collective-permute-start | bytes 49160 | tf_op jit(solution)/shard_map/ppermute | solution.py:38
  65.4 18.9 %collective-permute-start.5 = (bf16[16,64,128]{2,1,0:T(8,128)(2,1)S(1)}, bf16[16,64,128]{2,1,0:T(8,128)(2,1)S(1)}, u32[]{:S(2)}, u32[]{:S(2)}) collective-permute-start(bf16[16,64,128]{2,1,0:T(8,128)(2,1)S(1)} %get-tuple-element.18), channel_id=1, source_target_pairs={{32,0},{33,1},{34,2},{35,3},{40,8},{41,9},{42,10},{43,11},{48,16},... | collective-permute-start | bytes 786440 | tf_op jit(solution)/shard_map/ppermute | solution.py:42
  67.3 13.3 %collective-permute-start.4 = (bf16[16,32,128]{2,1,0:T(8,128)(2,1)S(1)}, bf16[16,32,128]{2,1,0:T(8,128)(2,1)S(1)}, u32[]{:S(2)}, u32[]{:S(2)}) collective-permute-start(bf16[16,32,128]{2,1,0:T(8,128)(2,1)S(1)} %get-tuple-element.17), channel_id=1, source_target_pairs={{0,32},{1,33},{2,34},{3,35},{8,40},{9,41},{10,42},{11,43},{16,48},... | collective-permute-start | bytes 393224 | tf_op jit(solution)/shard_map/ppermute | solution.py:38
  84.4 13.2 %copy-start = (f32[32,2048]{1,0:T(8,128)S(1)}, f32[32,2048]{1,0:T(8,128)}, u32[]{:S(2)}) copy-start(f32[32,2048]{1,0:T(8,128)} %key_prior_ref.1) | copy-start | bytes 786436
  84.4 13.2 %copy-start.1 = (f32[32,2048]{1,0:T(8,128)S(1)}, f32[32,2048]{1,0:T(8,128)}, u32[]{:S(2)}) copy-start(f32[32,2048]{1,0:T(8,128)} %value_prior_ref.1) | copy-start | bytes 786436

commit v4 on v3

--- a/solution.py
+++ b/solution.py
@@ -88,20 +88,29 @@
     return range(6) if qb == 0 else range(8) if qb == 1 else range(4)
 
 
-def fill_windows(own_ref, before_ref, after_ref, k_win, v_win, q_win, d_win):
-    for i in range(16):
-        low = slice(i * ROWS, (i + 1) * ROWS)
-        high = slice(SEG + i * ROWS, SEG + (i + 1) * ROWS)
-        first = slice(0, ROWS)
-        second = slice(ROWS, 2 * ROWS)
-        k_win[low, :] = before_ref[i, first, :]
-        v_win[low, :] = before_ref[i, second, :]
-        k_win[high, :] = own_ref[i, first, :]
-        v_win[high, :] = own_ref[i, second, :]
-        q_win[low, :] = own_ref[i, 2 * ROWS : 3 * ROWS, :]
-        d_win[low, :] = own_ref[i, 3 * ROWS : 4 * ROWS, :]
-        q_win[high, :] = after_ref[i, first, :]
-        d_win[high, :] = after_ref[i, second, :]
+def own_tiles(qb):
+    return range(4, 6) if qb == 0 else range(4, 8)
+
+
+def rows_of(ref, first, count, part):
+    rows = ref[first : first + count, part * ROWS : (part + 1) * ROWS, :]
+    return rows.reshape(count * ROWS, HD)
+
+
+def key_tile(own_ref, before_ref, kb, part):
+    if kb < 4:
+        return rows_of(before_ref, 4 * kb, 4, part)
+    return rows_of(own_ref, 4 * (kb - 4), 4, part)
+
+
+def query_block(own_ref, after_ref, qb, part):
+    if qb < 2:
+        return rows_of(own_ref, 8 * qb, 8, 2 + part)
+    return rows_of(after_ref, 8 * (qb - 2), 8, part)
+
+
+def positions(segment, qb):
+    return segment * SEG + qb * QB + lax.broadcasted_iota(jnp.int32, (1, QB), 1)
 
 
 def tile_allowed(base, q_pos, q_first, qb, kb):
@@ -135,68 +144,97 @@
             ]
 
 
-def split_kernel(own_ref, kv_ref, qd_ref):
+def split_kernel(own_ref, kv_ref):
     for i in range(16):
         kv_ref[i] = own_ref[i, 0 : 2 * ROWS, :]
+
+
+def block_stats(bounds, segment, qb, tiles, own_ref, before_ref, after_ref, s_buf):
+    base = (segment - 1) * SEG
+    q_pos = positions(segment, qb)
+    q_first = first_positions(bounds, q_pos)
+    q_rows = query_block(own_ref, after_ref, qb, 0)
+    d_rows = query_block(own_ref, after_ref, qb, 1)
+    top = jnp.full((8, QB), MASKED, jnp.float32)
+    for kb in tiles:
+        keys = slice(kb * KB, (kb + 1) * KB)
+        allowed = tile_allowed(base, q_pos, q_first, qb, kb)
+        k_rows = key_tile(own_ref, before_ref, kb, 0)
+        scores = jnp.where(allowed, dot_t(k_rows, q_rows), MASKED)
+        s_buf[keys, :] = scores
+        top = jnp.maximum(top, jnp.max(scores.reshape(KB // 8, 8, QB), axis=0))
+    top = jnp.max(top, axis=0, keepdims=True)
+    total = jnp.zeros((8, QB), jnp.float32)
+    for kb in tiles:
+        keys = slice(kb * KB, (kb + 1) * KB)
+        terms = jnp.exp2((s_buf[keys, :] - top) * EXPONENT)
+        s_buf[keys, :] = terms
+        total = total + jnp.sum(terms.reshape(KB // 8, 8, QB), axis=0)
+    total = jnp.sum(total, axis=0, keepdims=True)
+    inverse = 1.0 / total
+    delta = jnp.zeros((8, QB), jnp.float32)
+    for kb in tiles:
+        keys = slice(kb * KB, (kb + 1) * KB)
+        probs_b = (s_buf[keys, :] * inverse).astype(jnp.bfloat16).astype(jnp.float32)
+        weighted = probs_b * dot_t(key_tile(own_ref, before_ref, kb, 1), d_rows)
+        delta = delta + jnp.sum(weighted.reshape(KB // 8, 8, QB), axis=0)
+    return top, total, jnp.sum(delta, axis=0, keepdims=True) * total
+
+
+def down_kernel(lengths_ref, own_ref, qd_ref, s_buf, coded):
+    segment, unused_slot = place()
+    bounds = doc_bounds(lengths_ref)
+    for i in range(16):
         qd_ref[i] = own_ref[i, 2 * ROWS : 4 * ROWS, :]
+    coded[...] = jnp.zeros((2 * ROWS, HD), jnp.float32)
+    for qb in range(2):
+        stats = block_stats(bounds, segment, qb, own_tiles(qb), own_ref, None, None, s_buf)
+        for number, rest in enumerate(stats):
+            for piece in range(3):
+                rounded = rest.astype(jnp.bfloat16).astype(jnp.float32)
+                rest = rest - rounded
+                for half in range(2):
+                    row = (number * 3 + piece) * 4 + 2 * qb + half
+                    coded[row : row + 1, :] = rounded[:, half * HD : (half + 1) * HD]
+    qd_ref[16] = coded[...].astype(jnp.bfloat16)
 
 
 def stats_kernel(
-    lengths_ref,
-    own_ref,
-    before_ref,
-    after_ref,
-    own_stats,
-    after_stats,
-    k_win,
-    v_win,
-    q_win,
-    d_win,
-    s_buf,
+    lengths_ref, own_ref, before_ref, after_ref, own_stats, after_stats, s_buf, coded
 ):
     segment, unused_slot = place()
-    fill_windows(own_ref, before_ref, after_ref, k_win, v_win, q_win, d_win)
     bounds = doc_bounds(lengths_ref)
-    base = (segment - 1) * SEG
+    for qb in (1, 0):
+        stats = block_stats(bounds, segment, qb, tiles_of(qb), own_ref, before_ref, None, s_buf)
+        for number in range(3):
+            own_stats[number : number + 1, qb * QB : (qb + 1) * QB] = stats[number]
+    own_stats[3:8, :] = jnp.zeros((5, SEG), jnp.float32)
+    after_stats[...] = jnp.zeros((8, SEG), jnp.float32)
 
     def block(qb):
-        q_pos = segment * SEG + qb * QB + lax.broadcasted_iota(jnp.int32, (1, QB), 1)
-        q_first = first_positions(bounds, q_pos)
-        q_rows = q_win[qb * QB : (qb + 1) * QB, :]
-        d_rows = d_win[qb * QB : (qb + 1) * QB, :]
-        top = jnp.full((8, QB), MASKED, jnp.float32)
-        for kb in tiles_of(qb):
-            keys = slice(kb * KB, (kb + 1) * KB)
-            allowed = tile_allowed(base, q_pos, q_first, qb, kb)
-            scores = jnp.where(allowed, dot_t(k_win[keys, :], q_rows), MASKED)
-            s_buf[keys, :] = scores
-            top = jnp.maximum(top, jnp.max(scores.reshape(KB // 8, 8, QB), axis=0))
-        top = jnp.max(top, axis=0, keepdims=True)
-        total = jnp.zeros((8, QB), jnp.float32)
-        delta = jnp.zeros((8, QB), jnp.float32)
-        for kb in tiles_of(qb):
-            keys = slice(kb * KB, (kb + 1) * KB)
-            terms = jnp.exp2((s_buf[keys, :] - top) * EXPONENT)
-            s_buf[keys, :] = terms
-            total = total + jnp.sum(terms.reshape(KB // 8, 8, QB), axis=0)
-        total = jnp.sum(total, axis=0, keepdims=True)
-        inverse = 1.0 / total
-        for kb in tiles_of(qb):
-            keys = slice(kb * KB, (kb + 1) * KB)
-            probs_b = (s_buf[keys, :] * inverse).astype(jnp.bfloat16).astype(jnp.float32)
-            weighted = probs_b * dot_t(v_win[keys, :], d_rows)
-            delta = delta + jnp.sum(weighted.reshape(KB // 8, 8, QB), axis=0)
-        target = own_stats if qb < 2 else after_stats
-        cols = slice((qb % 2) * QB, (qb % 2 + 1) * QB)
-        target[0:1, cols] = top
-        target[1:2, cols] = total
-        target[2:3, cols] = jnp.sum(delta, axis=0, keepdims=True) * total
-
-    block(1)
-    block(0)
-    row = lax.broadcasted_iota(jnp.int32, (8, SEG), 0)
-    after_stats[...] = jnp.where(row == 0, MASKED, 0.0)
-    own_stats[3:8, :] = jnp.zeros((5, SEG), jnp.float32)
+        here = block_stats(bounds, segment, qb, range(8), own_ref, before_ref, after_ref, s_buf)
+        coded[...] = after_ref[16].astype(jnp.float32)
+        there = []
+        for number in range(3):
+            halves = []
+            for half in range(2):
+                row = number * 12 + 2 * (qb - 2) + half
+                halves.append(
+                    coded[row : row + 1, :]
+                    + coded[row + 4 : row + 5, :]
+                    + coded[row + 8 : row + 9, :]
+                )
+            there.append(jnp.concatenate(halves, axis=1))
+        top = jnp.maximum(here[0], there[0])
+        here_share = jnp.exp2((here[0] - top) * EXPONENT)
+        there_share = jnp.exp2((there[0] - top) * EXPONENT)
+        cols = slice((qb - 2) * QB, (qb - 1) * QB)
+        after_stats[0:1, cols] = top
+        for number in (1, 2):
+            after_stats[number : number + 1, cols] = (
+                here[number] * here_share + there[number] * there_share
+            )
+
     count = rows_after(lengths_ref, segment)
     pl.when(count > 0)(lambda: block(2))
     pl.when(count > QB)(lambda: block(3))
@@ -209,52 +247,44 @@
     after_ref,
     own_stats,
     after_stats,
-    own_there,
-    after_there,
+    there_stats,
     own_out,
     before_out,
     after_out,
-    k_win,
-    v_win,
-    q_win,
-    d_win,
     dk_acc,
     dv_acc,
     dq_acc,
 ):
     segment, unused_slot = place()
-    fill_windows(own_ref, before_ref, after_ref, k_win, v_win, q_win, d_win)
     bounds = doc_bounds(lengths_ref)
     base = (segment - 1) * SEG
-    missing = segment == 0
+    from_before = rows_after(lengths_ref, segment - 1)
 
     def block(qb):
-        q_pos = segment * SEG + qb * QB + lax.broadcasted_iota(jnp.int32, (1, QB), 1)
+        q_pos = positions(segment, qb)
         q_first = first_positions(bounds, q_pos)
-        rows = slice(qb * QB, (qb + 1) * QB)
-        q_rows = q_win[rows, :]
-        d_rows = d_win[rows, :]
+        q_rows = query_block(own_ref, after_ref, qb, 0)
+        d_rows = query_block(own_ref, after_ref, qb, 1)
         cols = slice((qb % 2) * QB, (qb % 2 + 1) * QB)
-        here = (own_stats if qb < 2 else after_stats)[:, cols]
-        there = (own_there if qb < 2 else after_there)[:, cols]
         if qb < 2:
-            row = lax.broadcasted_iota(jnp.int32, (8, QB), 0)
-            there = jnp.where(missing, jnp.where(row == 0, MASKED, 0.0), there)
-        top = jnp.maximum(here[0:1, :], there[0:1, :])
-        here_share = jnp.exp2((here[0:1, :] - top) * EXPONENT)
-        there_share = jnp.exp2((there[0:1, :] - top) * EXPONENT)
-        total = here[1:2, :] * here_share + there[1:2, :] * there_share
-        total = jnp.maximum(total, 1e-30)
-        delta = (here[2:3, :] * here_share + there[2:3, :] * there_share) / total
+            whole = q_pos - segment * SEG >= from_before
+            stats = [
+                jnp.where(whole, own_stats[n : n + 1, cols], there_stats[n : n + 1, cols])
+                for n in range(3)
+            ]
+        else:
+            stats = [after_stats[n : n + 1, cols] for n in range(3)]
+        top, total, delta = stats
+        delta = delta / total
         log_total = top * EXPONENT + jnp.log2(total)
         dq = jnp.zeros((QB, HD), jnp.float32)
         for kb in tiles_of(qb):
             keys = slice(kb * KB, (kb + 1) * KB)
             allowed = tile_allowed(base, q_pos, q_first, qb, kb)
-            k_rows = k_win[keys, :]
+            k_rows = key_tile(own_ref, before_ref, kb, 0)
             power = jnp.where(allowed, dot_t(k_rows, q_rows) * EXPONENT - log_total, MASKED)
             probs = jnp.exp2(power)
-            d_probs = dot_t(v_win[keys, :], d_rows)
+            d_probs = dot_t(key_tile(own_ref, before_ref, kb, 1), d_rows)
             d_scores = (probs * (d_probs - delta)).astype(jnp.bfloat16)
             dv = jnp.dot(probs.astype(jnp.bfloat16), d_rows, preferred_element_type=jnp.float32)
             dk = jnp.dot(d_scores, q_rows, preferred_element_type=jnp.float32)
@@ -267,7 +297,7 @@
             dq = dq + lax.dot_general(
                 d_scores, k_rows, CONTRACT_FIRST, preferred_element_type=jnp.float32
             )
-        dq_acc[rows, :] = dq * SCALE
+        dq_acc[qb * QB : (qb + 1) * QB, :] = dq * SCALE
 
     dq_acc[SEG:WIN, :] = jnp.zeros((SEG, HD), jnp.float32)
     block(1)
@@ -353,27 +383,34 @@
         limit=60 << 20,
     )
     own = exchange(chunks)
-    kv, qd = call(split_kernel, (own,), (half, half), [VMEM])
+    (kv,) = call(split_kernel, (own,), (half,), [VMEM])
     kv_before = to_after(kv)
+    scores = pltpu.VMEM((WIN, QB), jnp.float32)
+    coded = pltpu.VMEM((2 * ROWS, HD), jnp.float32)
+    (qd,) = call(
+        down_kernel,
+        (doc_lengths, own),
+        (bf16(17, 2 * ROWS, HD),),
+        [SMEM, VMEM],
+        scratch=[scores, coded],
+    )
     qd_after = to_before(qd)
-    windows = [pltpu.VMEM((WIN, HD), jnp.bfloat16)] * 4
     stats = jax.ShapeDtypeStruct((8, SEG), jnp.float32)
     own_stats, after_stats = call(
         stats_kernel,
         (doc_lengths, own, kv_before, qd_after),
         (stats, stats),
         [SMEM] + [VMEM] * 3,
-        scratch=windows + [pltpu.VMEM((WIN, QB), jnp.float32)],
+        scratch=[scores, coded],
         limit=32 << 20,
     )
-    own_there = to_after(after_stats)
-    after_there = to_before(own_stats)
+    there_stats = to_after(after_stats)
     own_grads, before_grads, after_grads = call(
         grads_kernel,
-        (doc_lengths, own, kv_before, qd_after, own_stats, after_stats, own_there, after_there),
+        (doc_lengths, own, kv_before, qd_after, own_stats, after_stats, there_stats),
         (jax.ShapeDtypeStruct((16, 3 * ROWS, HD), jnp.float32), half, bf16(16, ROWS, HD)),
-        [SMEM] + [VMEM] * 7,
-        scratch=windows + [pltpu.VMEM((WIN, HD), jnp.float32)] * 3,
+        [SMEM] + [VMEM] * 6,
+        scratch=[pltpu.VMEM((WIN, HD), jnp.float32)] * 3,
         limit=32 << 20,
     )
     dkv_there = to_before(before_grads)

time: 99.1 us -> 97.7 us (0.986)
  the two profiles are of different devices: /device:TPU:25 before, /device:TPU:17 now
where the time goes in v4:
time: 97.7 us; the launch traced here: 97.3 us
  blocking collectives  33.3 us (34%)
  waiting for transfers between devices  30.3 us (31%)
  starting transfers between devices  20.5 us (21%)
  Pallas kernels  12.6 us (13%)
    all_to_all x2, blocking collectives, exchange(): lax.all_to_all(chunks, AXES, split_axis=0, concat_axis=0, axis_index_grou...  33.3 us
    ppermute x3, waiting for transfers between devices, to_after(): return lax.ppermute(block, AXES, UP)  30.3 us
    pallas_call x7, Pallas kernels, call(): pl.pallas_call(kernel, in_specs=specs, out_specs=[VMEM] * len(outputs), o...  12.6 us
    ppermute x2, starting transfers between devices, to_before(): return lax.ppermute(block, AXES, DOWN)  12.4 us
    ppermute x3, starting transfers between devices, to_after(): return lax.ppermute(block, AXES, UP)  8.1 us
  transfers between devices with their start and end apart: 5, of which 3 were waited for; matrix products, arithmetic and copies ran while one was open for 0% of the time, Pallas kernels for 0%

profile of v4, /device:TPU:17, one launch (start us, length us, event | category | flops | bytes accessed | tf_op | source)
XLA Modules:
  0.0 97.3 jit_solution(2089766862880783130)
XLA Ops:
  0.6 1.9 %pack_kernel.1 = bf16[16,128,128]{2,1,0:T(8,128)(2,1)} custom-call(bf16[32,2048]{1,0:T(8,128)(2,1)} %q_hbm.1, bf16[32,2048]{1,0:T(8,128)(2,1)} %k_hbm.1, bf16[32,2048]{1,0:T(8,128)(2,1)} %v_hbm.1, bf16[32,2048]{1,0:T(8,128)(2,1)} %d_hbm.1), custom_call_target="tpu_custom_call" | custom-call | tf_op jit(solution)/shard_map/pack_kernel/pallas_call | solution.py:363
  2.6 0.0 copy-start.2
  2.6 16.6 %all_to_all.10.own_ref = bf16[16,128,128]{2,1,0:T(8,128)(2,1)S(1)} all-to-all(bf16[16,128,128]{2,1,0:T(8,128)(2,1)} %pack_kernel.1), channel_id=1, replica_groups={{0,1,2,3,8,9,10,11,16,17,18,19,24,25,26,27},{32,33,34,35,40,41,42,43,48..., dimensions={0} | all-to-all | bytes 1048576 | tf_op jit(solution)/shard_map/all_to_all | solution.py:46
  19.2 0.0 copy-done.2
  19.2 1.1 %down_kernel.1 = bf16[17,64,128]{2,1,0:T(8,128)(2,1)S(1)} custom-call(s32[32]{0:T(128)S(1)} %copy-done.2, bf16[16,128,128]{2,1,0:T(8,128)(2,1)S(1)} %all_to_all.10.own_ref), custom_call_target="tpu_custom_call" | custom-call | tf_op jit(solution)/shard_map/down_kernel/pallas_call | solution.py:363
  20.3 10.5 %collective-permute-start.1 = (bf16[17,64,128]{2,1,0:T(8,128)(2,1)S(1)}, bf16[17,64,128]{2,1,0:T(8,128)(2,1)S(1)}, u32[]{:S(2)}, u32[]{:S(2)}) collective-permute-start(bf16[17,64,128]{2,1,0:T(8,128)(2,1)S(1)} %down_kernel.1), channel_id=1, source_target_pairs={{32,0},{33,1},{34,2},{35,3},{40,8},{41,9},{42,10},{43,11},{48,16},... | collective-permute-start | bytes 835592 | tf_op jit(solution)/shard_map/ppermute | solution.py:42
  30.8 1.9 %collective-permute-start = (bf16[16,64,128]{2,1,0:T(8,128)(2,1)S(1)}, bf16[16,64,128]{2,1,0:T(8,128)(2,1)S(1)}, u32[]{:S(2)}, u32[]{:S(2)}) collective-permute-start(bf16[16,64,128]{2,1,0:T(8,128)(2,1)S(1)} %split_kernel.1), channel_id=1, source_target_pairs={{0,32},{1,33},{2,34},{3,35},{8,40},{9,41},{10,42},{11,43},{16,48},... | collective-permute-start | bytes 786440 | tf_op jit(solution)/shard_map/ppermute | solution.py:38
  32.7 17.1 %collective-permute-done.before_ref = bf16[16,64,128]{2,1,0:T(8,128)(2,1)S(1)} collective-permute-done((bf16[16,64,128]{2,1,0:T(8,128)(2,1)S(1)}, bf16[16,64,128]{2,1,0:T(8,128)(2,1)S(1)}, u32[]{:S(2)}, u32[]{:S(2)}) %collective-permute-start) | collective-permute-done | bytes 262176 | tf_op jit(solution)/shard_map/ppermute | solution.py:38
  49.9 0.0 collective-permute-done.1.after_ref
  49.9 2.9 %stats_kernel.1 = (f32[8,512]{1,0:T(8,128)S(1)}, f32[8,512]{1,0:T(8,128)S(1)}) custom-call(s32[32]{0:T(128)S(1)} %copy-done.2, bf16[16,128,128]{2,1,0:T(8,128)(2,1)S(1)} %all_to_all.10.own_ref, bf16[16,64,128]{2,1,0:T(8,128)(2,1)S(1)} %collective-permute-done.before_ref, bf16[17,64,128]{2,1,0:T(8,128)(2,1)S(1)} %collective-permute-done.1.after_ref), custom_call_target="tpu_custom_call" | custom-call | tf_op jit(solution)/shard_map/stats_kernel/pallas_call | solution.py:363
  52.8 1.9 %collective-permute-start.2 = (f32[8,512]{1,0:T(8,128)S(1)}, f32[8,512]{1,0:T(8,128)S(1)}, u32[]{:S(2)}, u32[]{:S(2)}) collective-permute-start(f32[8,512]{1,0:T(8,128)S(1)} %get-tuple-element.11.after_stats), channel_id=1, source_target_pairs={{0,32},{1,33},{2,34},{3,35},{8,40},{9,41},{10,42},{11,43},{16,48},... | collective-permute-start | bytes 49160 | tf_op jit(solution)/shard_map/ppermute | solution.py:38
  54.8 7.1 %collective-permute-done.2.there_stats = f32[8,512]{1,0:T(8,128)S(1)} collective-permute-done((f32[8,512]{1,0:T(8,128)S(1)}, f32[8,512]{1,0:T(8,128)S(1)}, u32[]{:S(2)}, u32[]{:S(2)}) %collective-permute-start.2) | collective-permute-done | bytes 16416 | tf_op jit(solution)/shard_map/ppermute | solution.py:38
  61.8 5.4 %grads_kernel.1 = (f32[16,96,128]{2,1,0:T(8,128)S(1)}, bf16[16,64,128]{2,1,0:T(8,128)(2,1)S(1)}, bf16[16,32,128]{2,1,0:T(8,128)(2,1)S(1)}) custom-call(s32[32]{0:T(128)S(1)} %copy-done.2, bf16[16,128,128]{2,1,0:T(8,128)(2,1)S(1)} %all_to_all.10.own_ref, bf16[16,64,128]{2,1,0:T(8,128)(2,1)S(1)} %collective-permute-done.before_ref, ...), custom_call_target="tpu_custom_call" | custom-call | tf_op jit(solution)/shard_map/grads_kernel/pallas_call | solution.py:363
  67.2 1.9 %collective-permute-start.4 = (bf16[16,64,128]{2,1,0:T(8,128)(2,1)S(1)}, bf16[16,64,128]{2,1,0:T(8,128)(2,1)S(1)}, u32[]{:S(2)}, u32[]{:S(2)}) collective-permute-start(bf16[16,64,128]{2,1,0:T(8,128)(2,1)S(1)} %get-tuple-element.14), channel_id=1, source_target_pairs={{32,0},{33,1},{34,2},{35,3},{40,8},{41,9},{42,10},{43,11},{48,16},... | collective-permute-start | bytes 786440 | tf_op jit(solution)/shard_map/ppermute | solution.py:42
  69.2 4.3 %collective-permute-start.3 = (bf16[16,32,128]{2,1,0:T(8,128)(2,1)S(1)}, bf16[16,32,128]{2,1,0:T(8,128)(2,1)S(1)}, u32[]{:S(2)}, u32[]{:S(2)}) collective-permute-start(bf16[16,32,128]{2,1,0:T(8,128)(2,1)S(1)} %get-tuple-element.13), channel_id=1, source_target_pairs={{0,32},{1,33},{2,34},{3,35},{8,40},{9,41},{10,42},{11,43},{16,48},... | collective-permute-start | bytes 393224 | tf_op jit(solution)/shard_map/ppermute | solution.py:38
  73.4 6.1 %collective-permute-done.3.dq_ref = bf16[16,32,128]{2,1,0:T(8,128)(2,1)S(1)} collective-permute-done((bf16[16,32,128]{2,1,0:T(8,128)(2,1)S(1)}, bf16[16,32,128]{2,1,0:T(8,128)(2,1)S(1)}, u32[]{:S(2)}, u32[]{:S(2)}) %collective-permute-start.3) | collective-permute-done | bytes 131104 | tf_op jit(solution)/shard_map/ppermute | solution.py:38
  79.5 0.0 collective-permute-done.4.dkv_ref
  79.5 0.1 merge_kernel.1
  79.6 0.0 copy-start
  79.6 0.0 copy-start.1
  79.6 16.7 %all_to_all.11.back_ref = bf16[16,96,128]{2,1,0:T(8,128)(2,1)S(1)} all-to-all(bf16[16,96,128]{2,1,0:T(8,128)(2,1)S(1)} %merge_kernel.1), channel_id=1, replica_groups={{0,1,2,3,8,9,10,11,16,17,18,19,24,25,26,27},{32,33,34,35,40,41,42,43,48..., dimensions={0} | all-to-all | bytes 786432 | tf_op jit(solution)/shard_map/all_to_all | solution.py:46
  96.3 0.0 copy-done
  96.3 0.0 copy-done.1
  96.3 1.0 %finish_kernel.1 = (bf16[32,2048]{1,0:T(8,128)(2,1)}, bf16[32,2048]{1,0:T(8,128)(2,1)}, bf16[32,2048]{1,0:T(8,128)(2,1)}, f32[32,2048]{1,0:T(8,128)}, f32[32,2048]{1,0:T(8,128)}) custom-call(bf16[16,96,128]{2,1,0:T(8,128)(2,1)S(1)} %all_to_all.11.back_ref, f32[32,2048]{1,0:T(8,128)S(1)} %copy-done, f32[32,2048]{1,0:T(8,128)S(1)} %copy-done.1), custom_call_target="tpu_custom_call" | custom-call | tf_op jit(solution)/shard_map/finish_kernel/pallas_call | solution.py:363
  (1 shorter events, 0.0 us)
Async XLA Ops:
  2.6 16.6 %copy-start.2 = (s32[32]{0:T(128)S(1)}, s32[32]{0:T(128)}, u32[]{:S(2)}) copy-start(s32[32]{0:T(128)} %lengths_ref.5) | copy-start | bytes 388
  20.3 29.6 %collective-permute-start.1 = (bf16[17,64,128]{2,1,0:T(8,128)(2,1)S(1)}, bf16[17,64,128]{2,1,0:T(8,128)(2,1)S(1)}, u32[]{:S(2)}, u32[]{:S(2)}) collective-permute-start(bf16[17,64,128]{2,1,0:T(8,128)(2,1)S(1)} %down_kernel.1), channel_id=1, source_target_pairs={{32,0},{33,1},{34,2},{35,3},{40,8},{41,9},{42,10},{43,11},{48,16},... | collective-permute-start | bytes 835592 | tf_op jit(solution)/shard_map/ppermute | solution.py:42
  30.8 19.1 %collective-permute-start = (bf16[16,64,128]{2,1,0:T(8,128)(2,1)S(1)}, bf16[16,64,128]{2,1,0:T(8,128)(2,1)S(1)}, u32[]{:S(2)}, u32[]{:S(2)}) collective-permute-start(bf16[16,64,128]{2,1,0:T(8,128)(2,1)S(1)} %split_kernel.1), channel_id=1, source_target_pairs={{0,32},{1,33},{2,34},{3,35},{8,40},{9,41},{10,42},{11,43},{16,48},... | collective-permute-start | bytes 786440 | tf_op jit(solution)/shard_map/ppermute | solution.py:38
  52.8 9.0 %collective-permute-start.2 = (f32[8,512]{1,0:T(8,128)S(1)}, f32[8,512]{1,0:T(8,128)S(1)}, u32[]{:S(2)}, u32[]{:S(2)}) collective-permute-start(f32[8,512]{1,0:T(8,128)S(1)} %get-tuple-element.11.after_stats), channel_id=1, source_target_pairs={{0,32},{1,33},{2,34},{3,35},{8,40},{9,41},{10,42},{11,43},{16,48},... | collective-permute-start | bytes 49160 | tf_op jit(solution)/shard_map/ppermute | solution.py:38
  67.2 12.3 %collective-permute-start.4 = (bf16[16,64,128]{2,1,0:T(8,128)(2,1)S(1)}, bf16[16,64,128]{2,1,0:T(8,128)(2,1)S(1)}, u32[]{:S(2)}, u32[]{:S(2)}) collective-permute-start(bf16[16,64,128]{2,1,0:T(8,128)(2,1)S(1)} %get-tuple-element.14), channel_id=1, source_target_pairs={{32,0},{33,1},{34,2},{35,3},{40,8},{41,9},{42,10},{43,11},{48,16},... | collective-permute-start | bytes 786440 | tf_op jit(solution)/shard_map/ppermute | solution.py:42
  69.2 10.3 %collective-permute-start.3 = (bf16[16,32,128]{2,1,0:T(8,128)(2,1)S(1)}, bf16[16,32,128]{2,1,0:T(8,128)(2,1)S(1)}, u32[]{:S(2)}, u32[]{:S(2)}) collective-permute-start(bf16[16,32,128]{2,1,0:T(8,128)(2,1)S(1)} %get-tuple-element.13), channel_id=1, source_target_pairs={{0,32},{1,33},{2,34},{3,35},{8,40},{9,41},{10,42},{11,43},{16,48},... | collective-permute-start | bytes 393224 | tf_op jit(solution)/shard_map/ppermute | solution.py:38
  79.6 16.7 %copy-start = (f32[32,2048]{1,0:T(8,128)S(1)}, f32[32,2048]{1,0:T(8,128)}, u32[]{:S(2)}) copy-start(f32[32,2048]{1,0:T(8,128)} %key_prior_ref.1) | copy-start | bytes 786436
  79.6 16.7 %copy-start.1 = (f32[32,2048]{1,0:T(8,128)S(1)}, f32[32,2048]{1,0:T(8,128)}, u32[]{:S(2)}) copy-start(f32[32,2048]{1,0:T(8,128)} %value_prior_ref.1) | copy-start | bytes 786436

commit v5 on v4

--- a/solution.py
+++ b/solution.py
@@ -57,31 +57,36 @@
     return segment.astype(jnp.int32), slot.astype(jnp.int32)
 
 
-def doc_bounds(lengths_ref):
-    bounds = []
-    first = jnp.int32(0)
-    for doc in range(NDOC):
-        bounds.append(first)
-        first = first + lengths_ref[doc]
-    return bounds
-
-
-def rows_after(lengths_ref, segment):
+def rows_after(table, segment):
     start = segment * SEG
     count = jnp.int32(0)
+    for first, end in table:
+        count = jnp.maximum(count, jnp.where(first < start, end - start - SEG, 0))
+    return count
+
+
+def fill_info(lengths_ref, info_ref):
+    segment, unused_slot = place()
+    table = []
     first = jnp.int32(0)
     for doc in range(NDOC):
         end = first + lengths_ref[doc]
-        count = jnp.maximum(count, jnp.where(first < start, end - start - SEG, 0))
+        table.append((first, end))
         first = end
-    return count
-
-
-def first_positions(bounds, q_pos):
-    q_first = jnp.zeros(q_pos.shape, jnp.int32)
-    for first in bounds:
-        q_first = jnp.where(q_pos >= first, first, q_first)
-    return jnp.where(q_pos >= TOKENS, TOKENS, q_first)
+    for part in range(2):
+        q_pos = (segment + part) * SEG + lax.broadcasted_iota(jnp.int32, (1, SEG), 1)
+        q_first = jnp.zeros((1, SEG), jnp.int32)
+        for first, unused_end in table:
+            q_first = jnp.where(q_pos >= first, first, q_first)
+        q_first = jnp.where(q_pos >= TOKENS, TOKENS, q_first)
+        info_ref[part : part + 1, :] = q_first - segment * SEG
+        count = rows_after(table, segment - part)
+        info_ref[2 + part : 3 + part, :] = jnp.full((1, SEG), count, jnp.int32)
+    info_ref[4:8, :] = jnp.zeros((4, SEG), jnp.int32)
+
+
+def info_scalar(info_ref, row):
+    return jnp.max(info_ref[row : row + 1, 0:HD])
 
 
 def tiles_of(qb):
@@ -109,14 +114,12 @@
     return rows_of(after_ref, 8 * (qb - 2), 8, part)
 
 
-def positions(segment, qb):
-    return segment * SEG + qb * QB + lax.broadcasted_iota(jnp.int32, (1, QB), 1)
-
-
-def tile_allowed(base, q_pos, q_first, qb, kb):
-    k_pos = base + kb * KB + lax.broadcasted_iota(jnp.int32, (KB, QB), 0)
+def tile_allowed(info_ref, qb, kb):
+    q_first = info_ref[qb // 2 : qb // 2 + 1, (qb % 2) * QB : (qb % 2 + 1) * QB]
+    k_pos = kb * KB - SEG + lax.broadcasted_iota(jnp.int32, (KB, QB), 0)
     allowed = k_pos >= q_first
     if kb >= 4 + 2 * qb:
+        q_pos = qb * QB + lax.broadcasted_iota(jnp.int32, (1, QB), 1)
         allowed = allowed & (k_pos <= q_pos)
     return allowed
 
@@ -149,18 +152,14 @@
         kv_ref[i] = own_ref[i, 0 : 2 * ROWS, :]
 
 
-def block_stats(bounds, segment, qb, tiles, own_ref, before_ref, after_ref, s_buf):
-    base = (segment - 1) * SEG
-    q_pos = positions(segment, qb)
-    q_first = first_positions(bounds, q_pos)
+def block_stats(info_ref, qb, tiles, own_ref, before_ref, after_ref, s_buf):
     q_rows = query_block(own_ref, after_ref, qb, 0)
     d_rows = query_block(own_ref, after_ref, qb, 1)
     top = jnp.full((8, QB), MASKED, jnp.float32)
     for kb in tiles:
         keys = slice(kb * KB, (kb + 1) * KB)
-        allowed = tile_allowed(base, q_pos, q_first, qb, kb)
         k_rows = key_tile(own_ref, before_ref, kb, 0)
-        scores = jnp.where(allowed, dot_t(k_rows, q_rows), MASKED)
+        scores = jnp.where(tile_allowed(info_ref, qb, kb), dot_t(k_rows, q_rows), MASKED)
         s_buf[keys, :] = scores
         top = jnp.maximum(top, jnp.max(scores.reshape(KB // 8, 8, QB), axis=0))
     top = jnp.max(top, axis=0, keepdims=True)
@@ -181,14 +180,13 @@
     return top, total, jnp.sum(delta, axis=0, keepdims=True) * total
 
 
-def down_kernel(lengths_ref, own_ref, qd_ref, s_buf, coded):
-    segment, unused_slot = place()
-    bounds = doc_bounds(lengths_ref)
+def down_kernel(lengths_ref, own_ref, kv_ref, qd_ref, info_ref, s_buf, coded):
     for i in range(16):
         qd_ref[i] = own_ref[i, 2 * ROWS : 4 * ROWS, :]
+    fill_info(lengths_ref, info_ref)
     coded[...] = jnp.zeros((2 * ROWS, HD), jnp.float32)
     for qb in range(2):
-        stats = block_stats(bounds, segment, qb, own_tiles(qb), own_ref, None, None, s_buf)
+        stats = block_stats(info_ref, qb, own_tiles(qb), own_ref, None, None, s_buf)
         for number, rest in enumerate(stats):
             for piece in range(3):
                 rounded = rest.astype(jnp.bfloat16).astype(jnp.float32)
@@ -199,21 +197,19 @@
     qd_ref[16] = coded[...].astype(jnp.bfloat16)
 
 
-def stats_kernel(
-    lengths_ref, own_ref, before_ref, after_ref, own_stats, after_stats, s_buf, coded
-):
-    segment, unused_slot = place()
-    bounds = doc_bounds(lengths_ref)
+def own_stats_kernel(info_ref, own_ref, before_ref, own_stats, s_buf):
     for qb in (1, 0):
-        stats = block_stats(bounds, segment, qb, tiles_of(qb), own_ref, before_ref, None, s_buf)
+        stats = block_stats(info_ref, qb, tiles_of(qb), own_ref, before_ref, None, s_buf)
         for number in range(3):
             own_stats[number : number + 1, qb * QB : (qb + 1) * QB] = stats[number]
     own_stats[3:8, :] = jnp.zeros((5, SEG), jnp.float32)
+
+
+def after_stats_kernel(info_ref, own_ref, before_ref, after_ref, after_stats, s_buf, coded):
     after_stats[...] = jnp.zeros((8, SEG), jnp.float32)
 
     def block(qb):
-        here = block_stats(bounds, segment, qb, range(8), own_ref, before_ref, after_ref, s_buf)
-        coded[...] = after_ref[16].astype(jnp.float32)
+        here = block_stats(info_ref, qb, range(8), own_ref, before_ref, after_ref, s_buf)
         there = []
         for number in range(3):
             halves = []
@@ -235,19 +231,75 @@
                 here[number] * here_share + there[number] * there_share
             )
 
-    count = rows_after(lengths_ref, segment)
+    count = info_scalar(info_ref, 2)
+
+    @pl.when(count > 0)
+    def first_block():
+        coded[...] = after_ref[16].astype(jnp.float32)
+        block(2)
+
+    pl.when(count > QB)(lambda: block(3))
+
+
+def block_grads(
+    info_ref, qb, stats, own_ref, before_ref, after_ref, dk_acc, dv_acc, dq_acc
+):
+    q_rows = query_block(own_ref, after_ref, qb, 0)
+    d_rows = query_block(own_ref, after_ref, qb, 1)
+    top, total, delta = stats
+    delta = delta / total
+    log_total = top * EXPONENT + jnp.log2(total)
+    dq = jnp.zeros((HD, QB), jnp.float32)
+    for kb in tiles_of(qb):
+        keys = slice(kb * KB, (kb + 1) * KB)
+        k_rows = key_tile(own_ref, before_ref, kb, 0)
+        power = dot_t(k_rows, q_rows) * EXPONENT - log_total
+        probs = jnp.exp2(jnp.where(tile_allowed(info_ref, qb, kb), power, MASKED))
+        d_probs = dot_t(key_tile(own_ref, before_ref, kb, 1), d_rows)
+        d_scores = (probs * (d_probs - delta)).astype(jnp.bfloat16)
+        dv_acc[keys, :] = dv_acc[keys, :] + jnp.dot(
+            probs.astype(jnp.bfloat16), d_rows, preferred_element_type=jnp.float32
+        )
+        dk_acc[keys, :] = dk_acc[keys, :] + jnp.dot(
+            d_scores, q_rows, preferred_element_type=jnp.float32
+        )
+        dq = dq + lax.dot_general(
+            k_rows, d_scores, CONTRACT_FIRST, preferred_element_type=jnp.float32
+        )
+    dq_acc[qb * QB : (qb + 1) * QB, :] = dq.T * SCALE
+
+
+def early_kernel(
+    info_ref, own_ref, before_ref, after_ref, own_stats, after_stats, dk_acc, dv_acc, dq_acc
+):
+    for acc in (dk_acc, dv_acc, dq_acc):
+        acc[...] = jnp.zeros((WIN, HD), jnp.float32)
+
+    def block(qb):
+        cols = slice((qb % 2) * QB, (qb % 2 + 1) * QB)
+        ref = own_stats if qb < 2 else after_stats
+        stats = [ref[n : n + 1, cols] for n in range(3)]
+        block_grads(
+            info_ref, qb, stats, own_ref, before_ref, after_ref, dk_acc, dv_acc, dq_acc
+        )
+
+    from_before = info_scalar(info_ref, 3)
+    count = info_scalar(info_ref, 2)
+    pl.when(from_before <= QB)(lambda: block(1))
+    pl.when(from_before <= 0)(lambda: block(0))
     pl.when(count > 0)(lambda: block(2))
     pl.when(count > QB)(lambda: block(3))
 
 
-def grads_kernel(
-    lengths_ref,
+def late_kernel(
+    info_ref,
     own_ref,
     before_ref,
-    after_ref,
     own_stats,
-    after_stats,
     there_stats,
+    dk_in,
+    dv_in,
+    dq_in,
     own_out,
     before_out,
     after_out,
@@ -255,57 +307,23 @@
     dv_acc,
     dq_acc,
 ):
-    segment, unused_slot = place()
-    bounds = doc_bounds(lengths_ref)
-    base = (segment - 1) * SEG
-    from_before = rows_after(lengths_ref, segment - 1)
+    dk_acc[...] = dk_in[...]
+    dv_acc[...] = dv_in[...]
+    dq_acc[...] = dq_in[...]
 
     def block(qb):
-        q_pos = positions(segment, qb)
-        q_first = first_positions(bounds, q_pos)
-        q_rows = query_block(own_ref, after_ref, qb, 0)
-        d_rows = query_block(own_ref, after_ref, qb, 1)
-        cols = slice((qb % 2) * QB, (qb % 2 + 1) * QB)
-        if qb < 2:
-            whole = q_pos - segment * SEG >= from_before
-            stats = [
-                jnp.where(whole, own_stats[n : n + 1, cols], there_stats[n : n + 1, cols])
-                for n in range(3)
-            ]
-        else:
-            stats = [after_stats[n : n + 1, cols] for n in range(3)]
-        top, total, delta = stats
-        delta = delta / total
-        log_total = top * EXPONENT + jnp.log2(total)
-        dq = jnp.zeros((QB, HD), jnp.float32)
-        for kb in tiles_of(qb):
-            keys = slice(kb * KB, (kb + 1) * KB)
-            allowed = tile_allowed(base, q_pos, q_first, qb, kb)
-            k_rows = key_tile(own_ref, before_ref, kb, 0)
-            power = jnp.where(allowed, dot_t(k_rows, q_rows) * EXPONENT - log_total, MASKED)
-            probs = jnp.exp2(power)
-            d_probs = dot_t(key_tile(own_ref, before_ref, kb, 1), d_rows)
-            d_scores = (probs * (d_probs - delta)).astype(jnp.bfloat16)
-            dv = jnp.dot(probs.astype(jnp.bfloat16), d_rows, preferred_element_type=jnp.float32)
-            dk = jnp.dot(d_scores, q_rows, preferred_element_type=jnp.float32)
-            if qb == 1:
-                dv_acc[keys, :] = dv
-                dk_acc[keys, :] = dk
-            else:
-                dv_acc[keys, :] = dv_acc[keys, :] + dv
-                dk_acc[keys, :] = dk_acc[keys, :] + dk
-            dq = dq + lax.dot_general(
-                d_scores, k_rows, CONTRACT_FIRST, preferred_element_type=jnp.float32
-            )
-        dq_acc[qb * QB : (qb + 1) * QB, :] = dq * SCALE
-
-    dq_acc[SEG:WIN, :] = jnp.zeros((SEG, HD), jnp.float32)
-    block(1)
-    block(0)
-    count = rows_after(lengths_ref, segment)
-    pl.when(count > 0)(lambda: block(2))
-    pl.when(count > QB)(lambda: block(3))
-
+        cols = slice(qb * QB, (qb + 1) * QB)
+        row = qb * QB + lax.broadcasted_iota(jnp.int32, (1, QB), 1)
+        here = row >= info_ref[3:4, cols]
+        stats = [
+            jnp.where(here, own_stats[n : n + 1, cols], there_stats[n : n + 1, cols])
+            for n in range(3)
+        ]
+        block_grads(info_ref, qb, stats, own_ref, before_ref, None, dk_acc, dv_acc, dq_acc)
+
+    from_before = info_scalar(info_ref, 3)
+    pl.when(from_before > QB)(lambda: block(1))
+    pl.when(from_before > 0)(lambda: block(0))
     for i in range(16):
         low = slice(i * ROWS, (i + 1) * ROWS)
         high = slice(SEG + i * ROWS, SEG + (i + 1) * ROWS)
@@ -357,15 +375,21 @@
 
 
 HBM = pl.BlockSpec(memory_space=pltpu.HBM)
-
-
-def call(kernel, inputs, outputs, specs, scratch=(), limit=16 << 20):
+ANY = pl.BlockSpec(memory_space=pl.ANY)
+
+
+def call(
+    kernel, inputs, outputs, specs, scratch=(), limit=16 << 20, gflop=0.5
+):
     return pl.pallas_call(
         kernel,
         in_specs=specs,
         out_specs=[VMEM] * len(outputs),
         out_shape=list(outputs),
         scratch_shapes=list(scratch),
+        cost_estimate=pl.CostEstimate(
+            flops=int(gflop * 1e9), bytes_accessed=1 << 20, transcendentals=0
+        ),
         compiler_params=pltpu.CompilerParams(vmem_limit_bytes=limit),
         name=kernel.__name__,
     )(*inputs)
@@ -387,31 +411,52 @@
     kv_before = to_after(kv)
     scores = pltpu.VMEM((WIN, QB), jnp.float32)
     coded = pltpu.VMEM((2 * ROWS, HD), jnp.float32)
-    (qd,) = call(
+    qd, info = call(
         down_kernel,
-        (doc_lengths, own),
-        (bf16(17, 2 * ROWS, HD),),
-        [SMEM, VMEM],
+        (doc_lengths, own, kv),
+        (bf16(17, 2 * ROWS, HD), jax.ShapeDtypeStruct((8, SEG), jnp.int32)),
+        [SMEM, VMEM, ANY],
         scratch=[scores, coded],
+        gflop=1.0,
     )
     qd_after = to_before(qd)
     stats = jax.ShapeDtypeStruct((8, SEG), jnp.float32)
-    own_stats, after_stats = call(
-        stats_kernel,
-        (doc_lengths, own, kv_before, qd_after),
-        (stats, stats),
-        [SMEM] + [VMEM] * 3,
+    (own_stats,) = call(
+        own_stats_kernel,
+        (info, own, kv_before),
+        (stats,),
+        [VMEM] * 3,
+        scratch=[scores],
+        gflop=1.5,
+    )
+    (after_stats,) = call(
+        after_stats_kernel,
+        (info, own, kv_before, qd_after),
+        (stats,),
+        [VMEM] * 4,
         scratch=[scores, coded],
-        limit=32 << 20,
+        gflop=1.0,
     )
     there_stats = to_after(after_stats)
+    acc = jax.ShapeDtypeStruct((WIN, HD), jnp.float32)
+    sums = call(
+        early_kernel,
+        (info, own, kv_before, qd_after, own_stats, after_stats),
+        (acc,) * 3,
+        [VMEM] * 6,
+        gflop=2.5,
+    )
     own_grads, before_grads, after_grads = call(
-        grads_kernel,
-        (doc_lengths, own, kv_before, qd_after, own_stats, after_stats, there_stats),
-        (jax.ShapeDtypeStruct((16, 3 * ROWS, HD), jnp.float32), half, bf16(16, ROWS, HD)),
-        [SMEM] + [VMEM] * 6,
+        late_kernel,
+        (info, own, kv_before, own_stats, there_stats, *sums),
+        (
+            jax.ShapeDtypeStruct((16, 3 * ROWS, HD), jnp.float32),
+            half,
+            bf16(16, ROWS, HD),
+        ),
+        [VMEM] * 8,
         scratch=[pltpu.VMEM((WIN, HD), jnp.float32)] * 3,
-        limit=32 << 20,
+        gflop=2.0,
     )
     dkv_there = to_before(before_grads)
     dq_there = to_after(after_grads)

time: 97.7 us -> 93.5 us (0.957)
  the two profiles are of different devices: /device:TPU:17 before, /device:TPU:25 now
where the time goes in v5:
time: 93.5 us; the launch traced here: 93.1 us
  waiting for transfers between devices  29.4 us (31%)
  blocking collectives  28.6 us (31%)
  starting transfers between devices  25.4 us (27%)
  Pallas kernels  8.95 us (10%)
    all_to_all x2, blocking collectives, exchange(): lax.all_to_all(chunks, AXES, split_axis=0, concat_axis=0, axis_index_grou...  28.6 us
    ppermute x3, starting transfers between devices, to_after(): return lax.ppermute(block, AXES, UP)  20.6 us
    ppermute x2, waiting for transfers between devices, to_before(): return lax.ppermute(block, AXES, DOWN)  17.4 us
    ppermute x3, waiting for transfers between devices, to_after(): return lax.ppermute(block, AXES, UP)  12 us
    pallas_call x9, Pallas kernels, call(): pl.pallas_call(kernel, in_specs=specs, out_specs=[VMEM] * len(outputs), o...  8.95 us
    ppermute x2, starting transfers between devices, to_before(): return lax.ppermute(block, AXES, DOWN)  4.78 us
  transfers between devices with their start and end apart: 5, of which 5 were waited for; matrix products, arithmetic and copies ran while one was open for 0% of the time, Pallas kernels for 3%

profile of v5, /device:TPU:25, one launch (start us, length us, event | category | flops | bytes accessed | tf_op | source)
XLA Modules:
  0.0 93.1 jit_solution(1635292468839439382)
XLA Ops:
  0.6 1.9 %pack_kernel.1 = bf16[16,128,128]{2,1,0:T(8,128)(2,1)} custom-call(bf16[32,2048]{1,0:T(8,128)(2,1)} %q_hbm.1, bf16[32,2048]{1,0:T(8,128)(2,1)} %k_hbm.1, bf16[32,2048]{1,0:T(8,128)(2,1)} %v_hbm.1, bf16[32,2048]{1,0:T(8,128)(2,1)} %d_hbm.1), custom_call_target="tpu_custom_call" | custom-call | flops 500000000 | bytes 1048576 | tf_op jit(solution)/shard_map/pack_kernel/pallas_call | solution.py:384
  2.6 15.7 %all_to_all.10.own_ref = bf16[16,128,128]{2,1,0:T(8,128)(2,1)S(1)} all-to-all(bf16[16,128,128]{2,1,0:T(8,128)(2,1)} %pack_kernel.1), channel_id=1, replica_groups={{0,1,2,3,8,9,10,11,16,17,18,19,24,25,26,27},{32,33,34,35,40,41,42,43,48..., dimensions={0} | all-to-all | bytes 1048576 | tf_op jit(solution)/shard_map/all_to_all | solution.py:46
  18.3 0.0 copy-start.2
  18.3 11.8 %collective-permute-start = (bf16[16,64,128]{2,1,0:T(8,128)(2,1)S(1)}, bf16[16,64,128]{2,1,0:T(8,128)(2,1)S(1)}, u32[]{:S(2)}, u32[]{:S(2)}) collective-permute-start(bf16[16,64,128]{2,1,0:T(8,128)(2,1)S(1)} %split_kernel.1.kv_ref), channel_id=1, source_target_pairs={{0,32},{1,33},{2,34},{3,35},{8,40},{9,41},{10,42},{11,43},{16,48},... | collective-permute-start | bytes 786440 | tf_op jit(solution)/shard_map/ppermute | solution.py:38
  30.1 0.0 copy-done.2
  30.1 1.1 %down_kernel.1 = (bf16[17,64,128]{2,1,0:T(8,128)(2,1)S(1)}, s32[8,512]{1,0:T(8,128)S(1)}) custom-call(s32[32]{0:T(128)S(1)} %copy-done.2, bf16[16,128,128]{2,1,0:T(8,128)(2,1)S(1)} %all_to_all.10.own_ref, bf16[16,64,128]{2,1,0:T(8,128)(2,1)S(1)} %split_kernel.1.kv_ref), custom_call_target="tpu_custom_call" | custom-call | flops 1000000000 | bytes 1048576 | tf_op jit(solution)/shard_map/down_kernel/pallas_call | solution.py:384
  31.2 1.9 %collective-permute-start.1 = (bf16[17,64,128]{2,1,0:T(8,128)(2,1)S(1)}, bf16[17,64,128]{2,1,0:T(8,128)(2,1)S(1)}, u32[]{:S(2)}, u32[]{:S(2)}) collective-permute-start(bf16[17,64,128]{2,1,0:T(8,128)(2,1)S(1)} %get-tuple-element.14), channel_id=1, source_target_pairs={{32,0},{33,1},{34,2},{35,3},{40,8},{41,9},{42,10},{43,11},{48,16},... | collective-permute-start | bytes 835592 | tf_op jit(solution)/shard_map/ppermute | solution.py:42
  33.2 5.4 %collective-permute-done.before_ref = bf16[16,64,128]{2,1,0:T(8,128)(2,1)S(1)} collective-permute-done((bf16[16,64,128]{2,1,0:T(8,128)(2,1)S(1)}, bf16[16,64,128]{2,1,0:T(8,128)(2,1)S(1)}, u32[]{:S(2)}, u32[]{:S(2)}) %collective-permute-start) | collective-permute-done | bytes 262176 | tf_op jit(solution)/shard_map/ppermute | solution.py:38
  38.6 1.0 %own_stats_kernel.1.own_stats = f32[8,512]{1,0:T(8,128)S(1)} custom-call(s32[8,512]{1,0:T(8,128)S(1)} %get-tuple-element.13.info_ref, bf16[16,128,128]{2,1,0:T(8,128)(2,1)S(1)} %all_to_all.10.own_ref, bf16[16,64,128]{2,1,0:T(8,128)(2,1)S(1)} %collective-permute-done.before_ref), custom_call_target="tpu_custom_call" | custom-call | flops 1500000000 | bytes 1048576 | tf_op jit(solution)/shard_map/own_stats_kernel/pallas_call | solution.py:384
  39.6 11.9 %collective-permute-done.1.after_ref = bf16[17,64,128]{2,1,0:T(8,128)(2,1)S(1)} collective-permute-done((bf16[17,64,128]{2,1,0:T(8,128)(2,1)S(1)}, bf16[17,64,128]{2,1,0:T(8,128)(2,1)S(1)}, u32[]{:S(2)}, u32[]{:S(2)}) %collective-permute-start.1) | collective-permute-done | bytes 278560 | tf_op jit(solution)/shard_map/ppermute | solution.py:42
  51.5 0.2 after_stats_kernel.1.after_stats
  51.7 1.9 %collective-permute-start.2 = (f32[8,512]{1,0:T(8,128)S(1)}, f32[8,512]{1,0:T(8,128)S(1)}, u32[]{:S(2)}, u32[]{:S(2)}) collective-permute-start(f32[8,512]{1,0:T(8,128)S(1)} %after_stats_kernel.1.after_stats), channel_id=1, source_target_pairs={{0,32},{1,33},{2,34},{3,35},{8,40},{9,41},{10,42},{11,43},{16,48},... | collective-permute-start | bytes 49160 | tf_op jit(solution)/shard_map/ppermute | solution.py:38
  53.6 0.2 early_kernel.1
  53.8 3.4 %collective-permute-done.2.there_stats = f32[8,512]{1,0:T(8,128)S(1)} collective-permute-done((f32[8,512]{1,0:T(8,128)S(1)}, f32[8,512]{1,0:T(8,128)S(1)}, u32[]{:S(2)}, u32[]{:S(2)}) %collective-permute-start.2) | collective-permute-done | bytes 16416 | tf_op jit(solution)/shard_map/ppermute | solution.py:38
  57.3 3.4 %late_kernel.1 = (f32[16,96,128]{2,1,0:T(8,128)S(1)}, bf16[16,64,128]{2,1,0:T(8,128)(2,1)S(1)}, bf16[16,32,128]{2,1,0:T(8,128)(2,1)S(1)}) custom-call(s32[8,512]{1,0:T(8,128)S(1)} %get-tuple-element.13.info_ref, bf16[16,128,128]{2,1,0:T(8,128)(2,1)S(1)} %all_to_all.10.own_ref, bf16[16,64,128]{2,1,0:T(8,128)(2,1)S(1)} %collective-permute-done.before_ref, ...), custom_call_target="tpu_custom_call" | custom-call | flops 2000000000 | bytes 1048576 | tf_op jit(solution)/shard_map/late_kernel/pallas_call | solution.py:384
  60.6 2.9 %collective-permute-start.4 = (bf16[16,64,128]{2,1,0:T(8,128)(2,1)S(1)}, bf16[16,64,128]{2,1,0:T(8,128)(2,1)S(1)}, u32[]{:S(2)}, u32[]{:S(2)}) collective-permute-start(bf16[16,64,128]{2,1,0:T(8,128)(2,1)S(1)} %get-tuple-element.20), channel_id=1, source_target_pairs={{32,0},{33,1},{34,2},{35,3},{40,8},{41,9},{42,10},{43,11},{48,16},... | collective-permute-start | bytes 786440 | tf_op jit(solution)/shard_map/ppermute | solution.py:42
  63.5 6.9 %collective-permute-start.3 = (bf16[16,32,128]{2,1,0:T(8,128)(2,1)S(1)}, bf16[16,32,128]{2,1,0:T(8,128)(2,1)S(1)}, u32[]{:S(2)}, u32[]{:S(2)}) collective-permute-start(bf16[16,32,128]{2,1,0:T(8,128)(2,1)S(1)} %get-tuple-element.19), channel_id=1, source_target_pairs={{0,32},{1,33},{2,34},{3,35},{8,40},{9,41},{10,42},{11,43},{16,48},... | collective-permute-start | bytes 393224 | tf_op jit(solution)/shard_map/ppermute | solution.py:38
  70.4 3.1 %collective-permute-done.3.dq_ref = bf16[16,32,128]{2,1,0:T(8,128)(2,1)S(1)} collective-permute-done((bf16[16,32,128]{2,1,0:T(8,128)(2,1)S(1)}, bf16[16,32,128]{2,1,0:T(8,128)(2,1)S(1)}, u32[]{:S(2)}, u32[]{:S(2)}) %collective-permute-start.3) | collective-permute-done | bytes 131104 | tf_op jit(solution)/shard_map/ppermute | solution.py:38
  73.6 5.5 %collective-permute-done.4.dkv_ref = bf16[16,64,128]{2,1,0:T(8,128)(2,1)S(1)} collective-permute-done((bf16[16,64,128]{2,1,0:T(8,128)(2,1)S(1)}, bf16[16,64,128]{2,1,0:T(8,128)(2,1)S(1)}, u32[]{:S(2)}, u32[]{:S(2)}) %collective-permute-start.4) | collective-permute-done | bytes 262176 | tf_op jit(solution)/shard_map/ppermute | solution.py:42
  79.1 0.1 merge_kernel.1
  79.2 0.0 copy-start
  79.2 0.0 copy-start.1
  79.2 12.9 %all_to_all.11.back_ref = bf16[16,96,128]{2,1,0:T(8,128)(2,1)S(1)} all-to-all(bf16[16,96,128]{2,1,0:T(8,128)(2,1)S(1)} %merge_kernel.1), channel_id=1, replica_groups={{0,1,2,3,8,9,10,11,16,17,18,19,24,25,26,27},{32,33,34,35,40,41,42,43,48..., dimensions={0} | all-to-all | bytes 786432 | tf_op jit(solution)/shard_map/all_to_all | solution.py:46
  92.1 0.0 copy-done
  92.1 0.0 copy-done.1
  92.1 1.0 %finish_kernel.1 = (bf16[32,2048]{1,0:T(8,128)(2,1)}, bf16[32,2048]{1,0:T(8,128)(2,1)}, bf16[32,2048]{1,0:T(8,128)(2,1)}, f32[32,2048]{1,0:T(8,128)}, f32[32,2048]{1,0:T(8,128)}) custom-call(bf16[16,96,128]{2,1,0:T(8,128)(2,1)S(1)} %all_to_all.11.back_ref, f32[32,2048]{1,0:T(8,128)S(1)} %copy-done, f32[32,2048]{1,0:T(8,128)S(1)} %copy-done.1), custom_call_target="tpu_custom_call" | custom-call | flops 500000000 | bytes 1048576 | tf_op jit(solution)/shard_map/finish_kernel/pallas_call | solution.py:384
  (1 shorter events, 0.0 us)
Async XLA Ops:
  18.3 11.8 %copy-start.2 = (s32[32]{0:T(128)S(1)}, s32[32]{0:T(128)}, u32[]{:S(2)}) copy-start(s32[32]{0:T(128)} %lengths_ref.1) | copy-start | bytes 388
  18.3 20.3 %collective-permute-start = (bf16[16,64,128]{2,1,0:T(8,128)(2,1)S(1)}, bf16[16,64,128]{2,1,0:T(8,128)(2,1)S(1)}, u32[]{:S(2)}, u32[]{:S(2)}) collective-permute-start(bf16[16,64,128]{2,1,0:T(8,128)(2,1)S(1)} %split_kernel.1.kv_ref), channel_id=1, source_target_pairs={{0,32},{1,33},{2,34},{3,35},{8,40},{9,41},{10,42},{11,43},{16,48},... | collective-permute-start | bytes 786440 | tf_op jit(solution)/shard_map/ppermute | solution.py:38
  31.2 20.2 %collective-permute-start.1 = (bf16[17,64,128]{2,1,0:T(8,128)(2,1)S(1)}, bf16[17,64,128]{2,1,0:T(8,128)(2,1)S(1)}, u32[]{:S(2)}, u32[]{:S(2)}) collective-permute-start(bf16[17,64,128]{2,1,0:T(8,128)(2,1)S(1)} %get-tuple-element.14), channel_id=1, source_target_pairs={{32,0},{33,1},{34,2},{35,3},{40,8},{41,9},{42,10},{43,11},{48,16},... | collective-permute-start | bytes 835592 | tf_op jit(solution)/shard_map/ppermute | solution.py:42
  51.7 5.6 %collective-permute-start.2 = (f32[8,512]{1,0:T(8,128)S(1)}, f32[8,512]{1,0:T(8,128)S(1)}, u32[]{:S(2)}, u32[]{:S(2)}) collective-permute-start(f32[8,512]{1,0:T(8,128)S(1)} %after_stats_kernel.1.after_stats), channel_id=1, source_target_pairs={{0,32},{1,33},{2,34},{3,35},{8,40},{9,41},{10,42},{11,43},{16,48},... | collective-permute-start | bytes 49160 | tf_op jit(solution)/shard_map/ppermute | solution.py:38
  60.6 18.5 %collective-permute-start.4 = (bf16[16,64,128]{2,1,0:T(8,128)(2,1)S(1)}, bf16[16,64,128]{2,1,0:T(8,128)(2,1)S(1)}, u32[]{:S(2)}, u32[]{:S(2)}) collective-permute-start(bf16[16,64,128]{2,1,0:T(8,128)(2,1)S(1)} %get-tuple-element.20), channel_id=1, source_target_pairs={{32,0},{33,1},{34,2},{35,3},{40,8},{41,9},{42,10},{43,11},{48,16},... | collective-permute-start | bytes 786440 | tf_op jit(solution)/shard_map/ppermute | solution.py:42
  63.5 10.1 %collective-permute-start.3 = (bf16[16,32,128]{2,1,0:T(8,128)(2,1)S(1)}, bf16[16,32,128]{2,1,0:T(8,128)(2,1)S(1)}, u32[]{:S(2)}, u32[]{:S(2)}) collective-permute-start(bf16[16,32,128]{2,1,0:T(8,128)(2,1)S(1)} %get-tuple-element.19), channel_id=1, source_target_pairs={{0,32},{1,33},{2,34},{3,35},{8,40},{9,41},{10,42},{11,43},{16,48},... | collective-permute-start | bytes 393224 | tf_op jit(solution)/shard_map/ppermute | solution.py:38
  79.2 12.9 %copy-start = (f32[32,2048]{1,0:T(8,128)S(1)}, f32[32,2048]{1,0:T(8,128)}, u32[]{:S(2)}) copy-start(f32[32,2048]{1,0:T(8,128)} %key_prior_ref.1) | copy-start | bytes 786436
  79.2 12.9 %copy-start.1 = (f32[32,2048]{1,0:T(8,128)S(1)}, f32[32,2048]{1,0:T(8,128)}, u32[]{:S(2)}) copy-start(f32[32,2048]{1,0:T(8,128)} %value_prior_ref.1) | copy-start | bytes 786436

commit v6 on v5

--- a/solution.py
+++ b/solution.py
@@ -57,31 +57,22 @@
     return segment.astype(jnp.int32), slot.astype(jnp.int32)
 
 
-def rows_after(table, segment):
-    start = segment * SEG
-    count = jnp.int32(0)
-    for first, end in table:
-        count = jnp.maximum(count, jnp.where(first < start, end - start - SEG, 0))
-    return count
-
-
 def fill_info(lengths_ref, info_ref):
     segment, unused_slot = place()
-    table = []
-    first = jnp.int32(0)
-    for doc in range(NDOC):
-        end = first + lengths_ref[doc]
-        table.append((first, end))
-        first = end
+    base = segment * SEG
+    q_pos = base + lax.broadcasted_iota(jnp.int32, (1, 2 * SEG), 1)
+    lengths = jnp.broadcast_to(lengths_ref[...].reshape(1, NDOC), (NDOC, NDOC))
+    doc = lax.broadcasted_iota(jnp.int32, (NDOC, NDOC), 0)
+    other = lax.broadcasted_iota(jnp.int32, (NDOC, NDOC), 1)
+    starts = jnp.sum(jnp.where(other < doc, lengths, 0), axis=1, keepdims=True)
+    q_first = jnp.max(jnp.where(starts <= q_pos, starts, 0), axis=0, keepdims=True)
+    q_first = jnp.where(q_pos >= TOKENS, TOKENS, q_first) - base
     for part in range(2):
-        q_pos = (segment + part) * SEG + lax.broadcasted_iota(jnp.int32, (1, SEG), 1)
-        q_first = jnp.zeros((1, SEG), jnp.int32)
-        for first, unused_end in table:
-            q_first = jnp.where(q_pos >= first, first, q_first)
-        q_first = jnp.where(q_pos >= TOKENS, TOKENS, q_first)
-        info_ref[part : part + 1, :] = q_first - segment * SEG
-        count = rows_after(table, segment - part)
-        info_ref[2 + part : 3 + part, :] = jnp.full((1, SEG), count, jnp.int32)
+        firsts = q_first[:, part * SEG : (part + 1) * SEG]
+        info_ref[part : part + 1, :] = firsts
+        limit = -SEG if part == 0 else 0
+        reach = jnp.sum((firsts < limit).astype(jnp.int32), axis=1, keepdims=True)
+        info_ref[3 - part : 4 - part, :] = jnp.broadcast_to(reach, (1, SEG))
     info_ref[4:8, :] = jnp.zeros((4, SEG), jnp.int32)
 
 
@@ -90,7 +81,7 @@
 
 
 def tiles_of(qb):
-    return range(6) if qb == 0 else range(8) if qb == 1 else range(4)
+    return (range(6), range(8), range(4), range(2, 4))[qb]
 
 
 def own_tiles(qb):
@@ -150,6 +141,10 @@
 def split_kernel(own_ref, kv_ref):
     for i in range(16):
         kv_ref[i] = own_ref[i, 0 : 2 * ROWS, :]
+
+
+def all_keys(own_ref, before_ref, tiles, part):
+    return jnp.concatenate([key_tile(own_ref, before_ref, kb, part) for kb in tiles], axis=0)
 
 
 def block_stats(info_ref, qb, tiles, own_ref, before_ref, after_ref, s_buf):
@@ -209,7 +204,7 @@
     after_stats[...] = jnp.zeros((8, SEG), jnp.float32)
 
     def block(qb):
-        here = block_stats(info_ref, qb, range(8), own_ref, before_ref, after_ref, s_buf)
+        here = block_stats(info_ref, qb, range(2 * qb - 4, 8), own_ref, before_ref, after_ref, s_buf)
         there = []
         for number in range(3):
             halves = []
@@ -242,53 +237,71 @@
 
 
 def block_grads(
-    info_ref, qb, stats, own_ref, before_ref, after_ref, dk_acc, dv_acc, dq_acc
+    info_ref, qb, stats, own_ref, before_ref, after_ref, dk_acc, dv_acc, dq_acc, *bufs
 ):
     q_rows = query_block(own_ref, after_ref, qb, 0)
     d_rows = query_block(own_ref, after_ref, qb, 1)
+    s_buf, dp_buf, p_buf, ds_buf = bufs
     top, total, delta = stats
     delta = delta / total
     log_total = top * EXPONENT + jnp.log2(total)
-    dq = jnp.zeros((HD, QB), jnp.float32)
-    for kb in tiles_of(qb):
+    tiles = tiles_of(qb)
+    span = slice(tiles[0] * KB, (tiles[-1] + 1) * KB)
+    k_rows = all_keys(own_ref, before_ref, tiles, 0)
+    s_buf[span, :] = dot_t(k_rows, q_rows)
+    dp_buf[span, :] = dot_t(all_keys(own_ref, before_ref, tiles, 1), d_rows)
+    for kb in tiles:
         keys = slice(kb * KB, (kb + 1) * KB)
-        k_rows = key_tile(own_ref, before_ref, kb, 0)
-        power = dot_t(k_rows, q_rows) * EXPONENT - log_total
+        power = s_buf[keys, :] * EXPONENT - log_total
         probs = jnp.exp2(jnp.where(tile_allowed(info_ref, qb, kb), power, MASKED))
-        d_probs = dot_t(key_tile(own_ref, before_ref, kb, 1), d_rows)
-        d_scores = (probs * (d_probs - delta)).astype(jnp.bfloat16)
-        dv_acc[keys, :] = dv_acc[keys, :] + jnp.dot(
-            probs.astype(jnp.bfloat16), d_rows, preferred_element_type=jnp.float32
-        )
-        dk_acc[keys, :] = dk_acc[keys, :] + jnp.dot(
-            d_scores, q_rows, preferred_element_type=jnp.float32
-        )
-        dq = dq + lax.dot_general(
-            k_rows, d_scores, CONTRACT_FIRST, preferred_element_type=jnp.float32
-        )
+        p_buf[keys, :] = probs.astype(jnp.bfloat16)
+        ds_buf[keys, :] = (probs * (dp_buf[keys, :] - delta)).astype(jnp.bfloat16)
+    d_scores = ds_buf[span, :]
+    dv_acc[span, :] = dv_acc[span, :] + jnp.dot(
+        p_buf[span, :], d_rows, preferred_element_type=jnp.float32
+    )
+    dk_acc[span, :] = dk_acc[span, :] + jnp.dot(
+        d_scores, q_rows, preferred_element_type=jnp.float32
+    )
+    dq = lax.dot_general(k_rows, d_scores, CONTRACT_FIRST, preferred_element_type=jnp.float32)
     dq_acc[qb * QB : (qb + 1) * QB, :] = dq.T * SCALE
 
 
-def early_kernel(
-    info_ref, own_ref, before_ref, after_ref, own_stats, after_stats, dk_acc, dv_acc, dq_acc
-):
-    for acc in (dk_acc, dv_acc, dq_acc):
-        acc[...] = jnp.zeros((WIN, HD), jnp.float32)
+def own_block(info_ref, qb, stats, own_ref, before_ref, *refs):
+    block_grads(info_ref, qb, stats, own_ref, before_ref, None, *refs)
+
+
+def early_kernel(info_ref, own_ref, before_ref, own_stats, dk_acc, dv_acc, dq_acc, *bufs):
+    dk_acc[...] = jnp.zeros((WIN, HD), jnp.float32)
+    dv_acc[...] = jnp.zeros((WIN, HD), jnp.float32)
 
     def block(qb):
-        cols = slice((qb % 2) * QB, (qb % 2 + 1) * QB)
-        ref = own_stats if qb < 2 else after_stats
-        stats = [ref[n : n + 1, cols] for n in range(3)]
-        block_grads(
-            info_ref, qb, stats, own_ref, before_ref, after_ref, dk_acc, dv_acc, dq_acc
-        )
+        stats = [own_stats[n : n + 1, qb * QB : (qb + 1) * QB] for n in range(3)]
+        own_block(info_ref, qb, stats, own_ref, before_ref, dk_acc, dv_acc, dq_acc, *bufs)
 
     from_before = info_scalar(info_ref, 3)
-    count = info_scalar(info_ref, 2)
     pl.when(from_before <= QB)(lambda: block(1))
     pl.when(from_before <= 0)(lambda: block(0))
+
+
+def after_kernel(
+    info_ref, before_ref, after_ref, after_stats, dk_acc, dv_acc, dq_out, dq_acc, *bufs
+):
+    dk_acc[...] = jnp.zeros((SEG, HD), jnp.float32)
+    dv_acc[...] = jnp.zeros((SEG, HD), jnp.float32)
+    dq_acc[...] = jnp.zeros((WIN, HD), jnp.float32)
+
+    def block(qb):
+        stats = [after_stats[n : n + 1, (qb - 2) * QB : (qb - 1) * QB] for n in range(3)]
+        block_grads(
+            info_ref, qb, stats, None, before_ref, after_ref, dk_acc, dv_acc, dq_acc, *bufs
+        )
+
+    count = info_scalar(info_ref, 2)
     pl.when(count > 0)(lambda: block(2))
     pl.when(count > QB)(lambda: block(3))
+    for i in range(16):
+        dq_out[i] = dq_acc[SEG + i * ROWS : SEG + (i + 1) * ROWS, :].astype(jnp.bfloat16)
 
 
 def late_kernel(
@@ -300,15 +313,19 @@
     dk_in,
     dv_in,
     dq_in,
+    dk_after,
+    dv_after,
     own_out,
     before_out,
-    after_out,
     dk_acc,
     dv_acc,
     dq_acc,
+    *bufs,
 ):
-    dk_acc[...] = dk_in[...]
-    dv_acc[...] = dv_in[...]
+    dk_acc[0:SEG, :] = dk_in[0:SEG, :] + dk_after[...]
+    dv_acc[0:SEG, :] = dv_in[0:SEG, :] + dv_after[...]
+    dk_acc[SEG:WIN, :] = dk_in[SEG:WIN, :]
+    dv_acc[SEG:WIN, :] = dv_in[SEG:WIN, :]
     dq_acc[...] = dq_in[...]
 
     def block(qb):
@@ -319,7 +336,7 @@
             jnp.where(here, own_stats[n : n + 1, cols], there_stats[n : n + 1, cols])
             for n in range(3)
         ]
-        block_grads(info_ref, qb, stats, own_ref, before_ref, None, dk_acc, dv_acc, dq_acc)
+        own_block(info_ref, qb, stats, own_ref, before_ref, dk_acc, dv_acc, dq_acc, *bufs)
 
     from_before = info_scalar(info_ref, 3)
     pl.when(from_before > QB)(lambda: block(1))
@@ -332,7 +349,6 @@
         own_out[i, 2 * ROWS : 3 * ROWS, :] = dv_acc[high, :]
         before_out[i, 0:ROWS, :] = (dk_acc[low, :] * SCALE).astype(jnp.bfloat16)
         before_out[i, ROWS : 2 * ROWS, :] = dv_acc[low, :].astype(jnp.bfloat16)
-        after_out[i] = dq_acc[high, :].astype(jnp.bfloat16)
 
 
 def merge_kernel(own_ref, dq_ref, dkv_ref, chunk_ref):
@@ -410,12 +426,13 @@
     (kv,) = call(split_kernel, (own,), (half,), [VMEM])
     kv_before = to_after(kv)
     scores = pltpu.VMEM((WIN, QB), jnp.float32)
+    buffers = [scores] * 2 + [pltpu.VMEM((WIN, QB), jnp.bfloat16)] * 2
     coded = pltpu.VMEM((2 * ROWS, HD), jnp.float32)
     qd, info = call(
         down_kernel,
         (doc_lengths, own, kv),
         (bf16(17, 2 * ROWS, HD), jax.ShapeDtypeStruct((8, SEG), jnp.int32)),
-        [SMEM, VMEM, ANY],
+        [VMEM, VMEM, ANY],
         scratch=[scores, coded],
         gflop=1.0,
     )
@@ -439,27 +456,35 @@
     )
     there_stats = to_after(after_stats)
     acc = jax.ShapeDtypeStruct((WIN, HD), jnp.float32)
-    sums = call(
+    half_acc = jax.ShapeDtypeStruct((SEG, HD), jnp.float32)
+    early = call(
         early_kernel,
-        (info, own, kv_before, qd_after, own_stats, after_stats),
-        (acc,) * 3,
-        [VMEM] * 6,
+        (info, own, kv_before, own_stats),
+        (acc, acc, half_acc),
+        [VMEM] * 4,
+        scratch=buffers,
         gflop=2.5,
     )
-    own_grads, before_grads, after_grads = call(
+    dk_after, dv_after, dq_after = call(
+        after_kernel,
+        (info, kv_before, qd_after, after_stats),
+        (half_acc, half_acc, bf16(16, ROWS, HD)),
+        [VMEM] * 4,
+        scratch=[pltpu.VMEM((WIN, HD), jnp.float32)] + buffers,
+        gflop=1.0,
+    )
+    own_grads, before_grads = call(
         late_kernel,
-        (info, own, kv_before, own_stats, there_stats, *sums),
-        (
-            jax.ShapeDtypeStruct((16, 3 * ROWS, HD), jnp.float32),
-            half,
-            bf16(16, ROWS, HD),
-        ),
-        [VMEM] * 8,
-        scratch=[pltpu.VMEM((WIN, HD), jnp.float32)] * 3,
+        (info, own, kv_before, own_stats, there_stats, *early, dk_after, dv_after),
+        (jax.ShapeDtypeStruct((16, 3 * ROWS, HD), jnp.float32), half),
+        [VMEM] * 10,
+        scratch=[pltpu.VMEM((WIN, HD), jnp.float32)] * 2
+        + [pltpu.VMEM((SEG, HD), jnp.float32)]
+        + buffers,
         gflop=2.0,
     )
     dkv_there = to_before(before_grads)
-    dq_there = to_after(after_grads)
+    dq_there = to_after(dq_after)
     (merged,) = call(
         merge_kernel,
         (own_grads, dq_there, dkv_there),

time: 93.5 us -> 90.6 us (0.969)
  waiting for transfers between devices: 29.4 us -> 23.7 us
  blocking collectives: 28.6 us -> 32 us
    ppermute x2, waiting for transfers between devices: 17.4 us -> 9.49 us  [to_before(): return lax.ppermute(block, AXES, DOWN)]
    all_to_all x2, blocking collectives: 28.6 us -> 32 us  [exchange(): lax.all_to_all(chunks, AXES, split_axis=0, concat_axis=0, axis_index_grou...]
    ppermute x3, waiting for transfers between devices: 12 us -> 14.2 us  [to_after(): return lax.ppermute(block, AXES, UP)]
    ppermute x2, starting transfers between devices: 4.78 us -> 3.84 us  [to_before(): return lax.ppermute(block, AXES, DOWN)]
    ppermute x3, starting transfers between devices: 20.6 us -> 21.6 us  [to_after(): return lax.ppermute(block, AXES, UP)]
    pallas_call x9 -> x10, Pallas kernels: 8.95 us -> 8.3 us  [call(): pl.pallas_call(kernel, in_specs=specs, out_specs=[VMEM] * len(outputs), o...]
  transfers between devices with their start and end apart: 5 -> 5, of which waited for: 5 -> 4; matrix products, arithmetic and copies ran while one was open for 0% -> 0% of each run, Pallas kernels for 3% -> 5%
where the time goes in v6:
time: 90.6 us; the launch traced here: 90.2 us
  blocking collectives  32 us (35%)
  starting transfers between devices  25.4 us (28%)
  waiting for transfers between devices  23.7 us (26%)
  Pallas kernels  8.3 us (9%)
    all_to_all x2, blocking collectives, exchange(): lax.all_to_all(chunks, AXES, split_axis=0, concat_axis=0, axis_index_grou...  32 us
    ppermute x3, starting transfers between devices, to_after(): return lax.ppermute(block, AXES, UP)  21.6 us
    ppermute x3, waiting for transfers between devices, to_after(): return lax.ppermute(block, AXES, UP)  14.2 us
    ppermute x2, waiting for transfers between devices, to_before(): return lax.ppermute(block, AXES, DOWN)  9.49 us
    pallas_call x10, Pallas kernels, call(): pl.pallas_call(kernel, in_specs=specs, out_specs=[VMEM] * len(outputs), o...  8.3 us
    ppermute x2, starting transfers between devices, to_before(): return lax.ppermute(block, AXES, DOWN)  3.84 us
  transfers between devices with their start and end apart: 5, of which 4 were waited for; matrix products, arithmetic and copies ran while one was open for 0% of the time, Pallas kernels for 5%

profile of v6, /device:TPU:25, one launch (start us, length us, event | category | flops | bytes accessed | tf_op | source)
XLA Modules:
  0.0 90.2 jit_solution(11208610048136427938)
XLA Ops:
  0.6 1.9 %pack_kernel.1 = bf16[16,128,128]{2,1,0:T(8,128)(2,1)} custom-call(bf16[32,2048]{1,0:T(8,128)(2,1)} %q_hbm.1, bf16[32,2048]{1,0:T(8,128)(2,1)} %k_hbm.1, bf16[32,2048]{1,0:T(8,128)(2,1)} %v_hbm.1, bf16[32,2048]{1,0:T(8,128)(2,1)} %d_hbm.1), custom_call_target="tpu_custom_call" | custom-call | flops 500000000 | bytes 1048576 | tf_op jit(solution)/shard_map/pack_kernel/pallas_call | solution.py:400
  2.6 15.7 %all_to_all.10.own_ref = bf16[16,128,128]{2,1,0:T(8,128)(2,1)S(1)} all-to-all(bf16[16,128,128]{2,1,0:T(8,128)(2,1)} %pack_kernel.1), channel_id=1, replica_groups={{0,1,2,3,8,9,10,11,16,17,18,19,24,25,26,27},{32,33,34,35,40,41,42,43,48..., dimensions={0} | all-to-all | bytes 1048576 | tf_op jit(solution)/shard_map/all_to_all | solution.py:46
  18.3 0.0 copy-start.2
  18.3 11.8 %collective-permute-start = (bf16[16,64,128]{2,1,0:T(8,128)(2,1)S(1)}, bf16[16,64,128]{2,1,0:T(8,128)(2,1)S(1)}, u32[]{:S(2)}, u32[]{:S(2)}) collective-permute-start(bf16[16,64,128]{2,1,0:T(8,128)(2,1)S(1)} %split_kernel.1.kv_ref), channel_id=1, source_target_pairs={{0,32},{1,33},{2,34},{3,35},{8,40},{9,41},{10,42},{11,43},{16,48},... | collective-permute-start | bytes 786440 | tf_op jit(solution)/shard_map/ppermute | solution.py:38
  30.1 0.0 copy-done.2
  30.1 0.6 down_kernel.1
  30.6 1.9 %collective-permute-start.1 = (bf16[17,64,128]{2,1,0:T(8,128)(2,1)S(1)}, bf16[17,64,128]{2,1,0:T(8,128)(2,1)S(1)}, u32[]{:S(2)}, u32[]{:S(2)}) collective-permute-start(bf16[17,64,128]{2,1,0:T(8,128)(2,1)S(1)} %get-tuple-element.16), channel_id=1, source_target_pairs={{32,0},{33,1},{34,2},{35,3},{40,8},{41,9},{42,10},{43,11},{48,16},... | collective-permute-start | bytes 835592 | tf_op jit(solution)/shard_map/ppermute | solution.py:42
  32.6 6.0 %collective-permute-done.before_ref = bf16[16,64,128]{2,1,0:T(8,128)(2,1)S(1)} collective-permute-done((bf16[16,64,128]{2,1,0:T(8,128)(2,1)S(1)}, bf16[16,64,128]{2,1,0:T(8,128)(2,1)S(1)}, u32[]{:S(2)}, u32[]{:S(2)}) %collective-permute-start) | collective-permute-done | bytes 262176 | tf_op jit(solution)/shard_map/ppermute | solution.py:38
  38.6 1.0 %own_stats_kernel.1.own_stats = f32[8,512]{1,0:T(8,128)S(1)} custom-call(s32[8,512]{1,0:T(8,128)S(1)} %get-tuple-element.15.info_ref, bf16[16,128,128]{2,1,0:T(8,128)(2,1)S(1)} %all_to_all.10.own_ref, bf16[16,64,128]{2,1,0:T(8,128)(2,1)S(1)} %collective-permute-done.before_ref), custom_call_target="tpu_custom_call" | custom-call | flops 1500000000 | bytes 1048576 | tf_op jit(solution)/shard_map/own_stats_kernel/pallas_call | solution.py:400
  39.6 1.8 %early_kernel.1 = (f32[1024,128]{1,0:T(8,128)S(1)}, f32[1024,128]{1,0:T(8,128)S(1)}, f32[512,128]{1,0:T(8,128)S(1)}) custom-call(s32[8,512]{1,0:T(8,128)S(1)} %get-tuple-element.15.info_ref, bf16[16,128,128]{2,1,0:T(8,128)(2,1)S(1)} %all_to_all.10.own_ref, bf16[16,64,128]{2,1,0:T(8,128)(2,1)S(1)} %collective-permute-done.before_ref, ...), custom_call_target="tpu_custom_call" | custom-call | flops 2500000000 | bytes 1048576 | tf_op jit(solution)/shard_map/early_kernel/pallas_call | solution.py:400
  41.4 9.5 %collective-permute-done.1.after_ref = bf16[17,64,128]{2,1,0:T(8,128)(2,1)S(1)} collective-permute-done((bf16[17,64,128]{2,1,0:T(8,128)(2,1)S(1)}, bf16[17,64,128]{2,1,0:T(8,128)(2,1)S(1)}, u32[]{:S(2)}, u32[]{:S(2)}) %collective-permute-start.1) | collective-permute-done | bytes 278560 | tf_op jit(solution)/shard_map/ppermute | solution.py:42
  50.9 0.8 after_stats_kernel.1.after_stats
  51.7 1.9 %collective-permute-start.2 = (f32[8,512]{1,0:T(8,128)S(1)}, f32[8,512]{1,0:T(8,128)S(1)}, u32[]{:S(2)}, u32[]{:S(2)}) collective-permute-start(f32[8,512]{1,0:T(8,128)S(1)} %after_stats_kernel.1.after_stats), channel_id=1, source_target_pairs={{0,32},{1,33},{2,34},{3,35},{8,40},{9,41},{10,42},{11,43},{16,48},... | collective-permute-start | bytes 49160 | tf_op jit(solution)/shard_map/ppermute | solution.py:38
  53.7 0.8 after_kernel.1
  54.5 2.7 %collective-permute-done.2.there_stats = f32[8,512]{1,0:T(8,128)S(1)} collective-permute-done((f32[8,512]{1,0:T(8,128)S(1)}, f32[8,512]{1,0:T(8,128)S(1)}, u32[]{:S(2)}, u32[]{:S(2)}) %collective-permute-start.2) | collective-permute-done | bytes 16416 | tf_op jit(solution)/shard_map/ppermute | solution.py:38
  57.1 0.3 late_kernel.1
  57.4 1.9 %collective-permute-start.4 = (bf16[16,64,128]{2,1,0:T(8,128)(2,1)S(1)}, bf16[16,64,128]{2,1,0:T(8,128)(2,1)S(1)}, u32[]{:S(2)}, u32[]{:S(2)}) collective-permute-start(bf16[16,64,128]{2,1,0:T(8,128)(2,1)S(1)} %get-tuple-element.24), channel_id=1, source_target_pairs={{32,0},{33,1},{34,2},{35,3},{40,8},{41,9},{42,10},{43,11},{48,16},... | collective-permute-start | bytes 786440 | tf_op jit(solution)/shard_map/ppermute | solution.py:42
  59.3 7.9 %collective-permute-start.3 = (bf16[16,32,128]{2,1,0:T(8,128)(2,1)S(1)}, bf16[16,32,128]{2,1,0:T(8,128)(2,1)S(1)}, u32[]{:S(2)}, u32[]{:S(2)}) collective-permute-start(bf16[16,32,128]{2,1,0:T(8,128)(2,1)S(1)} %get-tuple-element.23), channel_id=1, source_target_pairs={{0,32},{1,33},{2,34},{3,35},{8,40},{9,41},{10,42},{11,43},{16,48},... | collective-permute-start | bytes 393224 | tf_op jit(solution)/shard_map/ppermute | solution.py:38
  67.2 5.5 %collective-permute-done.3.dq_ref = bf16[16,32,128]{2,1,0:T(8,128)(2,1)S(1)} collective-permute-done((bf16[16,32,128]{2,1,0:T(8,128)(2,1)S(1)}, bf16[16,32,128]{2,1,0:T(8,128)(2,1)S(1)}, u32[]{:S(2)}, u32[]{:S(2)}) %collective-permute-start.3) | collective-permute-done | bytes 131104 | tf_op jit(solution)/shard_map/ppermute | solution.py:38
  72.8 0.0 collective-permute-done.4.dkv_ref
  72.8 0.1 merge_kernel.1
  72.9 0.0 copy-start
  72.9 0.0 copy-start.1
  72.9 16.3 %all_to_all.11.back_ref = bf16[16,96,128]{2,1,0:T(8,128)(2,1)S(1)} all-to-all(bf16[16,96,128]{2,1,0:T(8,128)(2,1)S(1)} %merge_kernel.1), channel_id=1, replica_groups={{0,1,2,3,8,9,10,11,16,17,18,19,24,25,26,27},{32,33,34,35,40,41,42,43,48..., dimensions={0} | all-to-all | bytes 786432 | tf_op jit(solution)/shard_map/all_to_all | solution.py:46
  89.2 0.0 copy-done
  89.2 0.0 copy-done.1
  89.2 1.0 %finish_kernel.1 = (bf16[32,2048]{1,0:T(8,128)(2,1)}, bf16[32,2048]{1,0:T(8,128)(2,1)}, bf16[32,2048]{1,0:T(8,128)(2,1)}, f32[32,2048]{1,0:T(8,128)}, f32[32,2048]{1,0:T(8,128)}) custom-call(bf16[16,96,128]{2,1,0:T(8,128)(2,1)S(1)} %all_to_all.11.back_ref, f32[32,2048]{1,0:T(8,128)S(1)} %copy-done, f32[32,2048]{1,0:T(8,128)S(1)} %copy-done.1), custom_call_target="tpu_custom_call" | custom-call | flops 500000000 | bytes 1048576 | tf_op jit(solution)/shard_map/finish_kernel/pallas_call | solution.py:400
  (1 shorter events, 0.0 us)
Async XLA Ops:
  18.3 11.8 %copy-start.2 = (s32[32]{0:T(128)S(1)}, s32[32]{0:T(128)}, u32[]{:S(2)}) copy-start(s32[32]{0:T(128)} %lengths_ref.1) | copy-start | bytes 388
  18.3 20.3 %collective-permute-start = (bf16[16,64,128]{2,1,0:T(8,128)(2,1)S(1)}, bf16[16,64,128]{2,1,0:T(8,128)(2,1)S(1)}, u32[]{:S(2)}, u32[]{:S(2)}) collective-permute-start(bf16[16,64,128]{2,1,0:T(8,128)(2,1)S(1)} %split_kernel.1.kv_ref), channel_id=1, source_target_pairs={{0,32},{1,33},{2,34},{3,35},{8,40},{9,41},{10,42},{11,43},{16,48},... | collective-permute-start | bytes 786440 | tf_op jit(solution)/shard_map/ppermute | solution.py:38
  30.6 20.2 %collective-permute-start.1 = (bf16[17,64,128]{2,1,0:T(8,128)(2,1)S(1)}, bf16[17,64,128]{2,1,0:T(8,128)(2,1)S(1)}, u32[]{:S(2)}, u32[]{:S(2)}) collective-permute-start(bf16[17,64,128]{2,1,0:T(8,128)(2,1)S(1)} %get-tuple-element.16), channel_id=1, source_target_pairs={{32,0},{33,1},{34,2},{35,3},{40,8},{41,9},{42,10},{43,11},{48,16},... | collective-permute-start | bytes 835592 | tf_op jit(solution)/shard_map/ppermute | solution.py:42
  51.7 5.4 %collective-permute-start.2 = (f32[8,512]{1,0:T(8,128)S(1)}, f32[8,512]{1,0:T(8,128)S(1)}, u32[]{:S(2)}, u32[]{:S(2)}) collective-permute-start(f32[8,512]{1,0:T(8,128)S(1)} %after_stats_kernel.1.after_stats), channel_id=1, source_target_pairs={{0,32},{1,33},{2,34},{3,35},{8,40},{9,41},{10,42},{11,43},{16,48},... | collective-permute-start | bytes 49160 | tf_op jit(solution)/shard_map/ppermute | solution.py:38
  57.4 15.4 %collective-permute-start.4 = (bf16[16,64,128]{2,1,0:T(8,128)(2,1)S(1)}, bf16[16,64,128]{2,1,0:T(8,128)(2,1)S(1)}, u32[]{:S(2)}, u32[]{:S(2)}) collective-permute-start(bf16[16,64,128]{2,1,0:T(8,128)(2,1)S(1)} %get-tuple-element.24), channel_id=1, source_target_pairs={{32,0},{33,1},{34,2},{35,3},{40,8},{41,9},{42,10},{43,11},{48,16},... | collective-permute-start | bytes 786440 | tf_op jit(solution)/shard_map/ppermute | solution.py:42
  59.3 13.4 %collective-permute-start.3 = (bf16[16,32,128]{2,1,0:T(8,128)(2,1)S(1)}, bf16[16,32,128]{2,1,0:T(8,128)(2,1)S(1)}, u32[]{:S(2)}, u32[]{:S(2)}) collective-permute-start(bf16[16,32,128]{2,1,0:T(8,128)(2,1)S(1)} %get-tuple-element.23), channel_id=1, source_target_pairs={{0,32},{1,33},{2,34},{3,35},{8,40},{9,41},{10,42},{11,43},{16,48},... | collective-permute-start | bytes 393224 | tf_op jit(solution)/shard_map/ppermute | solution.py:38
  72.9 16.4 %copy-start = (f32[32,2048]{1,0:T(8,128)S(1)}, f32[32,2048]{1,0:T(8,128)}, u32[]{:S(2)}) copy-start(f32[32,2048]{1,0:T(8,128)} %key_prior_ref.1) | copy-start | bytes 786436
  72.9 16.4 %copy-start.1 = (f32[32,2048]{1,0:T(8,128)S(1)}, f32[32,2048]{1,0:T(8,128)}, u32[]{:S(2)}) copy-start(f32[32,2048]{1,0:T(8,128)} %value_prior_ref.1) | copy-start | bytes 786436

commit v7 on v6

--- a/solution.py
+++ b/solution.py
@@ -81,7 +81,7 @@
 
 
 def tiles_of(qb):
-    return (range(6), range(8), range(4), range(2, 4))[qb]
+    return (range(6), range(8), range(8), range(2, 8))[qb]
 
 
 def own_tiles(qb):
@@ -105,8 +105,11 @@
     return rows_of(after_ref, 8 * (qb - 2), 8, part)
 
 
-def tile_allowed(info_ref, qb, kb):
-    q_first = info_ref[qb // 2 : qb // 2 + 1, (qb % 2) * QB : (qb % 2 + 1) * QB]
+def row_firsts(info_ref, qb):
+    return info_ref[qb // 2 : qb // 2 + 1, (qb % 2) * QB : (qb % 2 + 1) * QB]
+
+
+def tile_allowed(q_first, qb, kb):
     k_pos = kb * KB - SEG + lax.broadcasted_iota(jnp.int32, (KB, QB), 0)
     allowed = k_pos >= q_first
     if kb >= 4 + 2 * qb:
@@ -148,13 +151,14 @@
 
 
 def block_stats(info_ref, qb, tiles, own_ref, before_ref, after_ref, s_buf):
+    q_first = row_firsts(info_ref, qb)
     q_rows = query_block(own_ref, after_ref, qb, 0)
     d_rows = query_block(own_ref, after_ref, qb, 1)
     top = jnp.full((8, QB), MASKED, jnp.float32)
     for kb in tiles:
         keys = slice(kb * KB, (kb + 1) * KB)
         k_rows = key_tile(own_ref, before_ref, kb, 0)
-        scores = jnp.where(tile_allowed(info_ref, qb, kb), dot_t(k_rows, q_rows), MASKED)
+        scores = jnp.where(tile_allowed(q_first, qb, kb), dot_t(k_rows, q_rows), MASKED)
         s_buf[keys, :] = scores
         top = jnp.maximum(top, jnp.max(scores.reshape(KB // 8, 8, QB), axis=0))
     top = jnp.max(top, axis=0, keepdims=True)
@@ -175,6 +179,29 @@
     return top, total, jnp.sum(delta, axis=0, keepdims=True) * total
 
 
+def encode(stats, half_block, coded):
+    for number, rest in enumerate(stats):
+        for piece in range(3):
+            rounded = rest.astype(jnp.bfloat16).astype(jnp.float32)
+            rest = rest - rounded
+            for half in range(2):
+                row = (number * 3 + piece) * 4 + 2 * half_block + half
+                coded[row : row + 1, :] = rounded[:, half * HD : (half + 1) * HD]
+
+
+def decode(half_block, coded):
+    stats = []
+    for number in range(3):
+        halves = []
+        for half in range(2):
+            row = number * 12 + 2 * half_block + half
+            halves.append(
+                coded[row : row + 1, :] + coded[row + 4 : row + 5, :] + coded[row + 8 : row + 9, :]
+            )
+        stats.append(jnp.concatenate(halves, axis=1))
+    return stats
+
+
 def down_kernel(lengths_ref, own_ref, kv_ref, qd_ref, info_ref, s_buf, coded):
     for i in range(16):
         qd_ref[i] = own_ref[i, 2 * ROWS : 4 * ROWS, :]
@@ -182,13 +209,7 @@
     coded[...] = jnp.zeros((2 * ROWS, HD), jnp.float32)
     for qb in range(2):
         stats = block_stats(info_ref, qb, own_tiles(qb), own_ref, None, None, s_buf)
-        for number, rest in enumerate(stats):
-            for piece in range(3):
-                rounded = rest.astype(jnp.bfloat16).astype(jnp.float32)
-                rest = rest - rounded
-                for half in range(2):
-                    row = (number * 3 + piece) * 4 + 2 * qb + half
-                    coded[row : row + 1, :] = rounded[:, half * HD : (half + 1) * HD]
+        encode(stats, qb, coded)
     qd_ref[16] = coded[...].astype(jnp.bfloat16)
 
 
@@ -200,44 +221,8 @@
     own_stats[3:8, :] = jnp.zeros((5, SEG), jnp.float32)
 
 
-def after_stats_kernel(info_ref, own_ref, before_ref, after_ref, after_stats, s_buf, coded):
-    after_stats[...] = jnp.zeros((8, SEG), jnp.float32)
-
-    def block(qb):
-        here = block_stats(info_ref, qb, range(2 * qb - 4, 8), own_ref, before_ref, after_ref, s_buf)
-        there = []
-        for number in range(3):
-            halves = []
-            for half in range(2):
-                row = number * 12 + 2 * (qb - 2) + half
-                halves.append(
-                    coded[row : row + 1, :]
-                    + coded[row + 4 : row + 5, :]
-                    + coded[row + 8 : row + 9, :]
-                )
-            there.append(jnp.concatenate(halves, axis=1))
-        top = jnp.maximum(here[0], there[0])
-        here_share = jnp.exp2((here[0] - top) * EXPONENT)
-        there_share = jnp.exp2((there[0] - top) * EXPONENT)
-        cols = slice((qb - 2) * QB, (qb - 1) * QB)
-        after_stats[0:1, cols] = top
-        for number in (1, 2):
-            after_stats[number : number + 1, cols] = (
-                here[number] * here_share + there[number] * there_share
-            )
-
-    count = info_scalar(info_ref, 2)
-
-    @pl.when(count > 0)
-    def first_block():
-        coded[...] = after_ref[16].astype(jnp.float32)
-        block(2)
-
-    pl.when(count > QB)(lambda: block(3))
-
-
 def block_grads(
-    info_ref, qb, stats, own_ref, before_ref, after_ref, dk_acc, dv_acc, dq_acc, *bufs
+    q_first, qb, tiles, stats, own_ref, before_ref, after_ref, dk_acc, dv_acc, dq_acc, bufs
 ):
     q_rows = query_block(own_ref, after_ref, qb, 0)
     d_rows = query_block(own_ref, after_ref, qb, 1)
@@ -245,7 +230,6 @@
     top, total, delta = stats
     delta = delta / total
     log_total = top * EXPONENT + jnp.log2(total)
-    tiles = tiles_of(qb)
     span = slice(tiles[0] * KB, (tiles[-1] + 1) * KB)
     k_rows = all_keys(own_ref, before_ref, tiles, 0)
     s_buf[span, :] = dot_t(k_rows, q_rows)
@@ -253,7 +237,7 @@
     for kb in tiles:
         keys = slice(kb * KB, (kb + 1) * KB)
         power = s_buf[keys, :] * EXPONENT - log_total
-        probs = jnp.exp2(jnp.where(tile_allowed(info_ref, qb, kb), power, MASKED))
+        probs = jnp.exp2(jnp.where(tile_allowed(q_first, qb, kb), power, MASKED))
         p_buf[keys, :] = probs.astype(jnp.bfloat16)
         ds_buf[keys, :] = (probs * (dp_buf[keys, :] - delta)).astype(jnp.bfloat16)
     d_scores = ds_buf[span, :]
@@ -264,99 +248,120 @@
         d_scores, q_rows, preferred_element_type=jnp.float32
     )
     dq = lax.dot_general(k_rows, d_scores, CONTRACT_FIRST, preferred_element_type=jnp.float32)
-    dq_acc[qb * QB : (qb + 1) * QB, :] = dq.T * SCALE
-
-
-def own_block(info_ref, qb, stats, own_ref, before_ref, *refs):
-    block_grads(info_ref, qb, stats, own_ref, before_ref, None, *refs)
+    rows = slice(qb * QB, (qb + 1) * QB)
+    dq_acc[rows, :] = dq_acc[rows, :] + dq.T * SCALE
 
 
 def early_kernel(info_ref, own_ref, before_ref, own_stats, dk_acc, dv_acc, dq_acc, *bufs):
     dk_acc[...] = jnp.zeros((WIN, HD), jnp.float32)
     dv_acc[...] = jnp.zeros((WIN, HD), jnp.float32)
+    dq_acc[...] = jnp.zeros((SEG, HD), jnp.float32)
+    for qb in (1, 0):
+        q_first = row_firsts(info_ref, qb)
+        q_first = jnp.where(q_first >= -SEG, q_first, WIN)
+        stats = [own_stats[n : n + 1, qb * QB : (qb + 1) * QB] for n in range(3)]
+        block_grads(
+            q_first, qb, tiles_of(qb), stats, own_ref, before_ref, None, dk_acc, dv_acc, dq_acc, bufs
+        )
+
+
+def after_kernel(
+    info_ref,
+    own_ref,
+    before_ref,
+    after_ref,
+    dk_in,
+    dv_in,
+    before_out,
+    after_out,
+    dk_out,
+    dv_out,
+    dk_acc,
+    dv_acc,
+    dq_acc,
+    coded,
+    *bufs,
+):
+    dk_acc[...] = dk_in[...]
+    dv_acc[...] = dv_in[...]
+    dq_acc[...] = jnp.zeros((WIN, HD), jnp.float32)
 
     def block(qb):
-        stats = [own_stats[n : n + 1, qb * QB : (qb + 1) * QB] for n in range(3)]
-        own_block(info_ref, qb, stats, own_ref, before_ref, dk_acc, dv_acc, dq_acc, *bufs)
-
-    from_before = info_scalar(info_ref, 3)
-    pl.when(from_before <= QB)(lambda: block(1))
-    pl.when(from_before <= 0)(lambda: block(0))
-
-
-def after_kernel(
-    info_ref, before_ref, after_ref, after_stats, dk_acc, dv_acc, dq_out, dq_acc, *bufs
-):
-    dk_acc[...] = jnp.zeros((SEG, HD), jnp.float32)
-    dv_acc[...] = jnp.zeros((SEG, HD), jnp.float32)
-    dq_acc[...] = jnp.zeros((WIN, HD), jnp.float32)
-
-    def block(qb):
-        stats = [after_stats[n : n + 1, (qb - 2) * QB : (qb - 1) * QB] for n in range(3)]
+        tiles = tiles_of(qb)
+        here = block_stats(info_ref, qb, tiles, own_ref, before_ref, after_ref, bufs[0])
+        there = decode(qb - 2, coded)
+        top = jnp.maximum(here[0], there[0])
+        here_share = jnp.exp2((here[0] - top) * EXPONENT)
+        there_share = jnp.exp2((there[0] - top) * EXPONENT)
+        stats = [top] + [here[n] * here_share + there[n] * there_share for n in (1, 2)]
+        encode(stats, qb - 2, coded)
+        q_first = row_firsts(info_ref, qb)
+        q_first = jnp.where(q_first < 0, q_first, WIN)
         block_grads(
-            info_ref, qb, stats, None, before_ref, after_ref, dk_acc, dv_acc, dq_acc, *bufs
+            q_first, qb, tiles, stats, own_ref, before_ref, after_ref, dk_acc, dv_acc, dq_acc, bufs
         )
 
+    coded[...] = after_ref[16].astype(jnp.float32)
     count = info_scalar(info_ref, 2)
     pl.when(count > 0)(lambda: block(2))
     pl.when(count > QB)(lambda: block(3))
     for i in range(16):
-        dq_out[i] = dq_acc[SEG + i * ROWS : SEG + (i + 1) * ROWS, :].astype(jnp.bfloat16)
+        low = slice(i * ROWS, (i + 1) * ROWS)
+        before_out[i, 0:ROWS, :] = (dk_acc[low, :] * SCALE).astype(jnp.bfloat16)
+        before_out[i, ROWS : 2 * ROWS, :] = dv_acc[low, :].astype(jnp.bfloat16)
+        after_out[i] = dq_acc[SEG + i * ROWS : SEG + (i + 1) * ROWS, :].astype(jnp.bfloat16)
+    for half in range(2):
+        after_out[16 + half] = coded[half * ROWS : (half + 1) * ROWS, :].astype(jnp.bfloat16)
+    dk_out[...] = dk_acc[SEG:WIN, :]
+    dv_out[...] = dv_acc[SEG:WIN, :]
 
 
 def late_kernel(
     info_ref,
     own_ref,
-    before_ref,
-    own_stats,
-    there_stats,
     dk_in,
     dv_in,
     dq_in,
-    dk_after,
-    dv_after,
-    own_out,
-    before_out,
+    dq_there,
+    dkv_there,
+    chunk_ref,
     dk_acc,
     dv_acc,
     dq_acc,
+    coded,
     *bufs,
 ):
-    dk_acc[0:SEG, :] = dk_in[0:SEG, :] + dk_after[...]
-    dv_acc[0:SEG, :] = dv_in[0:SEG, :] + dv_after[...]
-    dk_acc[SEG:WIN, :] = dk_in[SEG:WIN, :]
-    dv_acc[SEG:WIN, :] = dv_in[SEG:WIN, :]
+    dk_acc[SEG:WIN, :] = dk_in[...]
+    dv_acc[SEG:WIN, :] = dv_in[...]
     dq_acc[...] = dq_in[...]
+    for half in range(2):
+        coded[half * ROWS : (half + 1) * ROWS, :] = dq_there[16 + half].astype(jnp.float32)
 
     def block(qb):
-        cols = slice(qb * QB, (qb + 1) * QB)
-        row = qb * QB + lax.broadcasted_iota(jnp.int32, (1, QB), 1)
-        here = row >= info_ref[3:4, cols]
-        stats = [
-            jnp.where(here, own_stats[n : n + 1, cols], there_stats[n : n + 1, cols])
-            for n in range(3)
-        ]
-        own_block(info_ref, qb, stats, own_ref, before_ref, dk_acc, dv_acc, dq_acc, *bufs)
+        q_first = row_firsts(info_ref, qb)
+        chosen = q_first < -SEG
+        top, total, delta = decode(qb, coded)
+        stats = (
+            jnp.where(chosen, top, 0.0),
+            jnp.where(chosen, total, 1.0),
+            jnp.where(chosen, delta, 0.0),
+        )
+        q_first = jnp.where(chosen, q_first, WIN)
+        block_grads(
+            q_first, qb, own_tiles(qb), stats, own_ref, None, None, dk_acc, dv_acc, dq_acc, bufs
+        )
 
     from_before = info_scalar(info_ref, 3)
+    pl.when(from_before > 0)(lambda: block(0))
     pl.when(from_before > QB)(lambda: block(1))
-    pl.when(from_before > 0)(lambda: block(0))
     for i in range(16):
         low = slice(i * ROWS, (i + 1) * ROWS)
         high = slice(SEG + i * ROWS, SEG + (i + 1) * ROWS)
-        own_out[i, 0:ROWS, :] = dq_acc[low, :]
-        own_out[i, ROWS : 2 * ROWS, :] = dk_acc[high, :] * SCALE
-        own_out[i, 2 * ROWS : 3 * ROWS, :] = dv_acc[high, :]
-        before_out[i, 0:ROWS, :] = (dk_acc[low, :] * SCALE).astype(jnp.bfloat16)
-        before_out[i, ROWS : 2 * ROWS, :] = dv_acc[low, :].astype(jnp.bfloat16)
-
-
-def merge_kernel(own_ref, dq_ref, dkv_ref, chunk_ref):
-    for i in range(16):
-        dq = own_ref[i, 0:ROWS, :] + dq_ref[i].astype(jnp.float32)
-        dkv = own_ref[i, ROWS : 3 * ROWS, :] + dkv_ref[i].astype(jnp.float32)
-        chunk_ref[i, 0:ROWS, :] = dq.astype(jnp.bfloat16)
-        chunk_ref[i, ROWS : 3 * ROWS, :] = dkv.astype(jnp.bfloat16)
+        dq = dq_acc[low, :] + dq_there[i].astype(jnp.float32)
+        dk = dk_acc[high, :] * SCALE + dkv_there[i, 0:ROWS, :].astype(jnp.float32)
+        dv = dv_acc[high, :] + dkv_there[i, ROWS : 2 * ROWS, :].astype(jnp.float32)
+        for part, rows in enumerate((dq, dk, dv)):
+            chunk_ref[i, part * ROWS : (part + 1) * ROWS, :] = rows.astype(jnp.bfloat16)
 
 
 def finish_kernel(
@@ -446,50 +451,33 @@
         scratch=[scores],
         gflop=1.5,
     )
-    (after_stats,) = call(
-        after_stats_kernel,
-        (info, own, kv_before, qd_after),
-        (stats,),
-        [VMEM] * 4,
-        scratch=[scores, coded],
-        gflop=1.0,
-    )
-    there_stats = to_after(after_stats)
     acc = jax.ShapeDtypeStruct((WIN, HD), jnp.float32)
     half_acc = jax.ShapeDtypeStruct((SEG, HD), jnp.float32)
-    early = call(
+    sums = pltpu.VMEM((WIN, HD), jnp.float32)
+    dk_early, dv_early, dq_early = call(
         early_kernel,
         (info, own, kv_before, own_stats),
         (acc, acc, half_acc),
         [VMEM] * 4,
         scratch=buffers,
-        gflop=2.5,
-    )
-    dk_after, dv_after, dq_after = call(
+        gflop=2.0,
+    )
+    before_grads, after_grads, dk_own, dv_own = call(
         after_kernel,
-        (info, kv_before, qd_after, after_stats),
-        (half_acc, half_acc, bf16(16, ROWS, HD)),
-        [VMEM] * 4,
-        scratch=[pltpu.VMEM((WIN, HD), jnp.float32)] + buffers,
+        (info, own, kv_before, qd_after, dk_early, dv_early),
+        (half, bf16(18, ROWS, HD), half_acc, half_acc),
+        [VMEM] * 6,
+        scratch=[sums, sums, sums, coded] + buffers,
         gflop=1.0,
     )
-    own_grads, before_grads = call(
+    dkv_there = to_before(before_grads)
+    dq_there = to_after(after_grads)
+    (merged,) = call(
         late_kernel,
-        (info, own, kv_before, own_stats, there_stats, *early, dk_after, dv_after),
-        (jax.ShapeDtypeStruct((16, 3 * ROWS, HD), jnp.float32), half),
-        [VMEM] * 10,
-        scratch=[pltpu.VMEM((WIN, HD), jnp.float32)] * 2
-        + [pltpu.VMEM((SEG, HD), jnp.float32)]
-        + buffers,
-        gflop=2.0,
-    )
-    dkv_there = to_before(before_grads)
-    dq_there = to_after(dq_after)
-    (merged,) = call(
-        merge_kernel,
-        (own_grads, dq_there, dkv_there),
+        (info, own, dk_own, dv_own, dq_early, dq_there, dkv_there),
         (bf16(16, 3 * ROWS, HD),),
-        [VMEM] * 3,
+        [VMEM] * 7,
+        scratch=[sums, sums, pltpu.VMEM((SEG, HD), jnp.float32), coded] + buffers,
     )
     back = exchange(merged)
     wide = jax.ShapeDtypeStruct((ROWS, width), jnp.float32)

time: 90.6 us -> 85.5 us (0.944)
  waiting for transfers between devices: 23.7 us -> 19.2 us
  blocking collectives: 32 us -> 34.2 us
  starting transfers between devices: 25.4 us -> 23.5 us
    ppermute x3 -> x2, waiting for transfers between devices: 14.2 us -> 9.21 us  [to_after(): return lax.ppermute(block, AXES, UP)]
    all_to_all x2, blocking collectives: 32 us -> 34.2 us  [exchange(): lax.all_to_all(chunks, AXES, split_axis=0, concat_axis=0, axis_index_grou...]
    ppermute x3 -> x2, starting transfers between devices: 21.6 us -> 19.7 us  [to_after(): return lax.ppermute(block, AXES, UP)]
    pallas_call x10 -> x8, Pallas kernels: 8.3 us -> 7.51 us  [call(): pl.pallas_call(kernel, in_specs=specs, out_specs=[VMEM] * len(outputs), o...]
  transfers between devices with their start and end apart: 5 -> 4, of which waited for: 4 -> 4; matrix products, arithmetic and copies ran while one was open for 0% -> 0% of each run, Pallas kernels for 5% -> 3%
where the time goes in v7:
time: 85.5 us; the launch traced here: 85.2 us
  blocking collectives  34.2 us (40%)
  starting transfers between devices  23.5 us (27%)
  waiting for transfers between devices  19.2 us (22%)
  Pallas kernels  7.51 us (9%)
    all_to_all x2, blocking collectives, exchange(): lax.all_to_all(chunks, AXES, split_axis=0, concat_axis=0, axis_index_grou...  34.2 us
    ppermute x2, starting transfers between devices, to_after(): return lax.ppermute(block, AXES, UP)  19.7 us
    ppermute x2, waiting for transfers between devices, to_before(): return lax.ppermute(block, AXES, DOWN)  9.99 us
    ppermute x2, waiting for transfers between devices, to_after(): return lax.ppermute(block, AXES, UP)  9.21 us
    pallas_call x8, Pallas kernels, call(): pl.pallas_call(kernel, in_specs=specs, out_specs=[VMEM] * len(outputs), o...  7.51 us
    ppermute x2, starting transfers between devices, to_before(): return lax.ppermute(block, AXES, DOWN)  3.84 us
  transfers between devices with their start and end apart: 4, of which 4 were waited for; matrix products, arithmetic and copies ran while one was open for 0% of the time, Pallas kernels for 3%

profile of v7, /device:TPU:25, one launch (start us, length us, event | category | flops | bytes accessed | tf_op | source)
XLA Modules:
  0.0 85.2 jit_solution(12818161772226214679)
XLA Ops:
  0.6 1.9 %pack_kernel.1 = bf16[16,128,128]{2,1,0:T(8,128)(2,1)} custom-call(bf16[32,2048]{1,0:T(8,128)(2,1)} %q_hbm.1, bf16[32,2048]{1,0:T(8,128)(2,1)} %k_hbm.1, bf16[32,2048]{1,0:T(8,128)(2,1)} %v_hbm.1, bf16[32,2048]{1,0:T(8,128)(2,1)} %d_hbm.1), custom_call_target="tpu_custom_call" | custom-call | flops 500000000 | bytes 1048576 | tf_op jit(solution)/shard_map/pack_kernel/pallas_call | solution.py:405
  2.6 15.7 %all_to_all.10.own_ref = bf16[16,128,128]{2,1,0:T(8,128)(2,1)S(1)} all-to-all(bf16[16,128,128]{2,1,0:T(8,128)(2,1)} %pack_kernel.1), channel_id=1, replica_groups={{0,1,2,3,8,9,10,11,16,17,18,19,24,25,26,27},{32,33,34,35,40,41,42,43,48..., dimensions={0} | all-to-all | bytes 1048576 | tf_op jit(solution)/shard_map/all_to_all | solution.py:46
  18.3 0.0 copy-start.2
  18.3 11.8 %collective-permute-start = (bf16[16,64,128]{2,1,0:T(8,128)(2,1)S(1)}, bf16[16,64,128]{2,1,0:T(8,128)(2,1)S(1)}, u32[]{:S(2)}, u32[]{:S(2)}) collective-permute-start(bf16[16,64,128]{2,1,0:T(8,128)(2,1)S(1)} %split_kernel.1.kv_ref), channel_id=1, source_target_pairs={{0,32},{1,33},{2,34},{3,35},{8,40},{9,41},{10,42},{11,43},{16,48},... | collective-permute-start | bytes 786440 | tf_op jit(solution)/shard_map/ppermute | solution.py:38
  30.1 0.0 copy-done.2
  30.1 0.6 down_kernel.1
  30.7 1.9 %collective-permute-start.1 = (bf16[17,64,128]{2,1,0:T(8,128)(2,1)S(1)}, bf16[17,64,128]{2,1,0:T(8,128)(2,1)S(1)}, u32[]{:S(2)}, u32[]{:S(2)}) collective-permute-start(bf16[17,64,128]{2,1,0:T(8,128)(2,1)S(1)} %get-tuple-element.15), channel_id=1, source_target_pairs={{32,0},{33,1},{34,2},{35,3},{40,8},{41,9},{42,10},{43,11},{48,16},... | collective-permute-start | bytes 835592 | tf_op jit(solution)/shard_map/ppermute | solution.py:42
  32.6 6.0 %collective-permute-done.before_ref = bf16[16,64,128]{2,1,0:T(8,128)(2,1)S(1)} collective-permute-done((bf16[16,64,128]{2,1,0:T(8,128)(2,1)S(1)}, bf16[16,64,128]{2,1,0:T(8,128)(2,1)S(1)}, u32[]{:S(2)}, u32[]{:S(2)}) %collective-permute-start) | collective-permute-done | bytes 262176 | tf_op jit(solution)/shard_map/ppermute | solution.py:38
  38.6 1.0 %own_stats_kernel.1.own_stats = f32[8,512]{1,0:T(8,128)S(1)} custom-call(s32[8,512]{1,0:T(8,128)S(1)} %get-tuple-element.14.info_ref, bf16[16,128,128]{2,1,0:T(8,128)(2,1)S(1)} %all_to_all.10.own_ref, bf16[16,64,128]{2,1,0:T(8,128)(2,1)S(1)} %collective-permute-done.before_ref), custom_call_target="tpu_custom_call" | custom-call | flops 1500000000 | bytes 1048576 | tf_op jit(solution)/shard_map/own_stats_kernel/pallas_call | solution.py:405
  39.6 1.4 %early_kernel.1 = (f32[1024,128]{1,0:T(8,128)S(1)}, f32[1024,128]{1,0:T(8,128)S(1)}, f32[512,128]{1,0:T(8,128)S(1)}) custom-call(s32[8,512]{1,0:T(8,128)S(1)} %get-tuple-element.14.info_ref, bf16[16,128,128]{2,1,0:T(8,128)(2,1)S(1)} %all_to_all.10.own_ref, bf16[16,64,128]{2,1,0:T(8,128)(2,1)S(1)} %collective-permute-done.before_ref, ...), custom_call_target="tpu_custom_call" | custom-call | flops 2000000000 | bytes 1048576 | tf_op jit(solution)/shard_map/early_kernel/pallas_call | solution.py:405
  41.0 9.9 %collective-permute-done.1.after_ref = bf16[17,64,128]{2,1,0:T(8,128)(2,1)S(1)} collective-permute-done((bf16[17,64,128]{2,1,0:T(8,128)(2,1)S(1)}, bf16[17,64,128]{2,1,0:T(8,128)(2,1)S(1)}, u32[]{:S(2)}, u32[]{:S(2)}) %collective-permute-start.1) | collective-permute-done | bytes 278560 | tf_op jit(solution)/shard_map/ppermute | solution.py:42
  50.9 0.3 after_kernel.1
  51.2 1.9 %collective-permute-start.3 = (bf16[16,64,128]{2,1,0:T(8,128)(2,1)S(1)}, bf16[16,64,128]{2,1,0:T(8,128)(2,1)S(1)}, u32[]{:S(2)}, u32[]{:S(2)}) collective-permute-start(bf16[16,64,128]{2,1,0:T(8,128)(2,1)S(1)} %get-tuple-element.22), channel_id=1, source_target_pairs={{32,0},{33,1},{34,2},{35,3},{40,8},{41,9},{42,10},{43,11},{48,16},... | collective-permute-start | bytes 786440 | tf_op jit(solution)/shard_map/ppermute | solution.py:42
  53.1 7.9 %collective-permute-start.2 = (bf16[18,32,128]{2,1,0:T(8,128)(2,1)S(1)}, bf16[18,32,128]{2,1,0:T(8,128)(2,1)S(1)}, u32[]{:S(2)}, u32[]{:S(2)}) collective-permute-start(bf16[18,32,128]{2,1,0:T(8,128)(2,1)S(1)} %get-tuple-element.21), channel_id=1, source_target_pairs={{0,32},{1,33},{2,34},{3,35},{8,40},{9,41},{10,42},{11,43},{16,48},... | collective-permute-start | bytes 442376 | tf_op jit(solution)/shard_map/ppermute | solution.py:38
  61.0 3.2 %collective-permute-done.2.dq_there = bf16[18,32,128]{2,1,0:T(8,128)(2,1)S(1)} collective-permute-done((bf16[18,32,128]{2,1,0:T(8,128)(2,1)S(1)}, bf16[18,32,128]{2,1,0:T(8,128)(2,1)S(1)}, u32[]{:S(2)}, u32[]{:S(2)}) %collective-permute-start.2) | collective-permute-done | bytes 147488 | tf_op jit(solution)/shard_map/ppermute | solution.py:38
  64.2 0.1 collective-permute-done.3.dkv_there
  64.3 1.3 %late_kernel.1 = bf16[16,96,128]{2,1,0:T(8,128)(2,1)S(1)} custom-call(s32[8,512]{1,0:T(8,128)S(1)} %get-tuple-element.14.info_ref, bf16[16,128,128]{2,1,0:T(8,128)(2,1)S(1)} %all_to_all.10.own_ref, f32[512,128]{1,0:T(8,128)S(1)} %get-tuple-element.18.dk_in, f32[512,128]{1,0:T(8,128)S(1)} %get-tuple-element.19.dv_in, f32[512,128]{1,0:T(8,128)S(1)} %get-tuple-element.20.dq_in, ...), custom_call_target="tpu_custom_call" | custom-call | flops 500000000 | bytes 1048576 | tf_op jit(solution)/shard_map/late_kernel/pallas_call | solution.py:405
  65.6 0.0 copy-start
  65.6 0.0 copy-start.1
  65.6 18.5 %all_to_all.11.back_ref = bf16[16,96,128]{2,1,0:T(8,128)(2,1)S(1)} all-to-all(bf16[16,96,128]{2,1,0:T(8,128)(2,1)S(1)} %late_kernel.1), channel_id=1, replica_groups={{0,1,2,3,8,9,10,11,16,17,18,19,24,25,26,27},{32,33,34,35,40,41,42,43,48..., dimensions={0} | all-to-all | bytes 786432 | tf_op jit(solution)/shard_map/all_to_all | solution.py:46
  84.2 0.0 copy-done
  84.2 0.0 copy-done.1
  84.2 1.0 %finish_kernel.1 = (bf16[32,2048]{1,0:T(8,128)(2,1)}, bf16[32,2048]{1,0:T(8,128)(2,1)}, bf16[32,2048]{1,0:T(8,128)(2,1)}, f32[32,2048]{1,0:T(8,128)}, f32[32,2048]{1,0:T(8,128)}) custom-call(bf16[16,96,128]{2,1,0:T(8,128)(2,1)S(1)} %all_to_all.11.back_ref, f32[32,2048]{1,0:T(8,128)S(1)} %copy-done, f32[32,2048]{1,0:T(8,128)S(1)} %copy-done.1), custom_call_target="tpu_custom_call" | custom-call | flops 500000000 | bytes 1048576 | tf_op jit(solution)/shard_map/finish_kernel/pallas_call | solution.py:405
  (1 shorter events, 0.0 us)
Async XLA Ops:
  18.3 11.8 %copy-start.2 = (s32[32]{0:T(128)S(1)}, s32[32]{0:T(128)}, u32[]{:S(2)}) copy-start(s32[32]{0:T(128)} %lengths_ref.1) | copy-start | bytes 388
  18.3 20.3 %collective-permute-start = (bf16[16,64,128]{2,1,0:T(8,128)(2,1)S(1)}, bf16[16,64,128]{2,1,0:T(8,128)(2,1)S(1)}, u32[]{:S(2)}, u32[]{:S(2)}) collective-permute-start(bf16[16,64,128]{2,1,0:T(8,128)(2,1)S(1)} %split_kernel.1.kv_ref), channel_id=1, source_target_pairs={{0,32},{1,33},{2,34},{3,35},{8,40},{9,41},{10,42},{11,43},{16,48},... | collective-permute-start | bytes 786440 | tf_op jit(solution)/shard_map/ppermute | solution.py:38
  30.7 20.2 %collective-permute-start.1 = (bf16[17,64,128]{2,1,0:T(8,128)(2,1)S(1)}, bf16[17,64,128]{2,1,0:T(8,128)(2,1)S(1)}, u32[]{:S(2)}, u32[]{:S(2)}) collective-permute-start(bf16[17,64,128]{2,1,0:T(8,128)(2,1)S(1)} %get-tuple-element.15), channel_id=1, source_target_pairs={{32,0},{33,1},{34,2},{35,3},{40,8},{41,9},{42,10},{43,11},{48,16},... | collective-permute-start | bytes 835592 | tf_op jit(solution)/shard_map/ppermute | solution.py:42
  51.2 13.1 %collective-permute-start.3 = (bf16[16,64,128]{2,1,0:T(8,128)(2,1)S(1)}, bf16[16,64,128]{2,1,0:T(8,128)(2,1)S(1)}, u32[]{:S(2)}, u32[]{:S(2)}) collective-permute-start(bf16[16,64,128]{2,1,0:T(8,128)(2,1)S(1)} %get-tuple-element.22), channel_id=1, source_target_pairs={{32,0},{33,1},{34,2},{35,3},{40,8},{41,9},{42,10},{43,11},{48,16},... | collective-permute-start | bytes 786440 | tf_op jit(solution)/shard_map/ppermute | solution.py:42
  53.1 11.1 %collective-permute-start.2 = (bf16[18,32,128]{2,1,0:T(8,128)(2,1)S(1)}, bf16[18,32,128]{2,1,0:T(8,128)(2,1)S(1)}, u32[]{:S(2)}, u32[]{:S(2)}) collective-permute-start(bf16[18,32,128]{2,1,0:T(8,128)(2,1)S(1)} %get-tuple-element.21), channel_id=1, source_target_pairs={{0,32},{1,33},{2,34},{3,35},{8,40},{9,41},{10,42},{11,43},{16,48},... | collective-permute-start | bytes 442376 | tf_op jit(solution)/shard_map/ppermute | solution.py:38
  65.6 18.6 %copy-start = (f32[32,2048]{1,0:T(8,128)S(1)}, f32[32,2048]{1,0:T(8,128)}, u32[]{:S(2)}) copy-start(f32[32,2048]{1,0:T(8,128)} %key_prior_ref.1) | copy-start | bytes 786436
  65.6 18.6 %copy-start.1 = (f32[32,2048]{1,0:T(8,128)S(1)}, f32[32,2048]{1,0:T(8,128)}, u32[]{:S(2)}) copy-start(f32[32,2048]{1,0:T(8,128)} %value_prior_ref.1) | copy-start | bytes 786436

commit v8 on v7

--- a/solution.py
+++ b/solution.py
@@ -31,15 +31,15 @@
 
 GROUPS = [[device_of(s, i) for i in range(16)] for s in range(SEGS)]
 UP = [(device_of(s, i), device_of(s + 1, i)) for s in range(SEGS - 1) for i in range(16)]
+EARLY = [(device_of(24, i), device_of(23, i)) for i in range(16)]
+LATE = [(device_of(8, i), device_of(7, i)) for i in range(16)]
 DOWN = [(target, source) for source, target in UP]
+DOWN_REST = [pair for pair in DOWN if pair not in EARLY]
+DOWN_FIRST = [pair for pair in DOWN if pair not in LATE]
 
 
 def to_after(block):
     return lax.ppermute(block, AXES, UP)
-
-
-def to_before(block):
-    return lax.ppermute(block, AXES, DOWN)
 
 
 def exchange(chunks):
@@ -141,7 +141,17 @@
             ]
 
 
-def split_kernel(own_ref, kv_ref):
+def halves_kernel(pair_ref, first_ref, second_ref):
+    for i in range(16):
+        first_ref[i] = pair_ref[i, 0:ROWS, :]
+        second_ref[i] = pair_ref[i, ROWS : 2 * ROWS, :]
+
+
+def again_kernel(qd_ref, kv_ref, again_ref):
+    again_ref[...] = qd_ref[...]
+
+
+def split_kernel(own_ref, qd_ref, kv_ref):
     for i in range(16):
         kv_ref[i] = own_ref[i, 0 : 2 * ROWS, :]
 
@@ -202,7 +212,7 @@
     return stats
 
 
-def down_kernel(lengths_ref, own_ref, kv_ref, qd_ref, info_ref, s_buf, coded):
+def down_kernel(lengths_ref, own_ref, qd_ref, info_ref, s_buf, coded):
     for i in range(16):
         qd_ref[i] = own_ref[i, 2 * ROWS : 4 * ROWS, :]
     fill_info(lengths_ref, info_ref)
@@ -213,7 +223,7 @@
     qd_ref[16] = coded[...].astype(jnp.bfloat16)
 
 
-def own_stats_kernel(info_ref, own_ref, before_ref, own_stats, s_buf):
+def own_stats_kernel(info_ref, own_ref, before_ref, early_ref, own_stats, s_buf):
     for qb in (1, 0):
         stats = block_stats(info_ref, qb, tiles_of(qb), own_ref, before_ref, None, s_buf)
         for number in range(3):
@@ -269,7 +279,8 @@
     info_ref,
     own_ref,
     before_ref,
-    after_ref,
+    rest_ref,
+    early_ref,
     dk_in,
     dv_in,
     before_out,
@@ -280,6 +291,7 @@
     dv_acc,
     dq_acc,
     coded,
+    after_ref,
     *bufs,
 ):
     dk_acc[...] = dk_in[...]
@@ -301,6 +313,16 @@
             q_first, qb, tiles, stats, own_ref, before_ref, after_ref, dk_acc, dv_acc, dq_acc, bufs
         )
 
+    segment, unused_slot = place()
+
+    @pl.when(segment == 23)
+    def from_early():
+        after_ref[...] = early_ref[...]
+
+    @pl.when(segment != 23)
+    def from_rest():
+        after_ref[...] = rest_ref[...]
+
     coded[...] = after_ref[16].astype(jnp.float32)
     count = info_scalar(info_ref, 2)
     pl.when(count > 0)(lambda: block(2))
@@ -323,7 +345,9 @@
     dv_in,
     dq_in,
     dq_there,
-    dkv_there,
+    dkv_first,
+    dk_late,
+    dv_late,
     chunk_ref,
     dk_acc,
     dv_acc,
@@ -354,14 +378,25 @@
     from_before = info_scalar(info_ref, 3)
     pl.when(from_before > 0)(lambda: block(0))
     pl.when(from_before > QB)(lambda: block(1))
-    for i in range(16):
-        low = slice(i * ROWS, (i + 1) * ROWS)
-        high = slice(SEG + i * ROWS, SEG + (i + 1) * ROWS)
-        dq = dq_acc[low, :] + dq_there[i].astype(jnp.float32)
-        dk = dk_acc[high, :] * SCALE + dkv_there[i, 0:ROWS, :].astype(jnp.float32)
-        dv = dv_acc[high, :] + dkv_there[i, ROWS : 2 * ROWS, :].astype(jnp.float32)
-        for part, rows in enumerate((dq, dk, dv)):
-            chunk_ref[i, part * ROWS : (part + 1) * ROWS, :] = rows.astype(jnp.bfloat16)
+    def finish(parts_of):
+        for i in range(16):
+            low = slice(i * ROWS, (i + 1) * ROWS)
+            high = slice(SEG + i * ROWS, SEG + (i + 1) * ROWS)
+            dq = dq_acc[low, :] + dq_there[i].astype(jnp.float32)
+            dk = dk_acc[high, :] * SCALE + parts_of(i)[0].astype(jnp.float32)
+            dv = dv_acc[high, :] + parts_of(i)[1].astype(jnp.float32)
+            for part, rows in enumerate((dq, dk, dv)):
+                chunk_ref[i, part * ROWS : (part + 1) * ROWS, :] = rows.astype(jnp.bfloat16)
+
+    segment, unused_slot = place()
+
+    @pl.when(segment == 7)
+    def with_late():
+        finish(lambda i: (dk_late[i], dv_late[i]))
+
+    @pl.when(segment != 7)
+    def with_first():
+        finish(lambda i: (dkv_first[i, 0:ROWS, :], dkv_first[i, ROWS : 2 * ROWS, :]))
 
 
 def finish_kernel(
@@ -428,26 +463,29 @@
         limit=60 << 20,
     )
     own = exchange(chunks)
-    (kv,) = call(split_kernel, (own,), (half,), [VMEM])
-    kv_before = to_after(kv)
     scores = pltpu.VMEM((WIN, QB), jnp.float32)
     buffers = [scores] * 2 + [pltpu.VMEM((WIN, QB), jnp.bfloat16)] * 2
     coded = pltpu.VMEM((2 * ROWS, HD), jnp.float32)
+    pack = bf16(17, 2 * ROWS, HD)
     qd, info = call(
         down_kernel,
-        (doc_lengths, own, kv),
-        (bf16(17, 2 * ROWS, HD), jax.ShapeDtypeStruct((8, SEG), jnp.int32)),
-        [VMEM, VMEM, ANY],
+        (doc_lengths, own),
+        (pack, jax.ShapeDtypeStruct((8, SEG), jnp.int32)),
+        [VMEM, VMEM],
         scratch=[scores, coded],
         gflop=1.0,
     )
-    qd_after = to_before(qd)
+    qd_early = lax.ppermute(qd, AXES, EARLY)
+    (kv,) = call(split_kernel, (own, qd), (half,), [VMEM, ANY])
+    kv_before = to_after(kv)
+    (qd_again,) = call(again_kernel, (qd, kv), (pack,), [VMEM, ANY])
+    qd_rest = lax.ppermute(qd_again, AXES, DOWN_REST)
     stats = jax.ShapeDtypeStruct((8, SEG), jnp.float32)
     (own_stats,) = call(
         own_stats_kernel,
-        (info, own, kv_before),
+        (info, own, kv_before, qd_early),
         (stats,),
-        [VMEM] * 3,
+        [VMEM] * 3 + [ANY],
         scratch=[scores],
         gflop=1.5,
     )
@@ -464,19 +502,23 @@
     )
     before_grads, after_grads, dk_own, dv_own = call(
         after_kernel,
-        (info, own, kv_before, qd_after, dk_early, dv_early),
+        (info, own, kv_before, qd_rest, qd_early, dk_early, dv_early),
         (half, bf16(18, ROWS, HD), half_acc, half_acc),
-        [VMEM] * 6,
-        scratch=[sums, sums, sums, coded] + buffers,
+        [VMEM] * 7,
+        scratch=[sums, sums, sums, coded, pltpu.VMEM(pack.shape, pack.dtype)] + buffers,
         gflop=1.0,
     )
-    dkv_there = to_before(before_grads)
+    dkv_first = lax.ppermute(before_grads, AXES, DOWN_FIRST)
     dq_there = to_after(after_grads)
+    quarter = bf16(16, ROWS, HD)
+    dk_late, dv_late = call(halves_kernel, (before_grads,), (quarter, quarter), [VMEM])
+    dk_late = lax.ppermute(dk_late, AXES, LATE)
+    dv_late = lax.ppermute(dv_late, AXES, LATE)
     (merged,) = call(
         late_kernel,
-        (info, own, dk_own, dv_own, dq_early, dq_there, dkv_there),
+        (info, own, dk_own, dv_own, dq_early, dq_there, dkv_first, dk_late, dv_late),
         (bf16(16, 3 * ROWS, HD),),
-        [VMEM] * 7,
+        [VMEM] * 9,
         scratch=[sums, sums, pltpu.VMEM((SEG, HD), jnp.float32), coded] + buffers,
     )
     back = exchange(merged)

time: 85.5 us -> 84.2 us (0.985)
  the two profiles are of different devices: /device:TPU:25 before, /device:TPU:17 now
where the time goes in v8:
time: 84.2 us; the launch traced here: 83 us
  blocking collectives  34.9 us (41%)
  starting transfers between devices  26.7 us (32%)
  waiting for transfers between devices  13.4 us (16%)
  Pallas kernels  7.1 us (8%)
    all_to_all x2, blocking collectives, exchange(): lax.all_to_all(chunks, AXES, split_axis=0, concat_axis=0, axis_index_grou...  34.9 us
    ppermute x2, starting transfers between devices, to_after(): return lax.ppermute(block, AXES, UP)  12.3 us
    ppermute x1, starting transfers between devices, shards(): qd_rest = lax.ppermute(qd_again, AXES, DOWN_REST)  7.47 us
    pallas_call x10, Pallas kernels, call(): pl.pallas_call(kernel, in_specs=specs, out_specs=[VMEM] * len(outputs), o...  7.1 us
    ppermute x2, waiting for transfers between devices, to_after(): return lax.ppermute(block, AXES, UP)  5.9 us
    ppermute x1, starting transfers between devices, shards(): dk_late = lax.ppermute(dk_late, AXES, LATE)  3.66 us
    ppermute x1, waiting for transfers between devices, shards(): qd_rest = lax.ppermute(qd_again, AXES, DOWN_REST)  3.07 us
    ppermute x1, waiting for transfers between devices, shards(): dv_late = lax.ppermute(dv_late, AXES, LATE)  2.89 us
  transfers between devices with their start and end apart: 7, of which 5 were waited for; matrix products, arithmetic and copies ran while one was open for 0% of the time, Pallas kernels for 3%

profile of v8, /device:TPU:17, one launch (start us, length us, event | category | flops | bytes accessed | tf_op | source)
XLA Modules:
  0.0 83.0 jit_solution(12031162839767308737)
XLA Ops:
  0.6 1.9 %pack_kernel.1 = bf16[16,128,128]{2,1,0:T(8,128)(2,1)} custom-call(bf16[32,2048]{1,0:T(8,128)(2,1)} %q_hbm.1, bf16[32,2048]{1,0:T(8,128)(2,1)} %k_hbm.1, bf16[32,2048]{1,0:T(8,128)(2,1)} %v_hbm.1, bf16[32,2048]{1,0:T(8,128)(2,1)} %d_hbm.1), custom_call_target="tpu_custom_call" | custom-call | flops 500000000 | bytes 1048576 | tf_op jit(solution)/shard_map/pack_kernel/pallas_call | solution.py:440
  2.6 0.0 copy-start.2
  2.6 16.6 %all_to_all.10.own_ref = bf16[16,128,128]{2,1,0:T(8,128)(2,1)S(1)} all-to-all(bf16[16,128,128]{2,1,0:T(8,128)(2,1)} %pack_kernel.1), channel_id=1, replica_groups={{0,1,2,3,8,9,10,11,16,17,18,19,24,25,26,27},{32,33,34,35,40,41,42,43,48..., dimensions={0} | all-to-all | bytes 1048576 | tf_op jit(solution)/shard_map/all_to_all | solution.py:46
  19.2 0.0 copy-done.2
  19.2 0.6 down_kernel.1
  19.7 0.7 collective-permute-start.2
  20.4 4.9 %collective-permute-start = (bf16[16,64,128]{2,1,0:T(8,128)(2,1)S(1)}, bf16[16,64,128]{2,1,0:T(8,128)(2,1)S(1)}, u32[]{:S(2)}, u32[]{:S(2)}) collective-permute-start(bf16[16,64,128]{2,1,0:T(8,128)(2,1)S(1)} %split_kernel.1.kv_ref), channel_id=1, source_target_pairs={{0,32},{1,33},{2,34},{3,35},{8,40},{9,41},{10,42},{11,43},{16,48},... | collective-permute-start | bytes 786440 | tf_op jit(solution)/shard_map/ppermute | solution.py:42
  25.4 7.5 %collective-permute-start.1 = (bf16[17,64,128]{2,1,0:T(8,128)(2,1)S(1)}, bf16[17,64,128]{2,1,0:T(8,128)(2,1)S(1)}, u32[]{:S(2)}, u32[]{:S(2)}) collective-permute-start(bf16[17,64,128]{2,1,0:T(8,128)(2,1)S(1)} %again_kernel.1), channel_id=1, source_target_pairs={{32,0},{33,1},{34,2},{35,3},{40,8},{41,9},{42,10},{43,11},{48,16},... | collective-permute-start | bytes 835592 | tf_op jit(solution)/shard_map/ppermute | solution.py:482
  32.8 5.9 %collective-permute-done.before_ref = bf16[16,64,128]{2,1,0:T(8,128)(2,1)S(1)} collective-permute-done((bf16[16,64,128]{2,1,0:T(8,128)(2,1)S(1)}, bf16[16,64,128]{2,1,0:T(8,128)(2,1)S(1)}, u32[]{:S(2)}, u32[]{:S(2)}) %collective-permute-start) | collective-permute-done | bytes 262176 | tf_op jit(solution)/shard_map/ppermute | solution.py:42
  38.7 0.0 collective-permute-done.2.early_ref
  38.7 1.0 %own_stats_kernel.1.own_stats = f32[8,512]{1,0:T(8,128)S(1)} custom-call(s32[8,512]{1,0:T(8,128)S(1)} %get-tuple-element.16.info_ref, bf16[16,128,128]{2,1,0:T(8,128)(2,1)S(1)} %all_to_all.10.own_ref, bf16[16,64,128]{2,1,0:T(8,128)(2,1)S(1)} %collective-permute-done.before_ref, bf16[17,64,128]{2,1,0:T(8,128)(2,1)S(1)} %collective-permute-done.2.early_ref), custom_call_target="tpu_custom_call" | custom-call | flops 1500000000 | bytes 1048576 | tf_op jit(solution)/shard_map/own_stats_kernel/pallas_call | solution.py:440
  39.7 1.4 %early_kernel.1 = (f32[1024,128]{1,0:T(8,128)S(1)}, f32[1024,128]{1,0:T(8,128)S(1)}, f32[512,128]{1,0:T(8,128)S(1)}) custom-call(s32[8,512]{1,0:T(8,128)S(1)} %get-tuple-element.16.info_ref, bf16[16,128,128]{2,1,0:T(8,128)(2,1)S(1)} %all_to_all.10.own_ref, bf16[16,64,128]{2,1,0:T(8,128)(2,1)S(1)} %collective-permute-done.before_ref, ...), custom_call_target="tpu_custom_call" | custom-call | flops 2000000000 | bytes 1048576 | tf_op jit(solution)/shard_map/early_kernel/pallas_call | solution.py:440
  41.1 3.1 %collective-permute-done.1.rest_ref = bf16[17,64,128]{2,1,0:T(8,128)(2,1)S(1)} collective-permute-done((bf16[17,64,128]{2,1,0:T(8,128)(2,1)S(1)}, bf16[17,64,128]{2,1,0:T(8,128)(2,1)S(1)}, u32[]{:S(2)}, u32[]{:S(2)}) %collective-permute-start.1) | collective-permute-done | bytes 278560 | tf_op jit(solution)/shard_map/ppermute | solution.py:482
  44.2 0.4 after_kernel.1
  44.6 1.3 %collective-permute-start.4 = (bf16[16,64,128]{2,1,0:T(8,128)(2,1)S(1)}, bf16[16,64,128]{2,1,0:T(8,128)(2,1)S(1)}, u32[]{:S(2)}, u32[]{:S(2)}) collective-permute-start(bf16[16,64,128]{2,1,0:T(8,128)(2,1)S(1)} %get-tuple-element.24.pair_ref), channel_id=1, source_target_pairs={{32,0},{33,1},{34,2},{35,3},{40,8},{41,9},{42,10},{43,11},{48,16},... | collective-permute-start | bytes 786440 | tf_op jit(solution)/shard_map/ppermute | solution.py:511
  45.9 7.4 %collective-permute-start.3 = (bf16[18,32,128]{2,1,0:T(8,128)(2,1)S(1)}, bf16[18,32,128]{2,1,0:T(8,128)(2,1)S(1)}, u32[]{:S(2)}, u32[]{:S(2)}) collective-permute-start(bf16[18,32,128]{2,1,0:T(8,128)(2,1)S(1)} %get-tuple-element.23), channel_id=1, source_target_pairs={{0,32},{1,33},{2,34},{3,35},{8,40},{9,41},{10,42},{11,43},{16,48},... | collective-permute-start | bytes 442376 | tf_op jit(solution)/shard_map/ppermute | solution.py:42
  53.4 3.7 %collective-permute-start.5 = (bf16[16,32,128]{2,1,0:T(8,128)(2,1)S(1)}, bf16[16,32,128]{2,1,0:T(8,128)(2,1)S(1)}, u32[]{:S(2)}, u32[]{:S(2)}) collective-permute-start(bf16[16,32,128]{2,1,0:T(8,128)(2,1)S(1)} %get-tuple-element.25), channel_id=1, source_target_pairs={{256,224},{257,225},{258,226},{259,227},{264,232},{265,233},{266,2... | collective-permute-start | bytes 393224 | tf_op jit(solution)/shard_map/ppermute | solution.py:515
  57.0 1.3 %collective-permute-start.6 = (bf16[16,32,128]{2,1,0:T(8,128)(2,1)S(1)}, bf16[16,32,128]{2,1,0:T(8,128)(2,1)S(1)}, u32[]{:S(2)}, u32[]{:S(2)}) collective-permute-start(bf16[16,32,128]{2,1,0:T(8,128)(2,1)S(1)} %get-tuple-element.26), channel_id=1, source_target_pairs={{256,224},{257,225},{258,226},{259,227},{264,232},{265,233},{266,2... | collective-permute-start | bytes 393224 | tf_op jit(solution)/shard_map/ppermute | solution.py:516
  58.3 0.6 collective-permute-done.5.dk_late
  59.0 2.9 %collective-permute-done.6.dv_late = bf16[16,32,128]{2,1,0:T(8,128)(2,1)S(1)} collective-permute-done((bf16[16,32,128]{2,1,0:T(8,128)(2,1)S(1)}, bf16[16,32,128]{2,1,0:T(8,128)(2,1)S(1)}, u32[]{:S(2)}, u32[]{:S(2)}) %collective-permute-start.6) | collective-permute-done | bytes 131104 | tf_op jit(solution)/shard_map/ppermute | solution.py:516
  61.9 0.0 collective-permute-done.3.dq_there
  61.9 0.9 %collective-permute-done.4.dkv_first = bf16[16,64,128]{2,1,0:T(8,128)(2,1)S(1)} collective-permute-done((bf16[16,64,128]{2,1,0:T(8,128)(2,1)S(1)}, bf16[16,64,128]{2,1,0:T(8,128)(2,1)S(1)}, u32[]{:S(2)}, u32[]{:S(2)}) %collective-permute-start.4) | collective-permute-done | bytes 262176 | tf_op jit(solution)/shard_map/ppermute | solution.py:511
  62.8 0.7 late_kernel.1
  63.5 0.0 copy-start
  63.5 0.0 copy-start.1
  63.6 18.4 %all_to_all.11.back_ref = bf16[16,96,128]{2,1,0:T(8,128)(2,1)S(1)} all-to-all(bf16[16,96,128]{2,1,0:T(8,128)(2,1)S(1)} %late_kernel.1), channel_id=1, replica_groups={{0,1,2,3,8,9,10,11,16,17,18,19,24,25,26,27},{32,33,34,35,40,41,42,43,48..., dimensions={0} | all-to-all | bytes 786432 | tf_op jit(solution)/shard_map/all_to_all | solution.py:46
  81.9 0.0 copy-done
  81.9 0.0 copy-done.1
  81.9 1.0 %finish_kernel.1 = (bf16[32,2048]{1,0:T(8,128)(2,1)}, bf16[32,2048]{1,0:T(8,128)(2,1)}, bf16[32,2048]{1,0:T(8,128)(2,1)}, f32[32,2048]{1,0:T(8,128)}, f32[32,2048]{1,0:T(8,128)}) custom-call(bf16[16,96,128]{2,1,0:T(8,128)(2,1)S(1)} %all_to_all.11.back_ref, f32[32,2048]{1,0:T(8,128)S(1)} %copy-done, f32[32,2048]{1,0:T(8,128)S(1)} %copy-done.1), custom_call_target="tpu_custom_call" | custom-call | flops 500000000 | bytes 1048576 | tf_op jit(solution)/shard_map/finish_kernel/pallas_call | solution.py:440
  (3 shorter events, 0.1 us)
Async XLA Ops:
  2.6 16.6 %copy-start.2 = (s32[32]{0:T(128)S(1)}, s32[32]{0:T(128)}, u32[]{:S(2)}) copy-start(s32[32]{0:T(128)} %lengths_ref.1) | copy-start | bytes 388
  19.7 19.0 %collective-permute-start.2 = (bf16[17,64,128]{2,1,0:T(8,128)(2,1)S(1)}, bf16[17,64,128]{2,1,0:T(8,128)(2,1)S(1)}, u32[]{:S(2)}, u32[]{:S(2)}) collective-permute-start(bf16[17,64,128]{2,1,0:T(8,128)(2,1)S(1)} %get-tuple-element.17.qd_ref), channel_id=1, source_target_pairs={{252,284},{253,285},{254,286},{255,287},{244,276},{245,277},{246,2... | collective-permute-start | bytes 835592 | tf_op jit(solution)/shard_map/ppermute | solution.py:478
  20.4 18.3 %collective-permute-start = (bf16[16,64,128]{2,1,0:T(8,128)(2,1)S(1)}, bf16[16,64,128]{2,1,0:T(8,128)(2,1)S(1)}, u32[]{:S(2)}, u32[]{:S(2)}) collective-permute-start(bf16[16,64,128]{2,1,0:T(8,128)(2,1)S(1)} %split_kernel.1.kv_ref), channel_id=1, source_target_pairs={{0,32},{1,33},{2,34},{3,35},{8,40},{9,41},{10,42},{11,43},{16,48},... | collective-permute-start | bytes 786440 | tf_op jit(solution)/shard_map/ppermute | solution.py:42
  25.4 18.8 %collective-permute-start.1 = (bf16[17,64,128]{2,1,0:T(8,128)(2,1)S(1)}, bf16[17,64,128]{2,1,0:T(8,128)(2,1)S(1)}, u32[]{:S(2)}, u32[]{:S(2)}) collective-permute-start(bf16[17,64,128]{2,1,0:T(8,128)(2,1)S(1)} %again_kernel.1), channel_id=1, source_target_pairs={{32,0},{33,1},{34,2},{35,3},{40,8},{41,9},{42,10},{43,11},{48,16},... | collective-permute-start | bytes 835592 | tf_op jit(solution)/shard_map/ppermute | solution.py:482
  44.6 18.2 %collective-permute-start.4 = (bf16[16,64,128]{2,1,0:T(8,128)(2,1)S(1)}, bf16[16,64,128]{2,1,0:T(8,128)(2,1)S(1)}, u32[]{:S(2)}, u32[]{:S(2)}) collective-permute-start(bf16[16,64,128]{2,1,0:T(8,128)(2,1)S(1)} %get-tuple-element.24.pair_ref), channel_id=1, source_target_pairs={{32,0},{33,1},{34,2},{35,3},{40,8},{41,9},{42,10},{43,11},{48,16},... | collective-permute-start | bytes 786440 | tf_op jit(solution)/shard_map/ppermute | solution.py:511
  45.9 16.0 %collective-permute-start.3 = (bf16[18,32,128]{2,1,0:T(8,128)(2,1)S(1)}, bf16[18,32,128]{2,1,0:T(8,128)(2,1)S(1)}, u32[]{:S(2)}, u32[]{:S(2)}) collective-permute-start(bf16[18,32,128]{2,1,0:T(8,128)(2,1)S(1)} %get-tuple-element.23), channel_id=1, source_target_pairs={{0,32},{1,33},{2,34},{3,35},{8,40},{9,41},{10,42},{11,43},{16,48},... | collective-permute-start | bytes 442376 | tf_op jit(solution)/shard_map/ppermute | solution.py:42
  53.4 5.6 %collective-permute-start.5 = (bf16[16,32,128]{2,1,0:T(8,128)(2,1)S(1)}, bf16[16,32,128]{2,1,0:T(8,128)(2,1)S(1)}, u32[]{:S(2)}, u32[]{:S(2)}) collective-permute-start(bf16[16,32,128]{2,1,0:T(8,128)(2,1)S(1)} %get-tuple-element.25), channel_id=1, source_target_pairs={{256,224},{257,225},{258,226},{259,227},{264,232},{265,233},{266,2... | collective-permute-start | bytes 393224 | tf_op jit(solution)/shard_map/ppermute | solution.py:515
  57.0 4.8 %collective-permute-start.6 = (bf16[16,32,128]{2,1,0:T(8,128)(2,1)S(1)}, bf16[16,32,128]{2,1,0:T(8,128)(2,1)S(1)}, u32[]{:S(2)}, u32[]{:S(2)}) collective-permute-start(bf16[16,32,128]{2,1,0:T(8,128)(2,1)S(1)} %get-tuple-element.26), channel_id=1, source_target_pairs={{256,224},{257,225},{258,226},{259,227},{264,232},{265,233},{266,2... | collective-permute-start | bytes 393224 | tf_op jit(solution)/shard_map/ppermute | solution.py:516
  63.5 18.4 %copy-start = (f32[32,2048]{1,0:T(8,128)S(1)}, f32[32,2048]{1,0:T(8,128)}, u32[]{:S(2)}) copy-start(f32[32,2048]{1,0:T(8,128)} %key_prior_ref.1) | copy-start | bytes 786436
  63.5 18.4 %copy-start.1 = (f32[32,2048]{1,0:T(8,128)S(1)}, f32[32,2048]{1,0:T(8,128)}, u32[]{:S(2)}) copy-start(f32[32,2048]{1,0:T(8,128)} %value_prior_ref.1) | copy-start | bytes 786436
